TPU v7x, 256 devices: a whole 4x4x8 slice. The times are simulated.
256 devices in a mesh: pos: 32 (over y, z_hi, core), tile: 8 (over x, z_lo).
Axes of the slice: x: 4, y: 4, z: 8 (z_hi: 4, z_lo: 2; z = z_hi * 2 + z_lo), core: 2. Of those that a mesh axis runs over, the one named last changes fastest.
Arguments:
- object_field: float32 [2, 2, 8192, 2048], P(None, None, 'pos', 'tile'), may hold values from -4 to 4
- probe_modes: float32 [4, 2, 256, 256], replicated, may hold values from -5 to 5
- amplitudes: float32 [256, 256, 256], P(('pos', 'tile')), may hold values from 0 to 3
- corners: int32 [256, 2], P(('pos', 'tile')), may hold values from 0 to 255
Outputs:
- object_grad: float32 [2, 2, 8192, 2048], P(None, None, 'pos', 'tile')
- probe_grad: float32 [4, 2, 256, 256], replicated
Inputs may be any that keep to these rules, and one draw needn't show every extreme that they name: `corners`: each position's window starts inside the block of the device that holds the position.
All inputs are finite; a program needn't handle non-finite values.
Results may differ from a plain program's by a relative error of at most 0.0003.
Values sent between devices are 32-bit elements; how exact they have to be, the bound alone decides.
No kernel may reach another device: no remote copies, remote signals or barrier semaphores. Data moves between devices by JAX's collectives and lax.ppermute only.
A program may use at most 128 MiB of HBM per device.

v0:
```python
import math

import jax
import jax.numpy as jnp
from jax import lax
from jax.sharding import PartitionSpec as P


def shifted(value, axis, steps):
    count = lax.axis_size(axis)
    first, last = (max(0, -steps), min(count, count - steps))
    return lax.ppermute(value, axis, [(source, source + steps) for source in range(first, last)])


def tables(length):
    counter = jnp.arange(length, dtype=jnp.int32)
    product = counter[:, None] * counter[None, :] % length
    angles = product.astype(jnp.float32) * (-2.0 * math.pi / length)
    normal = 1.0 / math.sqrt(length)
    frequency = jnp.where(counter < length // 2, counter, counter - length)
    squared = frequency * frequency
    phases = (squared[:, None] + squared[None, :]).astype(jnp.float32) * (-math.pi / (2.0 * length))
    fourier = (jnp.cos(angles) * normal, jnp.sin(angles) * normal)
    fresnel = (jnp.cos(phases), jnp.sin(phases))
    return (fourier, fresnel)


def matmul_high(left_operand, right_operand):
    return jnp.matmul(left_operand, right_operand, precision=lax.Precision.HIGHEST)


def product_left(matrix, operand):
    return (
        matmul_high(matrix[0], operand[0]) - matmul_high(matrix[1], operand[1]),
        matmul_high(matrix[0], operand[1]) + matmul_high(matrix[1], operand[0]),
    )


def product_right(operand, matrix):
    return (
        matmul_high(operand[0], matrix[0]) - matmul_high(operand[1], matrix[1]),
        matmul_high(operand[0], matrix[1]) + matmul_high(operand[1], matrix[0]),
    )


def multiply(first, second):
    return (
        first[0] * second[0] - first[1] * second[1],
        first[0] * second[1] + first[1] * second[0],
    )


def conjugate(value):
    return (value[0], -value[1])


def transform(operand, matrix):
    return product_right(product_left(matrix, operand), matrix)


def position_terms(window, probe_modes, amplitude, fourier, fresnel):
    layers = [
        (window[layer_index, 0], window[layer_index, 1]) for layer_index in range(window.shape[0])
    ]
    inverse = conjugate(fourier)
    incoming = [(probe_modes[:, 0], probe_modes[:, 1])]
    current = multiply(incoming[0], layers[0])
    layer_index = 1
    propagated = transform(multiply(fresnel, transform(current, fourier)), inverse)
    incoming.append(propagated)
    current = multiply(propagated, layers[layer_index])
    farfield = transform(current, fourier)
    intensity = jnp.sum(farfield[0] * farfield[0] + farfield[1] * farfield[1], axis=0)
    factor = 1.0 - amplitude / jnp.sqrt(intensity + 1.0)
    backward = transform((factor * farfield[0], factor * farfield[1]), inverse)
    gradients = []
    for layer_index in reversed(range(len(layers))):
        partial_term = multiply(conjugate(incoming[layer_index]), backward)
        gradients.append(
            jnp.stack([jnp.sum(partial_term[0], axis=0), jnp.sum(partial_term[1], axis=0)])
        )
        backward = multiply(conjugate(layers[layer_index]), backward)
        if layer_index > 0:
            backward = transform(
                multiply(conjugate(fresnel), transform(backward, fourier)), inverse
            )
    window_grad = jnp.stack(gradients[::-1])
    probe_term = jnp.stack([backward[0], backward[1]], axis=1)
    return (window_grad, probe_term)


def per_device(object_field, probe_modes, amplitudes, corners):
    length = probe_modes.shape[-1]
    block_size = object_field.shape[2]
    slices = object_field.shape[0]
    fourier, fresnel = tables(length)
    right_block = shifted(object_field, "tile", -1)
    upper_pair = jnp.concatenate([object_field, right_block], axis=3)
    lower_pair = shifted(upper_pair, "pos", -1)
    canvas = jnp.concatenate([upper_pair, lower_pair], axis=2)
    zero_index = jnp.zeros((), jnp.int32)

    def visit(carried, element):
        grad_canvas, probe_sum = carried
        amplitude, corner = element
        starts = (zero_index, zero_index, corner[0], corner[1])
        window = lax.dynamic_slice(canvas, starts, (slices, 2, length, length))
        window_grad, probe_term = position_terms(window, probe_modes, amplitude, fourier, fresnel)
        placed = lax.dynamic_slice(grad_canvas, starts, (slices, 2, length, length)) + window_grad
        return (
            (lax.dynamic_update_slice(grad_canvas, placed, starts), probe_sum + probe_term),
            None,
        )

    initial = (jnp.zeros(canvas.shape, jnp.float32), jnp.zeros(probe_modes.shape, jnp.float32))
    (grad_canvas, probe_sum), unused = lax.scan(visit, initial, (amplitudes, corners))
    probe_grad = lax.psum(probe_sum, ("pos", "tile"))
    upward = shifted(grad_canvas[:, :, block_size:, :], "pos", 1)
    upper_rows = grad_canvas[:, :, :block_size, :] + upward
    leftward = shifted(upper_rows[:, :, :, block_size:], "tile", 1)
    object_grad = upper_rows[:, :, :, :block_size] + leftward
    return (object_grad, probe_grad)


def solution(mesh):
    in_specs = (
        P(None, None, "pos", "tile"),
        P(),
        P(("pos", "tile"), None, None),
        P(("pos", "tile"), None),
    )
    out_specs = (P(None, None, "pos", "tile"), P())
    return jax.shard_map(
        per_device, mesh=mesh, in_specs=in_specs, out_specs=out_specs, check_vma=False
    )
```

profile of v0, /device:TPU:2, one launch (start us, length us, event | category | flops | bytes accessed | tf_op | source)
XLA Modules:
  0.0 502.6 jit_solution(7157107167341642745)
XLA Ops:
  7.2 3.8 collective-permute-start
  12.4 22.0 %collective-permute-done = f32[2,2,256,256]{3,2,1,0:T(8,128)S(1)} collective-permute-done((f32[2,2,256,256]{3,2,1,0:T(8,128)}, f32[2,2,256,256]{3,2,1,0:T(8,128)S(1)}, u32[]{:S(2)}, u32[]{:S(2)}) %collective-permute-start) | collective-permute-done | bytes 1048608 | tf_op jit(solution)/shard_map/ppermute | solution.py:12
  53.1 2.5 fusion.100
  55.6 2.2 fusion.10
  66.1 2.4 fusion.9
  72.5 2.2 fusion.8
  78.6 2.4 fusion.84
  83.1 2.2 fusion.7
  89.3 2.2 fusion.6
  91.5 2.4 convolution_subtract_fusion.6
  110.5 2.3 subtract_reduce_fusion
  115.0 2.4 fusion.76
  117.4 2.2 fusion.3
  123.5 2.2 fusion.2
  127.7 2.4 convolution_subtract_fusion.2
  140.6 2.3 fusion
  145.0 2.6 subtract_bitcast_fusion
  147.7 2.5 broadcast_in_dim.8
  150.2 12.1 %dynamic_update_slice.4 = f32[2,2,512,512]{3,2,1,0:T(8,128)} dynamic-update-slice(f32[2,2,512,512]{3,2,1,0:T(8,128)} %broadcast_in_dim.8, f32[2,2,256,256]{3,2,1,0:T(8,128)S(1)} %pad_maximum_fusion.1, s32[]{:T(128)} %constant.20.clone.1, s32[]{:T(128)} %constant.20.clone.1, s32[]{:T(128)S(6)} %select_n.141, s32[]{:T(128)S(6)} %select_n.142) | dynamic-update-slice | bytes 2097156 | tf_op jit(solution)/shard_map/while/body/eval_jaxpr/dynamic_update_slice | solution.py:111
  162.3 3.1 slice.63
  165.4 47.7 %collective-permute-start.2 = (f32[2,2,256,512]{3,2,1,0:T(8,128)}, f32[2,2,256,512]{3,2,1,0:T(8,128)}, u32[]{:S(2)}, u32[]{:S(2)}) collective-permute-start(f32[2,2,256,512]{3,2,1,0:T(8,128)} %slice.63), channel_id=1, source_target_pairs={{0,8},{8,16},{16,24},{24,32},{32,40},{40,48},{48,56},{56,64},{64,7... | collective-permute-start | bytes 6291464 | tf_op jit(solution)/shard_map/ppermute | solution.py:12
  215.8 2.7 slice_add_fusion
  221.5 269.9 %all-reduce.2.cloned.1.call-done = f32[4,2,256,256]{3,2,0,1:T(8,128)} async-done(((f32[4,2,256,256]{3,2,0,1:T(8,128)}), f32[4,2,256,256]{3,2,0,1:T(8,128)}) %all-reduce.2.cloned.1.call-update) | async-done | bytes 2097168 | tf_op jit(solution)/shard_map/psum | solution.py:117
  491.4 3.0 copy.8
  (60 shorter events, 82.6 us)
Async XLA Ops:
  7.2 28.7 %copy-start.2 = (s32[1,2]{1,0:T(1,128)S(1)}, s32[1,2]{1,0:T(1,128)}, u32[]{:S(2)}) copy-start(s32[1,2]{1,0:T(1,128)} %param.7) | copy-start | bytes 28
  7.2 484.2 %all-reduce.2.cloned.1.call-start = ((), (), s32[]{:S(2)}) async-start(), calls=%async_computation | async-start | bytes 4194304 | tf_op jit(solution)/shard_map/psum | solution.py:117
  7.2 27.2 %collective-permute-start = (f32[2,2,256,256]{3,2,1,0:T(8,128)}, f32[2,2,256,256]{3,2,1,0:T(8,128)S(1)}, u32[]{:S(2)}, u32[]{:S(2)}) collective-permute-start(f32[2,2,256,256]{3,2,1,0:T(8,128)} %param.4), channel_id=1, source_target_pairs={{1,0},{2,1},{3,2},{4,3},{5,4},{6,5},{7,6},{9,8},{10,9},{11,10},{12... | collective-permute-start | bytes 3145736 | tf_op jit(solution)/shard_map/ppermute | solution.py:12
  34.6 6.8 %collective-permute-start.1 = (f32[2,2,256,512]{3,2,1,0:T(8,128)S(1)}, f32[2,2,256,512]{3,2,1,0:T(8,128)}, u32[]{:S(2)}, u32[]{:S(2)}) collective-permute-start(f32[2,2,256,512]{3,2,1,0:T(8,128)S(1)} %constant_dynamic-update-slice_fusion), channel_id=1, source_target_pairs={{8,0},{16,8},{24,16},{32,24},{40,32},{48,40},{56,48},{64,56},{72,6... | collective-permute-start | bytes 6291464 | tf_op jit(solution)/shard_map/ppermute | solution.py:12
  43.1 1.6 copy-start
  93.9 2.1 copy-start.1
  165.4 50.4 %collective-permute-start.2 = (f32[2,2,256,512]{3,2,1,0:T(8,128)}, f32[2,2,256,512]{3,2,1,0:T(8,128)}, u32[]{:S(2)}, u32[]{:S(2)}) collective-permute-start(f32[2,2,256,512]{3,2,1,0:T(8,128)} %slice.63), channel_id=1, source_target_pairs={{0,8},{8,16},{16,24},{24,32},{32,40},{40,48},{48,56},{56,64},{64,7... | collective-permute-start | bytes 6291464 | tf_op jit(solution)/shard_map/ppermute | solution.py:12
  219.6 274.9 %collective-permute-start.3 = (f32[2,2,256,256]{3,2,1,0:T(8,128)}, f32[2,2,256,256]{3,2,1,0:T(8,128)S(1)}, u32[]{:S(2)}, u32[]{:S(2)}) collective-permute-start(f32[2,2,256,256]{3,2,1,0:T(8,128)} %slice.65), channel_id=1, source_target_pairs={{0,1},{1,2},{2,3},{3,4},{4,5},{5,6},{6,7},{8,9},{9,10},{10,11},{11... | collective-permute-start | bytes 3145736 | tf_op jit(solution)/shard_map/ppermute | solution.py:12
Sparse Core Ops, SparseCore 0:
  214.8 276.5 all-reduce.1
where the time goes:
time: 512 us; the launch traced here: 503 us
  waiting for transfers between devices  293 us (57%)
  matrix products  102 us (20%)
  starting transfers between devices  54.7 us (11%)
  local copies, waits for them, and re-layouts  25.4 us (5%)
  between operations  18.6 us (4%)
  other arithmetic  8.43 us (2%)
    psum x1, waiting for transfers between devices, per_device(): probe_grad = lax.psum(probe_sum, ('pos', 'tile'))  270 us
    dot_general x48, matrix products, matmul_high(): jnp.matmul(left_operand, right_operand, precision=lax.Precision.HIGHEST)  102 us
    ppermute x4, starting transfers between devices, shifted(): lax.ppermute(value, axis, [(source, source + steps) for source in range(f...  54.7 us
    ppermute x4, waiting for transfers between devices, shifted(): lax.ppermute(value, axis, [(source, source + steps) for source in range(f...  23.1 us
    dynamic_update_slice x1, local copies, waits for them, and re-layouts, visit(): lax.dynamic_update_slice(grad_canvas, placed, starts)  12.1 us
  transfers between devices with their start and end apart: 5, of which 3 were waited for; matrix products, arithmetic and copies ran while one was open for 2% of the time, Pallas kernels for 0%

commit v1 on v0

v1 whole, which is shorter than its diff:
```python
import math

import jax
import jax.numpy as jnp
import numpy as np
from jax import lax
from jax.experimental import pallas as pl
from jax.experimental.pallas import tpu as pltpu
from jax.sharding import PartitionSpec as P

N = 256
H = 128
F32 = jnp.float32
BF16 = jnp.bfloat16


def split_np(matrix):
    high = matrix.astype(np.float32).astype(jnp.bfloat16)
    low = (matrix - high.astype(np.float64)).astype(np.float32).astype(jnp.bfloat16)
    return high, low


def constants():
    count = np.arange(N)
    fourier = np.exp(-2j * np.pi * (np.outer(count, count) % N) / N) / math.sqrt(N)
    freq = np.where(count < H, count, count - N).astype(np.float64)
    fresnel = np.exp(-1j * np.pi * freq * freq / (2.0 * N))
    prop = (np.conj(fourier) * fresnel[None, :]) @ fourier
    straight, turned = prop[:H, :H], prop[:H, ::-1][:, :H]
    mats = []
    for part in ((straight + turned) / 2, (straight - turned) / 2):
        for side in (part, np.conj(part)):
            real, imag = side.real, side.imag
            right = np.block([[real, imag], [-imag, real]])
            high, low = split_np(right)
            mats.append(np.concatenate([high, high, low], axis=0))
            left = np.block([[real, -imag], [imag, real]])
            high, low = split_np(left)
            mats.append(np.concatenate([high, high, low], axis=1))
    half = np.arange(H) - 127.5
    angle = 2 * np.pi * np.outer(half, half) / N
    zero = np.zeros((H, H))
    both = np.block([[np.cos(angle) / 16, zero], [zero, np.sin(angle) / 16]])
    high, low = split_np(both)
    right_b = np.concatenate([high, high, low], axis=0)
    left_b = np.concatenate([high, high, low], axis=1)
    rights = np.stack([mats[0], mats[4], mats[2], mats[6], right_b])
    lefts = np.stack([mats[1], mats[5], mats[3], mats[7], left_b])
    order = np.concatenate([np.arange(H), N - 1 - np.arange(H)])
    tilt = np.exp(-2j * np.pi * 127.5 * order / N)
    phase = np.outer(tilt, tilt)
    phases = np.stack([phase.real, phase.imag]).astype(np.float32)
    return rights, lefts, phases


def mirror(value):
    lanes = H - 1 - lax.broadcasted_iota(jnp.int32, (N, H), 1)
    right = jnp.take_along_axis(value[:, H:], lanes, axis=1)
    value = jnp.concatenate([value[:, :H], right], axis=1)
    rows = 7 - lax.broadcasted_iota(jnp.int32, (8, N), 0)
    tiles = [
        jnp.take_along_axis(value[N - 8 - 8 * i : N - 8 * i], rows, axis=0) for i in range(H // 8)
    ]
    return jnp.concatenate([value[:H]] + tiles, axis=0)


def parts(value):
    high = value.astype(BF16)
    return high, (value - high.astype(F32)).astype(BF16)


def dot(left, right):
    return jnp.dot(left, right, preferred_element_type=F32)


CH = 16
CHUNKS = H // CH


def fold4(tl, tr, bl, br):
    a, b = tl + bl, tr + br
    c, d = tl - bl, tr - br
    return a + b, a - b, c + d, c - d


def mul(a, b):
    return a[0] * b[0] - a[1] * b[1], a[0] * b[1] + a[1] * b[0]


def mulc(a, b):
    return a[0] * b[0] + a[1] * b[1], a[0] * b[1] - a[1] * b[0]


QUADS = ((0, 0), (0, 1), (1, 0), (1, 1))


def quad(ref, lead, row, q):
    r, c = q
    return ref[lead + (slice(r * H + row, r * H + row + CH), slice(c * H, c * H + H))]


def put(ref, lead, row, q, value):
    r, c = q
    ref[lead + (slice(r * H + row, r * H + row + CH), slice(c * H, c * H + H))] = value


def store_right_prop(op, mode, row, real, imag):
    for index, (r, c) in enumerate(QUADS):
        for part, value in ((0, real[index]), (1, imag[index])):
            high, low = parts(value)
            rows = slice(mode * N + r * H + row, mode * N + r * H + row + CH)
            op[c, rows, part * H : part * H + H] = high
            op[c, rows, N + part * H : N + part * H + H] = low


def store_right_four(op, mode, row, real, imag):
    for index, (r, c) in enumerate(QUADS):
        for part, value in ((0, real[index]), (1, imag[index])):
            high, low = parts(value)
            rows = slice(mode * N + r * H + row, mode * N + r * H + row + CH)
            op[part, rows, c * H : c * H + H] = high
            op[part, rows, N + c * H : N + c * H + H] = low


def three(ref_value):
    return jnp.concatenate([ref_value, ref_value[:, :N]], axis=1)


def prop_products(op, mid, out, rights, lefts, even, odd, modes):
    for c, which in ((0, even), (1, odd)):
        for m in range(modes):
            rows = slice(m * N, m * N + N)
            res = dot(three(op[c, rows, :]), rights[which])
            high, low = parts(res)
            for level, value in ((0, high), (1, low)):
                for r in (0, 1):
                    for p in (0, 1):
                        mid[
                            r,
                            level * N + p * H : level * N + p * H + H,
                            m * N + c * H : m * N + c * H + H,
                        ] = value[r * H : r * H + H, p * H : p * H + H]
    for r, which in ((0, even), (1, odd)):
        for m in range(modes):
            cols = slice(m * N, m * N + N)
            x = mid[r, :, cols]
            x = jnp.concatenate([x, x[:N]], axis=0)
            out[r, :, cols] = dot(lefts[which], x)


def four_products(op, mid, out, rights, lefts, modes):
    for p in (0, 1):
        for m in range(modes):
            rows = slice(m * N, m * N + N)
            res = dot(three(op[p, rows, :]), rights[4])
            high, low = parts(res)
            mid[p, :N, m * N : m * N + N] = high
            mid[p, N:, m * N : m * N + N] = low
    for p in (0, 1):
        for m in range(modes):
            cols = slice(m * N, m * N + N)
            x = mid[p, :, cols]
            x = jnp.concatenate([x, x[:N]], axis=0)
            out[p, :, cols] = dot(lefts[4], x)


def load_prop(out, mode, row):
    result = []
    for p in (0, 1):
        result.append(
            [
                out[r, p * H + row : p * H + row + CH, mode * N + c * H : mode * N + c * H + H]
                for r, c in QUADS
            ]
        )
    return result


def load_four(out, mode, row, sign):
    real, imag = [
        [
            out[p, r * H + row : r * H + row + CH, mode * N + c * H : mode * N + c * H + H]
            for r, c in QUADS
        ]
        for p in (0, 1)
    ]
    if sign > 0:
        return (
            [real[0], imag[1], imag[2], -real[3]],
            [imag[0], -real[1], -real[2], -imag[3]],
        )
    return (
        [real[0], -imag[1], -imag[2], -real[3]],
        [imag[0], real[1], real[2], -imag[3]],
    )


def unfold4(ee, eo, oe, oo):
    a, b = ee + eo, ee - eo
    c, d = oe + oo, oe - oo
    return a + c, b + d, a - c, b - d


def main_kernel(
    corner, own, right, lower, probes, amp, rights, lefts, phases,
    terms, grads,
    obj, q1, op, mid, out, acc,
):
    modes = probes.shape[0]
    y0, x0 = corner[0, 0], corner[0, 1]
    up = lax.rem(N - y0, N)
    back = lax.rem(N - x0, N)
    below = lax.broadcasted_iota(jnp.int32, (N, N), 0) < y0
    beside = lax.broadcasted_iota(jnp.int32, (N, N), 1) < x0
    for s in range(2):
        window = []
        for p in range(2):
            upper = jnp.where(beside, right[s, p], own[s, p])
            value = jnp.where(below, lower[s, p], upper)
            value = pltpu.roll(pltpu.roll(value, up, 0), back, 1)
            window.append(mirror(value))
        if s == 1:
            window = mul(window, (phases[0], phases[1]))
        obj[s, 0], obj[s, 1] = window

    def field(ref, lead, row, q):
        return quad(ref, lead + (0,), row, q), quad(ref, lead + (1,), row, q)

    def fold_pairs(pairs):
        return fold4(*[v[0] for v in pairs]), fold4(*[v[1] for v in pairs])

    for m in range(modes):
        for k in range(CHUNKS):
            row = k * CH
            pairs = [mul(field(probes, (m,), row, q), field(obj, (0,), row, q)) for q in QUADS]
            store_right_prop(op, m, row, *fold_pairs(pairs))
    prop_products(op, mid, out, rights, lefts, 0, 1, modes)
    for m in range(modes):
        for k in range(CHUNKS):
            row = k * CH
            real, imag = load_prop(out, m, row)
            pixels = list(zip(unfold4(*real), unfold4(*imag)))
            for q, v in zip(QUADS, pixels):
                put(q1, (m, 0), row, q, v[0])
                put(q1, (m, 1), row, q, v[1])
            pairs = [mul(v, field(obj, (1,), row, q)) for q, v in zip(QUADS, pixels)]
            store_right_four(op, m, row, *fold_pairs(pairs))
    four_products(op, mid, out, rights, lefts, modes)
    for k in range(CHUNKS):
        row = k * CH
        total = [jnp.zeros((CH, H), F32)] * 4
        for m in range(modes):
            real, imag = load_four(out, m, row, 1)
            for i, v in enumerate(zip(unfold4(*real), unfold4(*imag))):
                total[i] = total[i] + (v[0] * v[0] + v[1] * v[1])
        factor = [
            1.0 - quad(amp, (0,), row, q) * lax.rsqrt(total[i] + 1.0) for i, q in enumerate(QUADS)
        ]
        for m in range(modes):
            real, imag = load_four(out, m, row, 1)
            pairs = [
                (factor[i] * v[0], factor[i] * v[1])
                for i, v in enumerate(zip(unfold4(*real), unfold4(*imag)))
            ]
            store_right_four(op, m, row, *fold_pairs(pairs))
    four_products(op, mid, out, rights, lefts, modes)
    for k in range(CHUNKS):
        row = k * CH
        total = [(jnp.zeros((CH, H), F32), jnp.zeros((CH, H), F32))] * 4
        for m in range(modes):
            real, imag = load_four(out, m, row, -1)
            pairs = []
            for i, v in enumerate(zip(unfold4(*real), unfold4(*imag))):
                q = QUADS[i]
                g = mulc(field(q1, (m,), row, q), v)
                total[i] = (total[i][0] + g[0], total[i][1] + g[1])
                pairs.append(mulc(field(obj, (1,), row, q), v))
            store_right_prop(op, m, row, *fold_pairs(pairs))
        for i, q in enumerate(QUADS):
            phase = (quad(phases, (0,), row, q), quad(phases, (1,), row, q))
            g = mulc(phase, total[i])
            put(acc, (1, 0), row, q, g[0])
            put(acc, (1, 1), row, q, g[1])
    prop_products(op, mid, out, rights, lefts, 2, 3, modes)
    for k in range(CHUNKS):
        row = k * CH
        total = [(jnp.zeros((CH, H), F32), jnp.zeros((CH, H), F32))] * 4
        for m in range(modes):
            real, imag = load_prop(out, m, row)
            for i, v in enumerate(zip(unfold4(*real), unfold4(*imag))):
                q = QUADS[i]
                g = mulc(field(probes, (m,), row, q), v)
                total[i] = (total[i][0] + g[0], total[i][1] + g[1])
                t = mulc(field(obj, (0,), row, q), v)
                put(terms, (m, 0), row, q, t[0])
                put(terms, (m, 1), row, q, t[1])
        for i, q in enumerate(QUADS):
            put(acc, (0, 0), row, q, total[i][0])
            put(acc, (0, 1), row, q, total[i][1])
    for m in range(modes):
        for p in range(2):
            terms[m, p] = mirror(terms[m, p])
    for s in range(2):
        for p in range(2):
            grads[s, p] = pltpu.roll(pltpu.roll(mirror(acc[s, p]), y0, 0), x0, 1)


def mirror_kernel(source, target):
    target[0] = mirror(source[0])


def mirrored(images):
    return pl.pallas_call(
        mirror_kernel,
        grid=(images.shape[0],),
        in_specs=[pl.BlockSpec((1, N, N), lambda i: (i, 0, 0))],
        out_specs=pl.BlockSpec((1, N, N), lambda i: (i, 0, 0)),
        out_shape=jax.ShapeDtypeStruct(images.shape, F32),
    )(images)


def compute(corner, own, right, lower, probes, amp):
    rights, lefts, phases = (jnp.asarray(v) for v in constants())
    modes = probes.shape[0]
    flip = mirrored(probes.reshape(-1, N, N)).reshape(probes.shape)
    flip_amp = mirrored(amp)
    vmem = pl.BlockSpec(memory_space=pltpu.VMEM)
    return pl.pallas_call(
        main_kernel,
        in_specs=[pl.BlockSpec(memory_space=pltpu.SMEM)] + [vmem] * 8,
        out_specs=[vmem, vmem],
        out_shape=[
            jax.ShapeDtypeStruct(probes.shape, F32),
            jax.ShapeDtypeStruct(own.shape, F32),
        ],
        scratch_shapes=[
            pltpu.VMEM((2, 2, N, N), F32),
            pltpu.VMEM((modes, 2, N, N), F32),
            pltpu.VMEM((2, modes * N, 2 * N), BF16),
            pltpu.VMEM((2, 2 * N, modes * N), BF16),
            pltpu.VMEM((2, N, modes * N), F32),
            pltpu.VMEM((2, 2, N, N), F32),
        ],
        compiler_params=pltpu.CompilerParams(vmem_limit_bytes=56 * 1024 * 1024),
        cost_estimate=pl.CostEstimate(
            flops=12_000_000_000, bytes_accessed=12 << 20, transcendentals=0
        ),
    )(corner, own, right, lower, flip, flip_amp, rights, lefts, phases)


POS = ("y", "zh", "core")
TILE = ("x", "zl")


def shifted(value, axes, steps):
    count = math.prod(lax.axis_size(axis) for axis in axes)
    first, last = (max(0, -steps), min(count, count - steps))
    return lax.ppermute(value, axes, [(source, source + steps) for source in range(first, last)])


def piece(value, index):
    return lax.dynamic_index_in_dim(value, index, 0, keepdims=False)


def ring(value, axis, step):
    count = lax.axis_size(axis)
    return lax.ppermute(value, axis, [(i, (i + step) % count) for i in range(count)])


def scatter_sum(value, axis):
    count, me = lax.axis_size(axis), lax.axis_index(axis)
    arrived = [
        ring(piece(value, (me + step) % count), axis, step) for step in range(1, count)
    ]
    total = piece(value, me)
    for part in arrived:
        total = total + part
    return total


def gather(value, axis):
    count, me = lax.axis_size(axis), lax.axis_index(axis)
    whole = jnp.zeros((count,) + value.shape, value.dtype)
    whole = lax.dynamic_update_index_in_dim(whole, value, me, 0)
    for step in range(1, count):
        part = ring(value, axis, step)
        whole = lax.dynamic_update_index_in_dim(whole, part, (me + count - step) % count, 0)
    return whole


def exchange_sum(value, axis, bit):
    count = lax.axis_size(axis)
    return value + lax.ppermute(value, axis, [(i, i ^ bit) for i in range(count)])


def total_over_devices(value, order):
    shape = value.shape
    axes = ("core",) + order
    for axis in axes:
        value = scatter_sum(value.reshape(lax.axis_size(axis), -1, N), axis)
    value = exchange_sum(value, "zl", 1)
    value = exchange_sum(value, "zh", 1)
    value = exchange_sum(value, "zh", 2)
    for axis in axes[::-1]:
        value = gather(value, axis)
        value = value.reshape(-1, N)
    return value.reshape(shape)


def per_device(object_field, probe_modes, amplitudes, corners):
    row = lax.broadcasted_iota(jnp.int32, (N, N), 0)
    col = lax.broadcasted_iota(jnp.int32, (N, N), 1)
    y0, x0 = corners[0, 0], corners[0, 1]
    above = shifted(corners, POS, 1)
    y1, x1 = above[0, 0], above[0, 1]
    right = shifted(object_field, TILE, -1)
    mixed = jnp.where(col < x1, right, object_field)
    lower = shifted(mixed, POS, -1)
    terms, grads = compute(corners, object_field, right, lower, probe_modes, amplitudes)
    arrived = shifted(grads, POS, 1)
    probe_grad = total_over_devices(terms, ("x", "y"))
    kept = jnp.where(row >= y0, grads, 0.0)
    taken = jnp.where(row < y1, arrived, 0.0)
    leaving = jnp.where(col < x0, kept, 0.0) + jnp.where(col < x1, taken, 0.0)
    staying = jnp.where(col >= x0, kept, 0.0) + jnp.where(col >= x1, taken, 0.0)
    object_grad = staying + shifted(leaving, TILE, 1)
    return (object_grad, probe_grad)


def solution(mesh):
    split = jax.sharding.Mesh(mesh.devices.reshape(4, 4, 2, 4, 2), POS + TILE)
    in_specs = (
        P(None, None, POS, TILE),
        P(),
        P(POS + TILE, None, None),
        P(POS + TILE, None),
    )
    out_specs = (P(None, None, POS, TILE), P())
    return jax.shard_map(
        per_device, mesh=split, in_specs=in_specs, out_specs=out_specs, check_vma=False
    )
```

time: 512 us -> 192 us (0.38)
  the two profiles are of different devices: /device:TPU:2 before, /device:TPU:17 now
where the time goes in v1:
time: 192 us
  waiting for transfers between devices  101 us (53%)
  starting transfers between devices  50.1 us (26%)
  Pallas kernels  24.7 us (13%)
  other arithmetic  8.57 us (4%)
  local copies, waits for them, and re-layouts  6.21 us (3%)
    ppermute x14, waiting for transfers between devices, ring(): lax.ppermute(value, axis, [(i, (i + step) % count) for i in range(count)])  41.9 us
    ppermute x5, waiting for transfers between devices, shifted(): lax.ppermute(value, axes, [(source, source + steps) for source in range(f...  31.6 us
    ppermute x3, waiting for transfers between devices, exchange_sum(): lax.ppermute(value, axis, [(i, i ^ bit) for i in range(count)])  27.7 us
    ppermute x14, starting transfers between devices, ring(): lax.ppermute(value, axis, [(i, (i + step) % count) for i in range(count)])  26.3 us
    pallas_call x1, Pallas kernels, compute(): pl.pallas_call(main_kernel, in_specs=[pl.BlockSpec(memory_space=pltpu.SME...  16.9 us
    ppermute x5, starting transfers between devices, shifted(): lax.ppermute(value, axes, [(source, source + steps) for source in range(f...  16.6 us
    pallas_call x2, Pallas kernels, mirrored(): pl.pallas_call(mirror_kernel, grid=(images.shape[0],), in_specs=[pl.Block...  7.73 us
    ppermute x3, starting transfers between devices, exchange_sum(): lax.ppermute(value, axis, [(i, i ^ bit) for i in range(count)])  7.24 us
  transfers between devices with their start and end apart: 22, of which 14 were waited for; matrix products, arithmetic and copies ran while one was open for 4% of the time, Pallas kernels for 4%

profile of v1, /device:TPU:17, one launch (start us, length us, event | category | flops | bytes accessed | tf_op | source)
XLA Modules:
  0.0 191.7 jit_solution(17445073249372548955)
XLA Ops:
  1.9 5.5 %collective-permute-start.1 = (s32[1,2]{1,0:T(1,128)}, s32[1,2]{1,0:T(1,128)S(1)}, u32[]{:S(2)}, u32[]{:S(2)}) collective-permute-start(s32[1,2]{1,0:T(1,128)} %corner.1), channel_id=1, source_target_pairs={{0,8},{8,16},{16,24},{24,32},{32,40},{40,48},{48,56},{56,64},{64,7... | collective-permute-start | bytes 32 | tf_op jit(solution)/shard_map/ppermute | solution.py:358
  9.4 17.8 %collective-permute-done.right = f32[2,2,256,256]{3,2,1,0:T(8,128)S(1)} collective-permute-done((f32[2,2,256,256]{3,2,1,0:T(8,128)}, f32[2,2,256,256]{3,2,1,0:T(8,128)S(1)}, u32[]{:S(2)}, u32[]{:S(2)}) %collective-permute-start) | collective-permute-done | bytes 1048608 | tf_op jit(solution)/shard_map/ppermute | solution.py:358
  28.9 3.2 %collective-permute-start.2 = (f32[2,2,256,256]{3,2,1,0:T(8,128)S(1)}, f32[2,2,256,256]{3,2,1,0:T(8,128)S(1)}, u32[]{:S(2)}, u32[]{:S(2)}) collective-permute-start(f32[2,2,256,256]{3,2,1,0:T(8,128)S(1)} %broadcast_select_fusion), channel_id=1, source_target_pairs={{8,0},{16,8},{24,16},{32,24},{40,32},{48,40},{56,48},{64,56},{72,6... | collective-permute-start | bytes 3145736 | tf_op jit(solution)/shard_map/ppermute | solution.py:358
  32.2 6.0 %shard_map.86 = f32[8,256,256]{2,1,0:T(8,128)} custom-call(f32[8,256,256]{2,1,0:T(8,128)} %bitcast.69), custom_call_target="tpu_custom_call" | custom-call | tf_op jit(solution)/shard_map/pallas_call | solution.py:313
  38.1 1.8 shard_map.87.amp
  39.9 13.0 %collective-permute-done.2.lower = f32[2,2,256,256]{3,2,1,0:T(8,128)S(1)} collective-permute-done((f32[2,2,256,256]{3,2,1,0:T(8,128)S(1)}, f32[2,2,256,256]{3,2,1,0:T(8,128)S(1)}, u32[]{:S(2)}, u32[]{:S(2)}) %collective-permute-start.2) | collective-permute-done | bytes 1048608 | tf_op jit(solution)/shard_map/ppermute | solution.py:358
  53.8 16.9 %shard_map.88 = (f32[4,2,256,256]{3,2,1,0:T(8,128)}, f32[2,2,256,256]{3,2,1,0:T(8,128)}) custom-call(s32[1,2]{1,0:T(1,128)} %corner.1, f32[2,2,256,256]{3,2,1,0:T(8,128)} %own.1, f32[2,2,256,256]{3,2,1,0:T(8,128)} %copy-done.3, f32[2,2,256,256]{3,2,1,0:T(8,128)} %copy-done.5, f32[4,2,256,256]{3,2,1,0:T(8,128)} %bitcast.70, f32[1,256,256]{2,1,0:T(8,128)} %shard_map.87.amp, ...), custom_call_target="tpu_custom_call" | custom-call | flops 12000000000 | bytes 12582912 | tf_op jit(solution)/shard_map/pallas_call | solution.py:328
  72.2 7.7 %collective-permute-start.5 = (f32[1024,256]{1,0:T(8,128)S(1)}, f32[1024,256]{1,0:T(8,128)}, u32[]{:S(2)}, u32[]{:S(2)}) collective-permute-start(f32[1024,256]{1,0:T(8,128)S(1)} %dynamic-slice_bitcast_fusion), channel_id=1, source_target_pairs={{0,8},{8,0},{1,9},{9,1},{2,10},{10,2},{3,11},{11,3},{4,12},{12,4},... | collective-permute-start | bytes 3145736 | tf_op jit(solution)/shard_map/ppermute | solution.py:367
  80.0 2.4 %collective-permute-done.5 = f32[1024,256]{1,0:T(8,128)} collective-permute-done((f32[1024,256]{1,0:T(8,128)S(1)}, f32[1024,256]{1,0:T(8,128)}, u32[]{:S(2)}, u32[]{:S(2)}) %collective-permute-start.5) | collective-permute-done | bytes 1048608 | tf_op jit(solution)/shard_map/ppermute | solution.py:367
  87.7 2.1 %collective-permute-start.8 = (f32[256,256]{1,0:T(8,128)S(1)}, f32[256,256]{1,0:T(8,128)S(1)}, u32[]{:S(2)}, u32[]{:S(2)}) collective-permute-start(f32[256,256]{1,0:T(8,128)S(1)} %get-tuple-element.9), channel_id=1, source_target_pairs={{0,6},{2,0},{4,2},{6,4},{1,7},{3,1},{5,3},{7,5},{8,14},{10,8},{12,... | collective-permute-start | bytes 786440 | tf_op jit(solution)/shard_map/ppermute | solution.py:367
  89.8 3.7 %collective-permute-done.6 = f32[256,256]{1,0:T(8,128)S(1)} collective-permute-done((f32[256,256]{1,0:T(8,128)}, f32[256,256]{1,0:T(8,128)S(1)}, u32[]{:S(2)}, u32[]{:S(2)}) %collective-permute-start.6) | collective-permute-done | bytes 262176 | tf_op jit(solution)/shard_map/ppermute | solution.py:367
  93.5 6.4 %collective-permute-done.7 = f32[256,256]{1,0:T(8,128)S(1)} collective-permute-done((f32[256,256]{1,0:T(8,128)S(1)}, f32[256,256]{1,0:T(8,128)S(1)}, u32[]{:S(2)}, u32[]{:S(2)}) %collective-permute-start.7) | collective-permute-done | bytes 262176 | tf_op jit(solution)/shard_map/ppermute | solution.py:367
  100.1 2.4 %collective-permute-start.11 = (f32[64,256]{1,0:T(8,128)S(1)}, f32[64,256]{1,0:T(8,128)S(1)}, u32[]{:S(2)}, u32[]{:S(2)}) collective-permute-start(f32[64,256]{1,0:T(8,128)S(1)} %get-tuple-element.12), channel_id=1, source_target_pairs={{0,192},{64,0},{128,64},{192,128},{1,193},{65,1},{129,65},{193,129... | collective-permute-start | bytes 196616 | tf_op jit(solution)/shard_map/ppermute | solution.py:367
  102.5 2.2 %collective-permute-done.10 = f32[64,256]{1,0:T(8,128)S(1)} collective-permute-done((f32[64,256]{1,0:T(8,128)S(1)}, f32[64,256]{1,0:T(8,128)S(1)}, u32[]{:S(2)}, u32[]{:S(2)}) %collective-permute-start.10) | collective-permute-done | bytes 65568 | tf_op jit(solution)/shard_map/ppermute | solution.py:367
  106.8 2.8 %collective-permute-done.12 = f32[64,256]{1,0:T(8,128)S(1)} collective-permute-done((f32[64,256]{1,0:T(8,128)S(1)}, f32[64,256]{1,0:T(8,128)S(1)}, u32[]{:S(2)}, u32[]{:S(2)}) %collective-permute-start.12) | collective-permute-done | bytes 65568 | tf_op jit(solution)/shard_map/ppermute | solution.py:393
  109.6 2.3 %collective-permute-start.13 = (f32[64,256]{1,0:T(8,128)S(1)}, f32[64,256]{1,0:T(8,128)S(1)}, u32[]{:S(2)}, u32[]{:S(2)}) collective-permute-start(f32[64,256]{1,0:T(8,128)S(1)} %add.197), channel_id=1, source_target_pairs={{0,16},{16,0},{32,48},{48,32},{1,17},{17,1},{33,49},{49,33},{2,18}... | collective-permute-start | bytes 196616 | tf_op jit(solution)/shard_map/ppermute | solution.py:393
  112.5 5.2 %collective-permute-start.3 = (f32[2,2,256,256]{3,2,1,0:T(8,128)S(1)}, f32[2,2,256,256]{3,2,1,0:T(8,128)S(1)}, u32[]{:S(2)}, u32[]{:S(2)}) collective-permute-start(f32[2,2,256,256]{3,2,1,0:T(8,128)S(1)} %copy-done), channel_id=1, source_target_pairs={{0,8},{8,16},{16,24},{24,32},{32,40},{40,48},{48,56},{56,64},{64,7... | collective-permute-start | bytes 3145736 | tf_op jit(solution)/shard_map/ppermute | solution.py:358
  117.8 4.5 %collective-permute-start.14 = (f32[64,256]{1,0:T(8,128)S(1)}, f32[64,256]{1,0:T(8,128)S(1)}, u32[]{:S(2)}, u32[]{:S(2)}) collective-permute-start(f32[64,256]{1,0:T(8,128)S(1)} %add.198), channel_id=1, source_target_pairs={{0,32},{16,48},{32,0},{48,16},{1,33},{17,49},{33,1},{49,17},{2,34}... | collective-permute-start | bytes 196616 | tf_op jit(solution)/shard_map/ppermute | solution.py:393
  123.0 24.9 %collective-permute-done.14 = f32[64,256]{1,0:T(8,128)S(1)} collective-permute-done((f32[64,256]{1,0:T(8,128)S(1)}, f32[64,256]{1,0:T(8,128)S(1)}, u32[]{:S(2)}, u32[]{:S(2)}) %collective-permute-start.14) | collective-permute-done | bytes 65568 | tf_op jit(solution)/shard_map/ppermute | solution.py:393
  149.3 2.5 %collective-permute-start.16 = (f32[64,256]{1,0:T(8,128)S(1)}, f32[64,256]{1,0:T(8,128)S(1)}, u32[]{:S(2)}, u32[]{:S(2)}) collective-permute-start(f32[64,256]{1,0:T(8,128)S(1)} %get-tuple-element.7), channel_id=1, source_target_pairs={{0,128},{64,192},{128,0},{192,64},{1,129},{65,193},{129,1},{193,65... | collective-permute-start | bytes 196616 | tf_op jit(solution)/shard_map/ppermute | solution.py:367
  151.8 2.1 %collective-permute-start.17 = (f32[64,256]{1,0:T(8,128)S(1)}, f32[64,256]{1,0:T(8,128)S(1)}, u32[]{:S(2)}, u32[]{:S(2)}) collective-permute-start(f32[64,256]{1,0:T(8,128)S(1)} %get-tuple-element.7), channel_id=1, source_target_pairs={{0,192},{64,0},{128,64},{192,128},{1,193},{65,1},{129,65},{193,129... | collective-permute-start | bytes 196616 | tf_op jit(solution)/shard_map/ppermute | solution.py:367
  158.5 2.8 %collective-permute-start.19 = (f32[256,256]{1,0:T(8,128)S(1)}, f32[256,256]{1,0:T(8,128)S(1)}, u32[]{:S(2)}, u32[]{:S(2)}) collective-permute-start(f32[256,256]{1,0:T(8,128)S(1)} %bitcast.74), channel_id=1, source_target_pairs={{0,4},{2,6},{4,0},{6,2},{1,5},{3,7},{5,1},{7,3},{8,12},{10,14},{12... | collective-permute-start | bytes 786440 | tf_op jit(solution)/shard_map/ppermute | solution.py:367
  163.1 18.0 %collective-permute-done.18 = f32[256,256]{1,0:T(8,128)S(1)} collective-permute-done((f32[256,256]{1,0:T(8,128)S(1)}, f32[256,256]{1,0:T(8,128)S(1)}, u32[]{:S(2)}, u32[]{:S(2)}) %collective-permute-start.18) | collective-permute-done | bytes 262176 | tf_op jit(solution)/shard_map/ppermute | solution.py:367
  181.2 6.2 %collective-permute-done.19 = f32[256,256]{1,0:T(8,128)S(1)} collective-permute-done((f32[256,256]{1,0:T(8,128)S(1)}, f32[256,256]{1,0:T(8,128)S(1)}, u32[]{:S(2)}, u32[]{:S(2)}) %collective-permute-start.19) | collective-permute-done | bytes 262176 | tf_op jit(solution)/shard_map/ppermute | solution.py:367
  (65 shorter events, 28.3 us)
Async XLA Ops:
  0.6 26.5 %collective-permute-start = (f32[2,2,256,256]{3,2,1,0:T(8,128)}, f32[2,2,256,256]{3,2,1,0:T(8,128)S(1)}, u32[]{:S(2)}, u32[]{:S(2)}) collective-permute-start(f32[2,2,256,256]{3,2,1,0:T(8,128)} %own.1), channel_id=1, source_target_pairs={{1,0},{2,1},{3,2},{4,3},{5,4},{6,5},{7,6},{9,8},{10,9},{11,10},{12... | collective-permute-start | bytes 3145736 | tf_op jit(solution)/shard_map/ppermute | solution.py:358
  1.9 6.3 %collective-permute-start.1 = (s32[1,2]{1,0:T(1,128)}, s32[1,2]{1,0:T(1,128)S(1)}, u32[]{:S(2)}, u32[]{:S(2)}) collective-permute-start(s32[1,2]{1,0:T(1,128)} %corner.1), channel_id=1, source_target_pairs={{0,8},{8,16},{16,24},{24,32},{32,40},{40,48},{48,56},{56,64},{64,7... | collective-permute-start | bytes 32 | tf_op jit(solution)/shard_map/ppermute | solution.py:358
  28.9 24.0 %collective-permute-start.2 = (f32[2,2,256,256]{3,2,1,0:T(8,128)S(1)}, f32[2,2,256,256]{3,2,1,0:T(8,128)S(1)}, u32[]{:S(2)}, u32[]{:S(2)}) collective-permute-start(f32[2,2,256,256]{3,2,1,0:T(8,128)S(1)} %broadcast_select_fusion), channel_id=1, source_target_pairs={{8,0},{16,8},{24,16},{32,24},{40,32},{48,40},{56,48},{64,56},{72,6... | collective-permute-start | bytes 3145736 | tf_op jit(solution)/shard_map/ppermute | solution.py:358
  72.2 10.2 %collective-permute-start.5 = (f32[1024,256]{1,0:T(8,128)S(1)}, f32[1024,256]{1,0:T(8,128)}, u32[]{:S(2)}, u32[]{:S(2)}) collective-permute-start(f32[1024,256]{1,0:T(8,128)S(1)} %dynamic-slice_bitcast_fusion), channel_id=1, source_target_pairs={{0,8},{8,0},{1,9},{9,1},{2,10},{10,2},{3,11},{11,3},{4,12},{12,4},... | collective-permute-start | bytes 3145736 | tf_op jit(solution)/shard_map/ppermute | solution.py:367
  83.8 28.2 %copy-start.4 = (s32[1,2]{1,0:T(1,128)S(1)}, s32[1,2]{1,0:T(1,128)}, u32[]{:S(2)}) copy-start(s32[1,2]{1,0:T(1,128)} %corner.1) | copy-start | bytes 28
  83.8 28.7 %copy-start = (f32[2,2,256,256]{3,2,1,0:T(8,128)S(1)}, f32[2,2,256,256]{3,2,1,0:T(8,128)}, u32[]{:S(2)}) copy-start(f32[2,2,256,256]{3,2,1,0:T(8,128)} %get-tuple-element.4) | copy-start | bytes 3145732
  84.5 8.9 %collective-permute-start.6 = (f32[256,256]{1,0:T(8,128)}, f32[256,256]{1,0:T(8,128)S(1)}, u32[]{:S(2)}, u32[]{:S(2)}) collective-permute-start(f32[256,256]{1,0:T(8,128)} %get-tuple-element.8), channel_id=1, source_target_pairs={{0,2},{2,4},{4,6},{6,0},{1,3},{3,5},{5,7},{7,1},{8,10},{10,12},{12... | collective-permute-start | bytes 786440 | tf_op jit(solution)/shard_map/ppermute | solution.py:367
  86.2 13.7 %collective-permute-start.7 = (f32[256,256]{1,0:T(8,128)S(1)}, f32[256,256]{1,0:T(8,128)S(1)}, u32[]{:S(2)}, u32[]{:S(2)}) collective-permute-start(f32[256,256]{1,0:T(8,128)S(1)} %get-tuple-element.10), channel_id=1, source_target_pairs={{0,4},{2,6},{4,0},{6,2},{1,5},{3,7},{5,1},{7,3},{8,12},{10,14},{12... | collective-permute-start | bytes 786440 | tf_op jit(solution)/shard_map/ppermute | solution.py:367
  87.7 12.2 %collective-permute-start.8 = (f32[256,256]{1,0:T(8,128)S(1)}, f32[256,256]{1,0:T(8,128)S(1)}, u32[]{:S(2)}, u32[]{:S(2)}) collective-permute-start(f32[256,256]{1,0:T(8,128)S(1)} %get-tuple-element.9), channel_id=1, source_target_pairs={{0,6},{2,0},{4,2},{6,4},{1,7},{3,1},{5,3},{7,5},{8,14},{10,8},{12,... | collective-permute-start | bytes 786440 | tf_op jit(solution)/shard_map/ppermute | solution.py:367
  100.0 4.7 %collective-permute-start.10 = (f32[64,256]{1,0:T(8,128)S(1)}, f32[64,256]{1,0:T(8,128)S(1)}, u32[]{:S(2)}, u32[]{:S(2)}) collective-permute-start(f32[64,256]{1,0:T(8,128)S(1)} %get-tuple-element.13), channel_id=1, source_target_pairs={{0,128},{64,192},{128,0},{192,64},{1,129},{65,193},{129,1},{193,65... | collective-permute-start | bytes 196616 | tf_op jit(solution)/shard_map/ppermute | solution.py:367
  100.1 4.6 %collective-permute-start.11 = (f32[64,256]{1,0:T(8,128)S(1)}, f32[64,256]{1,0:T(8,128)S(1)}, u32[]{:S(2)}, u32[]{:S(2)}) collective-permute-start(f32[64,256]{1,0:T(8,128)S(1)} %get-tuple-element.12), channel_id=1, source_target_pairs={{0,192},{64,0},{128,64},{192,128},{1,193},{65,1},{129,65},{193,129... | collective-permute-start | bytes 196616 | tf_op jit(solution)/shard_map/ppermute | solution.py:367
  102.5 3.8 %collective-permute-start.9 = (f32[64,256]{1,0:T(8,128)S(1)}, f32[64,256]{1,0:T(8,128)S(1)}, u32[]{:S(2)}, u32[]{:S(2)}) collective-permute-start(f32[64,256]{1,0:T(8,128)S(1)} %get-tuple-element.11), channel_id=1, source_target_pairs={{0,64},{64,128},{128,192},{192,0},{1,65},{65,129},{129,193},{193,1... | collective-permute-start | bytes 196616 | tf_op jit(solution)/shard_map/ppermute | solution.py:367
  106.4 3.2 %collective-permute-start.12 = (f32[64,256]{1,0:T(8,128)S(1)}, f32[64,256]{1,0:T(8,128)S(1)}, u32[]{:S(2)}, u32[]{:S(2)}) collective-permute-start(f32[64,256]{1,0:T(8,128)S(1)} %fusion.3), channel_id=1, source_target_pairs={{0,1},{1,0},{2,3},{3,2},{4,5},{5,4},{6,7},{7,6},{8,9},{9,8},{10,11... | collective-permute-start | bytes 196616 | tf_op jit(solution)/shard_map/ppermute | solution.py:393
  109.6 8.2 %collective-permute-start.13 = (f32[64,256]{1,0:T(8,128)S(1)}, f32[64,256]{1,0:T(8,128)S(1)}, u32[]{:S(2)}, u32[]{:S(2)}) collective-permute-start(f32[64,256]{1,0:T(8,128)S(1)} %add.197), channel_id=1, source_target_pairs={{0,16},{16,0},{32,48},{48,32},{1,17},{17,1},{33,49},{49,33},{2,18}... | collective-permute-start | bytes 196616 | tf_op jit(solution)/shard_map/ppermute | solution.py:393
  112.5 44.3 %collective-permute-start.3 = (f32[2,2,256,256]{3,2,1,0:T(8,128)S(1)}, f32[2,2,256,256]{3,2,1,0:T(8,128)S(1)}, u32[]{:S(2)}, u32[]{:S(2)}) collective-permute-start(f32[2,2,256,256]{3,2,1,0:T(8,128)S(1)} %copy-done), channel_id=1, source_target_pairs={{0,8},{8,16},{16,24},{24,32},{32,40},{40,48},{48,56},{56,64},{64,7... | collective-permute-start | bytes 3145736 | tf_op jit(solution)/shard_map/ppermute | solution.py:358
  117.8 30.0 %collective-permute-start.14 = (f32[64,256]{1,0:T(8,128)S(1)}, f32[64,256]{1,0:T(8,128)S(1)}, u32[]{:S(2)}, u32[]{:S(2)}) collective-permute-start(f32[64,256]{1,0:T(8,128)S(1)} %add.198), channel_id=1, source_target_pairs={{0,32},{16,48},{32,0},{48,16},{1,33},{17,49},{33,1},{49,17},{2,34}... | collective-permute-start | bytes 196616 | tf_op jit(solution)/shard_map/ppermute | solution.py:393
  147.9 6.0 %collective-permute-start.15 = (f32[64,256]{1,0:T(8,128)S(1)}, f32[64,256]{1,0:T(8,128)S(1)}, u32[]{:S(2)}, u32[]{:S(2)}) collective-permute-start(f32[64,256]{1,0:T(8,128)S(1)} %get-tuple-element.7), channel_id=1, source_target_pairs={{0,64},{64,128},{128,192},{192,0},{1,65},{65,129},{129,193},{193,1... | collective-permute-start | bytes 196616 | tf_op jit(solution)/shard_map/ppermute | solution.py:367
  149.3 4.7 %collective-permute-start.16 = (f32[64,256]{1,0:T(8,128)S(1)}, f32[64,256]{1,0:T(8,128)S(1)}, u32[]{:S(2)}, u32[]{:S(2)}) collective-permute-start(f32[64,256]{1,0:T(8,128)S(1)} %get-tuple-element.7), channel_id=1, source_target_pairs={{0,128},{64,192},{128,0},{192,64},{1,129},{65,193},{129,1},{193,65... | collective-permute-start | bytes 196616 | tf_op jit(solution)/shard_map/ppermute | solution.py:367
  151.8 3.4 %collective-permute-start.17 = (f32[64,256]{1,0:T(8,128)S(1)}, f32[64,256]{1,0:T(8,128)S(1)}, u32[]{:S(2)}, u32[]{:S(2)}) collective-permute-start(f32[64,256]{1,0:T(8,128)S(1)} %get-tuple-element.7), channel_id=1, source_target_pairs={{0,192},{64,0},{128,64},{192,128},{1,193},{65,1},{129,65},{193,129... | collective-permute-start | bytes 196616 | tf_op jit(solution)/shard_map/ppermute | solution.py:367
  155.2 25.9 %collective-permute-start.18 = (f32[256,256]{1,0:T(8,128)S(1)}, f32[256,256]{1,0:T(8,128)S(1)}, u32[]{:S(2)}, u32[]{:S(2)}) collective-permute-start(f32[256,256]{1,0:T(8,128)S(1)} %bitcast.73), channel_id=1, source_target_pairs={{0,2},{2,4},{4,6},{6,0},{1,3},{3,5},{5,7},{7,1},{8,10},{10,12},{12... | collective-permute-start | bytes 786440 | tf_op jit(solution)/shard_map/ppermute | solution.py:367
  157.1 31.8 %collective-permute-start.4 = (f32[2,2,256,256]{3,2,1,0:T(8,128)S(1)}, f32[2,2,256,256]{3,2,1,0:T(8,128)S(1)}, u32[]{:S(2)}, u32[]{:S(2)}) collective-permute-start(f32[2,2,256,256]{3,2,1,0:T(8,128)S(1)} %select_add_fusion), channel_id=1, source_target_pairs={{0,1},{1,2},{2,3},{3,4},{4,5},{5,6},{6,7},{8,9},{9,10},{10,11},{11... | collective-permute-start | bytes 3145736 | tf_op jit(solution)/shard_map/ppermute | solution.py:358
  158.5 28.9 %collective-permute-start.19 = (f32[256,256]{1,0:T(8,128)S(1)}, f32[256,256]{1,0:T(8,128)S(1)}, u32[]{:S(2)}, u32[]{:S(2)}) collective-permute-start(f32[256,256]{1,0:T(8,128)S(1)} %bitcast.74), channel_id=1, source_target_pairs={{0,4},{2,6},{4,0},{6,2},{1,5},{3,7},{5,1},{7,3},{8,12},{10,14},{12... | collective-permute-start | bytes 786440 | tf_op jit(solution)/shard_map/ppermute | solution.py:367
  161.3 26.1 %collective-permute-start.20 = (f32[256,256]{1,0:T(8,128)S(1)}, f32[256,256]{1,0:T(8,128)S(1)}, u32[]{:S(2)}, u32[]{:S(2)}) collective-permute-start(f32[256,256]{1,0:T(8,128)S(1)} %bitcast.75), channel_id=1, source_target_pairs={{0,6},{2,0},{4,2},{6,4},{1,7},{3,1},{5,3},{7,5},{8,14},{10,8},{12,... | collective-permute-start | bytes 786440 | tf_op jit(solution)/shard_map/ppermute | solution.py:367
  187.4 2.8 %collective-permute-start.21 = (f32[1024,256]{1,0:T(8,128)S(1)}, f32[1024,256]{1,0:T(8,128)S(1)}, u32[]{:S(2)}, u32[]{:S(2)}) collective-permute-start(f32[1024,256]{1,0:T(8,128)S(1)} %bitcast.64), channel_id=1, source_target_pairs={{0,8},{8,0},{1,9},{9,1},{2,10},{10,2},{3,11},{11,3},{4,12},{12,4},... | collective-permute-start | bytes 3145736 | tf_op jit(solution)/shard_map/ppermute | solution.py:367
  (4 other events, 24.9 us)

commit v2 on v1

--- a/solution.py
+++ b/solution.py
@@ -31,26 +31,18 @@
     for part in ((straight + turned) / 2, (straight - turned) / 2):
         for side in (part, np.conj(part)):
             real, imag = side.real, side.imag
-            right = np.block([[real, imag], [-imag, real]])
-            high, low = split_np(right)
-            mats.append(np.concatenate([high, high, low], axis=0))
-            left = np.block([[real, -imag], [imag, real]])
-            high, low = split_np(left)
-            mats.append(np.concatenate([high, high, low], axis=1))
+            mats.append(np.stack(split_np(np.block([[real, imag], [-imag, real]]))))
     half = np.arange(H) - 127.5
     angle = 2 * np.pi * np.outer(half, half) / N
     zero = np.zeros((H, H))
     both = np.block([[np.cos(angle) / 16, zero], [zero, np.sin(angle) / 16]])
-    high, low = split_np(both)
-    right_b = np.concatenate([high, high, low], axis=0)
-    left_b = np.concatenate([high, high, low], axis=1)
-    rights = np.stack([mats[0], mats[4], mats[2], mats[6], right_b])
-    lefts = np.stack([mats[1], mats[5], mats[3], mats[7], left_b])
+    mats.append(np.stack(split_np(both)))
+    table = np.stack(mats)
     order = np.concatenate([np.arange(H), N - 1 - np.arange(H)])
     tilt = np.exp(-2j * np.pi * 127.5 * order / N)
     phase = np.outer(tilt, tilt)
     phases = np.stack([phase.real, phase.imag]).astype(np.float32)
-    return rights, lefts, phases
+    return table, phases
 
 
 def mirror(value):
@@ -122,15 +114,24 @@
             op[part, rows, N + c * H : N + c * H + H] = low
 
 
+def stack_rows(table, which):
+    return jnp.concatenate([table[which, 0], table[which, 0], table[which, 1]], axis=0)
+
+
+def stack_cols(table, which):
+    return jnp.concatenate([table[which, 0], table[which, 0], table[which, 1]], axis=1)
+
+
 def three(ref_value):
     return jnp.concatenate([ref_value, ref_value[:, :N]], axis=1)
 
 
-def prop_products(op, mid, out, rights, lefts, even, odd, modes):
-    for c, which in ((0, even), (1, odd)):
+def prop_products(op, mid, out, table, conjugate, modes):
+    for c in (0, 1):
+        matrix = stack_rows(table, 2 * c + conjugate)
         for m in range(modes):
             rows = slice(m * N, m * N + N)
-            res = dot(three(op[c, rows, :]), rights[which])
+            res = dot(three(op[c, rows, :]), matrix)
             high, low = parts(res)
             for level, value in ((0, high), (1, low)):
                 for r in (0, 1):
@@ -140,28 +141,31 @@
                             level * N + p * H : level * N + p * H + H,
                             m * N + c * H : m * N + c * H + H,
                         ] = value[r * H : r * H + H, p * H : p * H + H]
-    for r, which in ((0, even), (1, odd)):
+    for r in (0, 1):
+        matrix = stack_cols(table, 2 * r + 1 - conjugate)
         for m in range(modes):
             cols = slice(m * N, m * N + N)
             x = mid[r, :, cols]
             x = jnp.concatenate([x, x[:N]], axis=0)
-            out[r, :, cols] = dot(lefts[which], x)
-
-
-def four_products(op, mid, out, rights, lefts, modes):
+            out[r, :, cols] = dot(matrix, x)
+
+
+def four_products(op, mid, out, table, modes):
+    matrix = stack_rows(table, 4)
     for p in (0, 1):
         for m in range(modes):
             rows = slice(m * N, m * N + N)
-            res = dot(three(op[p, rows, :]), rights[4])
+            res = dot(three(op[p, rows, :]), matrix)
             high, low = parts(res)
             mid[p, :N, m * N : m * N + N] = high
             mid[p, N:, m * N : m * N + N] = low
+    matrix = stack_cols(table, 4)
     for p in (0, 1):
         for m in range(modes):
             cols = slice(m * N, m * N + N)
             x = mid[p, :, cols]
             x = jnp.concatenate([x, x[:N]], axis=0)
-            out[p, :, cols] = dot(lefts[4], x)
+            out[p, :, cols] = dot(matrix, x)
 
 
 def load_prop(out, mode, row):
@@ -202,21 +206,23 @@
 
 
 def main_kernel(
-    corner, own, right, lower, probes, amp, rights, lefts, phases,
+    place, own, right, other, probes, amp, table, phases,
     terms, grads,
     obj, q1, op, mid, out, acc,
 ):
     modes = probes.shape[0]
-    y0, x0 = corner[0, 0], corner[0, 1]
+    y0, x0, odd, live = place[0], place[1], place[2], place[3]
     up = lax.rem(N - y0, N)
     back = lax.rem(N - x0, N)
-    below = lax.broadcasted_iota(jnp.int32, (N, N), 0) < y0
+    rows = lax.broadcasted_iota(jnp.int32, (N, N), 0)
+    mine = jnp.where(rows >= y0, 1 - odd, odd) > 0
     beside = lax.broadcasted_iota(jnp.int32, (N, N), 1) < x0
+    scale = live.astype(F32)
     for s in range(2):
         window = []
         for p in range(2):
-            upper = jnp.where(beside, right[s, p], own[s, p])
-            value = jnp.where(below, lower[s, p], upper)
+            value = jnp.where(beside, right[s, p], own[s, p]) * scale
+            value = jnp.where(mine, value, other[s, p])
             value = pltpu.roll(pltpu.roll(value, up, 0), back, 1)
             window.append(mirror(value))
         if s == 1:
@@ -234,7 +240,7 @@
             row = k * CH
             pairs = [mul(field(probes, (m,), row, q), field(obj, (0,), row, q)) for q in QUADS]
             store_right_prop(op, m, row, *fold_pairs(pairs))
-    prop_products(op, mid, out, rights, lefts, 0, 1, modes)
+    prop_products(op, mid, out, table, 0, modes)
     for m in range(modes):
         for k in range(CHUNKS):
             row = k * CH
@@ -245,7 +251,7 @@
                 put(q1, (m, 1), row, q, v[1])
             pairs = [mul(v, field(obj, (1,), row, q)) for q, v in zip(QUADS, pixels)]
             store_right_four(op, m, row, *fold_pairs(pairs))
-    four_products(op, mid, out, rights, lefts, modes)
+    four_products(op, mid, out, table, modes)
     for k in range(CHUNKS):
         row = k * CH
         total = [jnp.zeros((CH, H), F32)] * 4
@@ -263,7 +269,7 @@
                 for i, v in enumerate(zip(unfold4(*real), unfold4(*imag)))
             ]
             store_right_four(op, m, row, *fold_pairs(pairs))
-    four_products(op, mid, out, rights, lefts, modes)
+    four_products(op, mid, out, table, modes)
     for k in range(CHUNKS):
         row = k * CH
         total = [(jnp.zeros((CH, H), F32), jnp.zeros((CH, H), F32))] * 4
@@ -281,7 +287,7 @@
             g = mulc(phase, total[i])
             put(acc, (1, 0), row, q, g[0])
             put(acc, (1, 1), row, q, g[1])
-    prop_products(op, mid, out, rights, lefts, 2, 3, modes)
+    prop_products(op, mid, out, table, 1, modes)
     for k in range(CHUNKS):
         row = k * CH
         total = [(jnp.zeros((CH, H), F32), jnp.zeros((CH, H), F32))] * 4
@@ -319,15 +325,15 @@
     )(images)
 
 
-def compute(corner, own, right, lower, probes, amp):
-    rights, lefts, phases = (jnp.asarray(v) for v in constants())
+def compute(place, own, right, other, probes, amp):
+    table, phases = (jnp.asarray(v) for v in constants())
     modes = probes.shape[0]
     flip = mirrored(probes.reshape(-1, N, N)).reshape(probes.shape)
     flip_amp = mirrored(amp)
     vmem = pl.BlockSpec(memory_space=pltpu.VMEM)
     return pl.pallas_call(
         main_kernel,
-        in_specs=[pl.BlockSpec(memory_space=pltpu.SMEM)] + [vmem] * 8,
+        in_specs=[pl.BlockSpec(memory_space=pltpu.SMEM)] + [vmem] * 7,
         out_specs=[vmem, vmem],
         out_shape=[
             jax.ShapeDtypeStruct(probes.shape, F32),
@@ -341,15 +347,17 @@
             pltpu.VMEM((2, N, modes * N), F32),
             pltpu.VMEM((2, 2, N, N), F32),
         ],
-        compiler_params=pltpu.CompilerParams(vmem_limit_bytes=56 * 1024 * 1024),
+        compiler_params=pltpu.CompilerParams(vmem_limit_bytes=48 * 1024 * 1024),
         cost_estimate=pl.CostEstimate(
             flops=12_000_000_000, bytes_accessed=12 << 20, transcendentals=0
         ),
-    )(corner, own, right, lower, flip, flip_amp, rights, lefts, phases)
+    )(place, own, right, other, flip, flip_amp, table, phases)
 
 
 POS = ("y", "zh", "core")
 TILE = ("x", "zl")
+ROWS = 32
+COLUMNS = 8
 
 
 def shifted(value, axes, steps):
@@ -367,15 +375,22 @@
     return lax.ppermute(value, axis, [(i, (i + step) % count) for i in range(count)])
 
 
-def scatter_sum(value, axis):
+def pieces(value, axis):
     count, me = lax.axis_size(axis), lax.axis_index(axis)
-    arrived = [
-        ring(piece(value, (me + step) % count), axis, step) for step in range(1, count)
-    ]
-    total = piece(value, me)
+    value = value.reshape(count, -1, N)
+    return [piece(value, (me + step) % count) for step in range(1, count)] + [piece(value, me)]
+
+
+def scatter_sum(parts, axis):
+    arrived = [ring(part, axis, step + 1) for step, part in enumerate(parts[:-1])]
+    total = parts[-1]
     for part in arrived:
         total = total + part
     return total
+
+
+def after(value, *others):
+    return lax.optimization_barrier((value,) + others)[0]
 
 
 def gather(value, axis):
@@ -393,37 +408,57 @@
     return value + lax.ppermute(value, axis, [(i, i ^ bit) for i in range(count)])
 
 
-def total_over_devices(value, order):
-    shape = value.shape
-    axes = ("core",) + order
-    for axis in axes:
-        value = scatter_sum(value.reshape(lax.axis_size(axis), -1, N), axis)
+def spread(value, order):
     value = exchange_sum(value, "zl", 1)
     value = exchange_sum(value, "zh", 1)
     value = exchange_sum(value, "zh", 2)
-    for axis in axes[::-1]:
-        value = gather(value, axis)
-        value = value.reshape(-1, N)
-    return value.reshape(shape)
+    for axis in order[::-1] + ("core",):
+        value = gather(value, axis).reshape(-1, N)
+    return value
+
+
+def moved(value, even, odd):
+    pairs = []
+    for row in range(ROWS):
+        for column in range(COLUMNS):
+            target = row + (odd if column % 2 else even)
+            if column % 2:
+                target %= ROWS
+            if 0 <= target < ROWS:
+                pairs.append((row * COLUMNS + column, target * COLUMNS + column))
+    return lax.ppermute(value, POS + TILE, pairs)
 
 
 def per_device(object_field, probe_modes, amplitudes, corners):
     row = lax.broadcasted_iota(jnp.int32, (N, N), 0)
     col = lax.broadcasted_iota(jnp.int32, (N, N), 1)
-    y0, x0 = corners[0, 0], corners[0, 1]
-    above = shifted(corners, POS, 1)
-    y1, x1 = above[0, 0], above[0, 1]
+    odd = lax.axis_index("zl")
+    is_odd = odd == 1
+    first = (lax.axis_index(POS) == 0) & is_odd
+    above = lax.ppermute(corners, POS, [(i, (i + 1) % ROWS) for i in range(ROWS)])
+    yp, xp = [jnp.where(is_odd, above[0, i], corners[0, i]) for i in (0, 1)]
+    yq, xq = [jnp.where(is_odd, corners[0, i], above[0, i]) for i in (0, 1)]
+    amplitude = moved(amplitudes, 0, 1)
     right = shifted(object_field, TILE, -1)
-    mixed = jnp.where(col < x1, right, object_field)
-    lower = shifted(mixed, POS, -1)
-    terms, grads = compute(corners, object_field, right, lower, probe_modes, amplitudes)
-    arrived = shifted(grads, POS, 1)
-    probe_grad = total_over_devices(terms, ("x", "y"))
-    kept = jnp.where(row >= y0, grads, 0.0)
-    taken = jnp.where(row < y1, arrived, 0.0)
-    leaving = jnp.where(col < x0, kept, 0.0) + jnp.where(col < x1, taken, 0.0)
-    staying = jnp.where(col >= x0, kept, 0.0) + jnp.where(col >= x1, taken, 0.0)
-    object_grad = staying + shifted(leaving, TILE, 1)
+    mixed = jnp.where(col < xq, right, object_field)
+    other = moved(mixed, -1, 1)
+    live = jnp.where(first, 0, 1)
+    place = jnp.stack([yp, xp, odd, live]).astype(jnp.int32)
+    terms, grads = compute(place, object_field, right, other, probe_modes, amplitude)
+    arrived = moved(grads, 1, -1)
+    partial = scatter_sum(pieces(terms, "core"), "core")
+    across = pieces(partial, "x")
+    partial = scatter_sum(across, "x")
+    partial = scatter_sum(pieces(partial, "y"), "y")
+    arrived = after(arrived, *across)
+    kept = jnp.where(((row >= yp) != is_odd) & ~first, grads, 0.0)
+    taken = jnp.where((row < yq) != is_odd, arrived, 0.0)
+    leaving = jnp.where(col < xp, kept, 0.0) + jnp.where(col < xq, taken, 0.0)
+    staying = jnp.where(col >= xp, kept, 0.0) + jnp.where(col >= xq, taken, 0.0)
+    received = shifted(leaving, TILE, 1)
+    partial = after(partial, received)
+    object_grad = staying + received
+    probe_grad = spread(partial, ("x", "y")).reshape(terms.shape)
     return (object_grad, probe_grad)
 
 

time: 192 us -> 171 us (0.89)
  the two profiles are of different devices: /device:TPU:17 before, /device:TPU:1 now
where the time goes in v2:
time: 171 us; the launch traced here: 170 us
  waiting for transfers between devices  60.7 us (35%)
  starting transfers between devices  60.2 us (35%)
  Pallas kernels  22.5 us (13%)
  local copies, waits for them, and re-layouts  12.2 us (7%)
  other arithmetic  8.67 us (5%)
  between operations  5.91 us (3%)
    ppermute x2, waiting for transfers between devices, shifted(): lax.ppermute(value, axes, [(source, source + steps) for source in range(f...  26.6 us
    ppermute x14, starting transfers between devices, ring(): lax.ppermute(value, axis, [(i, (i + step) % count) for i in range(count)])  26 us
    ppermute x14, waiting for transfers between devices, ring(): lax.ppermute(value, axis, [(i, (i + step) % count) for i in range(count)])  24.9 us
    pallas_call x1, Pallas kernels, compute(): pl.pallas_call(main_kernel, in_specs=[pl.BlockSpec(memory_space=pltpu.SME...  14.7 us
    ppermute x3, starting transfers between devices, exchange_sum(): lax.ppermute(value, axis, [(i, i ^ bit) for i in range(count)])  14 us
    ppermute x3, starting transfers between devices, moved(): return lax.ppermute(value, POS + TILE, pairs)  13.1 us
    pallas_call x2, Pallas kernels, mirrored(): pl.pallas_call(mirror_kernel, grid=(images.shape[0],), in_specs=[pl.Block...  7.79 us
    unnamed x16, local copies, waits for them, and re-layouts  6.9 us
  transfers between devices with their start and end apart: 23, of which 17 were waited for; matrix products, arithmetic and copies ran while one was open for 5% of the time, Pallas kernels for 5%

profile of v2, /device:TPU:1, one launch (start us, length us, event | category | flops | bytes accessed | tf_op | source)
XLA Modules:
  0.0 170.3 jit_solution(16460653932250104008)
XLA Ops:
  1.9 4.5 %collective-permute-start = (s32[1,2]{1,0:T(1,128)}, s32[1,2]{1,0:T(1,128)S(1)}, u32[]{:S(2)}, u32[]{:S(2)}) collective-permute-start(s32[1,2]{1,0:T(1,128)} %param.9), channel_id=1, source_target_pairs={{0,8},{8,16},{16,24},{24,32},{32,40},{40,48},{48,56},{56,64},{64,7... | collective-permute-start | bytes 32 | tf_op jit(solution)/shard_map/ppermute | solution.py:438
  9.6 16.5 %collective-permute-done.1.right = f32[2,2,256,256]{3,2,1,0:T(8,128)S(1)} collective-permute-done((f32[2,2,256,256]{3,2,1,0:T(8,128)}, f32[2,2,256,256]{3,2,1,0:T(8,128)S(1)}, u32[]{:S(2)}, u32[]{:S(2)}) %collective-permute-start.1) | collective-permute-done | bytes 1048608 | tf_op jit(solution)/shard_map/ppermute | solution.py:366
  26.2 2.3 %broadcast_select_fusion = f32[2,2,256,256]{3,2,1,0:T(8,128)} fusion(f32[2,2,256,256]{3,2,1,0:T(8,128)S(1)} %collective-permute-done.1.right, f32[2,2,256,256]{3,2,1,0:T(8,128)} %own.1, pred[256]{0:T(512)(128)(4,1)S(1)} %iota_compare_fusion.2), kind=kLoop, calls=%fused_computation.6 | loop fusion | flops 262144 | bytes 3145984 | tf_op jit(solution)/shard_map/jit(_where)/select_n | solution.py:443
  28.5 5.0 %collective-permute-start.2 = (f32[2,2,256,256]{3,2,1,0:T(8,128)}, f32[2,2,256,256]{3,2,1,0:T(8,128)S(1)}, u32[]{:S(2)}, u32[]{:S(2)}) collective-permute-start(f32[2,2,256,256]{3,2,1,0:T(8,128)} %broadcast_select_fusion), channel_id=1, source_target_pairs={{1,9},{3,11},{5,13},{7,15},{8,0},{9,17},{10,2},{11,19},{12,4},{13,... | collective-permute-start | bytes 3145736 | tf_op jit(solution)/shard_map/ppermute | solution.py:429
  35.2 6.0 %shard_map.77 = f32[8,256,256]{2,1,0:T(8,128)} custom-call(f32[8,256,256]{2,1,0:T(8,128)} %bitcast.70), custom_call_target="tpu_custom_call" | custom-call | tf_op jit(solution)/shard_map/pallas_call | solution.py:319
  46.3 2.9 %collective-permute-done.2.other = f32[2,2,256,256]{3,2,1,0:T(8,128)S(1)} collective-permute-done((f32[2,2,256,256]{3,2,1,0:T(8,128)}, f32[2,2,256,256]{3,2,1,0:T(8,128)S(1)}, u32[]{:S(2)}, u32[]{:S(2)}) %collective-permute-start.2) | collective-permute-done | bytes 1048608 | tf_op jit(solution)/shard_map/ppermute | solution.py:429
  53.3 14.7 %shard_map.79 = (f32[4,2,256,256]{3,2,1,0:T(8,128)}, f32[2,2,256,256]{3,2,1,0:T(8,128)S(1)}) custom-call(s32[4]{0:T(128)S(1)} %pad_add_fusion.place, f32[2,2,256,256]{3,2,1,0:T(8,128)S(1)} %copy-done, f32[2,2,256,256]{3,2,1,0:T(8,128)S(1)} %collective-permute-done.1.right, f32[2,2,256,256]{3,2,1,0:T(8,128)S(1)} %copy-done.3, f32[4,2,256,256]{3,2,1,0:T(8,128)} %bitcast.71, ...), custom_call_target="tpu_custom_call" | custom-call | flops 12000000000 | bytes 12582912 | tf_op jit(solution)/shard_map/pallas_call | solution.py:334
  69.5 6.5 %collective-permute-start.4 = (f32[2,2,256,256]{3,2,1,0:T(8,128)S(1)}, f32[2,2,256,256]{3,2,1,0:T(8,128)S(1)}, u32[]{:S(2)}, u32[]{:S(2)}) collective-permute-start(f32[2,2,256,256]{3,2,1,0:T(8,128)S(1)} %get-tuple-element.6), channel_id=1, source_target_pairs={{0,8},{1,249},{2,10},{3,251},{4,12},{5,253},{6,14},{7,255},{8,16},... | collective-permute-start | bytes 3145736 | tf_op jit(solution)/shard_map/ppermute | solution.py:429
  78.6 4.4 %collective-permute-start.9 = (f32[256,256]{1,0:T(8,128)}, f32[256,256]{1,0:T(8,128)S(1)}, u32[]{:S(2)}, u32[]{:S(2)}) collective-permute-start(f32[256,256]{1,0:T(8,128)} %get-tuple-element.14), channel_id=1, source_target_pairs={{0,6},{2,0},{4,2},{6,4},{1,7},{3,1},{5,3},{7,5},{8,14},{10,8},{12,... | collective-permute-start | bytes 786440 | tf_op jit(solution)/shard_map/ppermute | solution.py:375
  85.1 9.3 %collective-permute-done.9 = f32[256,256]{1,0:T(8,128)S(1)} collective-permute-done((f32[256,256]{1,0:T(8,128)}, f32[256,256]{1,0:T(8,128)S(1)}, u32[]{:S(2)}, u32[]{:S(2)}) %collective-permute-start.9) | collective-permute-done | bytes 262176 | tf_op jit(solution)/shard_map/ppermute | solution.py:375
  95.1 3.5 %collective-permute-done.7 = f32[256,256]{1,0:T(8,128)} collective-permute-done((f32[256,256]{1,0:T(8,128)}, f32[256,256]{1,0:T(8,128)}, u32[]{:S(2)}, u32[]{:S(2)}) %collective-permute-start.7) | collective-permute-done | bytes 262176 | tf_op jit(solution)/shard_map/ppermute | solution.py:375
  106.3 2.9 %collective-permute-done.11 = f32[64,256]{1,0:T(8,128)S(1)} collective-permute-done((f32[64,256]{1,0:T(8,128)}, f32[64,256]{1,0:T(8,128)S(1)}, u32[]{:S(2)}, u32[]{:S(2)}) %collective-permute-start.11) | collective-permute-done | bytes 65568 | tf_op jit(solution)/shard_map/ppermute | solution.py:375
  110.9 10.0 %collective-permute-done.6 = f32[2,2,256,256]{3,2,1,0:T(8,128)S(1)} collective-permute-done((f32[2,2,256,256]{3,2,1,0:T(8,128)}, f32[2,2,256,256]{3,2,1,0:T(8,128)S(1)}, u32[]{:S(2)}, u32[]{:S(2)}) %collective-permute-start.6) | collective-permute-done | bytes 1048608 | tf_op jit(solution)/shard_map/ppermute | solution.py:366
  120.9 2.1 %collective-permute-start.13 = (f32[64,256]{1,0:T(8,128)S(1)}, f32[64,256]{1,0:T(8,128)S(1)}, u32[]{:S(2)}, u32[]{:S(2)}) collective-permute-start(f32[64,256]{1,0:T(8,128)S(1)} %fusion.1), channel_id=1, source_target_pairs={{0,1},{1,0},{2,3},{3,2},{4,5},{5,4},{6,7},{7,6},{8,9},{9,8},{10,11... | collective-permute-start | bytes 196616 | tf_op jit(solution)/shard_map/ppermute | solution.py:408
  123.0 2.4 %collective-permute-done.13 = f32[64,256]{1,0:T(8,128)S(1)} collective-permute-done((f32[64,256]{1,0:T(8,128)S(1)}, f32[64,256]{1,0:T(8,128)S(1)}, u32[]{:S(2)}, u32[]{:S(2)}) %collective-permute-start.13) | collective-permute-done | bytes 65568 | tf_op jit(solution)/shard_map/ppermute | solution.py:408
  125.4 2.0 %collective-permute-start.14 = (f32[64,256]{1,0:T(8,128)S(1)}, f32[64,256]{1,0:T(8,128)S(1)}, u32[]{:S(2)}, u32[]{:S(2)}) collective-permute-start(f32[64,256]{1,0:T(8,128)S(1)} %add.205), channel_id=1, source_target_pairs={{0,16},{16,0},{32,48},{48,32},{1,17},{17,1},{33,49},{49,33},{2,18}... | collective-permute-start | bytes 196616 | tf_op jit(solution)/shard_map/ppermute | solution.py:408
  127.4 2.1 %collective-permute-done.14 = f32[64,256]{1,0:T(8,128)S(1)} collective-permute-done((f32[64,256]{1,0:T(8,128)S(1)}, f32[64,256]{1,0:T(8,128)S(1)}, u32[]{:S(2)}, u32[]{:S(2)}) %collective-permute-start.14) | collective-permute-done | bytes 65568 | tf_op jit(solution)/shard_map/ppermute | solution.py:408
  129.5 10.0 %collective-permute-start.15 = (f32[64,256]{1,0:T(8,128)S(1)}, f32[64,256]{1,0:T(8,128)S(1)}, u32[]{:S(2)}, u32[]{:S(2)}) collective-permute-start(f32[64,256]{1,0:T(8,128)S(1)} %add.206), channel_id=1, source_target_pairs={{0,32},{16,48},{32,0},{48,16},{1,33},{17,49},{33,1},{49,17},{2,34}... | collective-permute-start | bytes 196616 | tf_op jit(solution)/shard_map/ppermute | solution.py:408
  139.5 1.8 %collective-permute-done.15 = f32[64,256]{1,0:T(8,128)S(1)} collective-permute-done((f32[64,256]{1,0:T(8,128)S(1)}, f32[64,256]{1,0:T(8,128)S(1)}, u32[]{:S(2)}, u32[]{:S(2)}) %collective-permute-start.15) | collective-permute-done | bytes 65568 | tf_op jit(solution)/shard_map/ppermute | solution.py:408
  142.7 2.6 %collective-permute-start.17 = (f32[64,256]{1,0:T(8,128)S(1)}, f32[64,256]{1,0:T(8,128)S(1)}, u32[]{:S(2)}, u32[]{:S(2)}) collective-permute-start(f32[64,256]{1,0:T(8,128)S(1)} %get-tuple-element.11), channel_id=1, source_target_pairs={{0,128},{64,192},{128,0},{192,64},{1,129},{65,193},{129,1},{193,65... | collective-permute-start | bytes 196616 | tf_op jit(solution)/shard_map/ppermute | solution.py:375
  148.5 1.9 %collective-permute-start.19 = (f32[256,256]{1,0:T(8,128)S(1)}, f32[256,256]{1,0:T(8,128)S(1)}, u32[]{:S(2)}, u32[]{:S(2)}) collective-permute-start(f32[256,256]{1,0:T(8,128)S(1)} %bitcast.74), channel_id=1, source_target_pairs={{0,2},{2,4},{4,6},{6,0},{1,3},{3,5},{5,7},{7,1},{8,10},{10,12},{12... | collective-permute-start | bytes 786440 | tf_op jit(solution)/shard_map/ppermute | solution.py:375
  153.0 2.0 %collective-permute-done.19 = f32[256,256]{1,0:T(8,128)S(1)} collective-permute-done((f32[256,256]{1,0:T(8,128)S(1)}, f32[256,256]{1,0:T(8,128)S(1)}, u32[]{:S(2)}, u32[]{:S(2)}) %collective-permute-start.19) | collective-permute-done | bytes 262176 | tf_op jit(solution)/shard_map/ppermute | solution.py:375
  155.0 2.9 %collective-permute-done.20 = f32[256,256]{1,0:T(8,128)S(1)} collective-permute-done((f32[256,256]{1,0:T(8,128)S(1)}, f32[256,256]{1,0:T(8,128)S(1)}, u32[]{:S(2)}, u32[]{:S(2)}) %collective-permute-start.20) | collective-permute-done | bytes 262176 | tf_op jit(solution)/shard_map/ppermute | solution.py:375
  158.4 8.2 %collective-permute-start.22 = (f32[1024,256]{1,0:T(8,128)S(1)}, f32[1024,256]{1,0:T(8,128)S(1)}, u32[]{:S(2)}, u32[]{:S(2)}) collective-permute-start(f32[1024,256]{1,0:T(8,128)S(1)} %bitcast.65), channel_id=1, source_target_pairs={{0,8},{8,0},{1,9},{9,1},{2,10},{10,2},{3,11},{11,3},{4,12},{12,4},... | collective-permute-start | bytes 3145736 | tf_op jit(solution)/shard_map/ppermute | solution.py:375
  (72 shorter events, 37.8 us)
Async XLA Ops:
  0.6 25.5 %collective-permute-start.1 = (f32[2,2,256,256]{3,2,1,0:T(8,128)}, f32[2,2,256,256]{3,2,1,0:T(8,128)S(1)}, u32[]{:S(2)}, u32[]{:S(2)}) collective-permute-start(f32[2,2,256,256]{3,2,1,0:T(8,128)} %own.1), channel_id=1, source_target_pairs={{1,0},{2,1},{3,2},{4,3},{5,4},{6,5},{7,6},{9,8},{10,9},{11,10},{12... | collective-permute-start | bytes 3145736 | tf_op jit(solution)/shard_map/ppermute | solution.py:366
  1.9 5.8 %collective-permute-start = (s32[1,2]{1,0:T(1,128)}, s32[1,2]{1,0:T(1,128)S(1)}, u32[]{:S(2)}, u32[]{:S(2)}) collective-permute-start(s32[1,2]{1,0:T(1,128)} %param.9), channel_id=1, source_target_pairs={{0,8},{8,16},{16,24},{24,32},{32,40},{40,48},{48,56},{56,64},{64,7... | collective-permute-start | bytes 32 | tf_op jit(solution)/shard_map/ppermute | solution.py:438
  28.5 20.6 %collective-permute-start.2 = (f32[2,2,256,256]{3,2,1,0:T(8,128)}, f32[2,2,256,256]{3,2,1,0:T(8,128)S(1)}, u32[]{:S(2)}, u32[]{:S(2)}) collective-permute-start(f32[2,2,256,256]{3,2,1,0:T(8,128)} %broadcast_select_fusion), channel_id=1, source_target_pairs={{1,9},{3,11},{5,13},{7,15},{8,0},{9,17},{10,2},{11,19},{12,4},{13,... | collective-permute-start | bytes 3145736 | tf_op jit(solution)/shard_map/ppermute | solution.py:429
  33.6 10.2 %collective-permute-start.3 = (f32[1,256,256]{2,1,0:T(8,128)}, f32[1,256,256]{2,1,0:T(8,128)S(1)}, u32[]{:S(2)}, u32[]{:S(2)}) collective-permute-start(f32[1,256,256]{2,1,0:T(8,128)} %param.8), channel_id=1, source_target_pairs={{0,0},{1,9},{2,2},{3,11},{4,4},{5,13},{6,6},{7,15},{8,8},{9,17},{1... | collective-permute-start | bytes 786440 | tf_op jit(solution)/shard_map/ppermute | solution.py:429
  35.2 14.9 %copy-start = (f32[2,2,256,256]{3,2,1,0:T(8,128)S(1)}, f32[2,2,256,256]{3,2,1,0:T(8,128)}, u32[]{:S(2)}) copy-start(f32[2,2,256,256]{3,2,1,0:T(8,128)} %own.1) | copy-start | bytes 3145732
  69.4 6.6 %collective-permute-start.5 = (f32[1024,256]{1,0:T(8,128)S(1)}, f32[1024,256]{1,0:T(8,128)}, u32[]{:S(2)}, u32[]{:S(2)}) collective-permute-start(f32[1024,256]{1,0:T(8,128)S(1)} %dynamic-slice_bitcast_fusion), channel_id=1, source_target_pairs={{0,8},{8,0},{1,9},{9,1},{2,10},{10,2},{3,11},{11,3},{4,12},{12,4},... | collective-permute-start | bytes 3145736 | tf_op jit(solution)/shard_map/ppermute | solution.py:375
  69.5 30.2 %collective-permute-start.4 = (f32[2,2,256,256]{3,2,1,0:T(8,128)S(1)}, f32[2,2,256,256]{3,2,1,0:T(8,128)S(1)}, u32[]{:S(2)}, u32[]{:S(2)}) collective-permute-start(f32[2,2,256,256]{3,2,1,0:T(8,128)S(1)} %get-tuple-element.6), channel_id=1, source_target_pairs={{0,8},{1,249},{2,10},{3,251},{4,12},{5,253},{6,14},{7,255},{8,16},... | collective-permute-start | bytes 3145736 | tf_op jit(solution)/shard_map/ppermute | solution.py:429
  78.6 15.8 %collective-permute-start.9 = (f32[256,256]{1,0:T(8,128)}, f32[256,256]{1,0:T(8,128)S(1)}, u32[]{:S(2)}, u32[]{:S(2)}) collective-permute-start(f32[256,256]{1,0:T(8,128)} %get-tuple-element.14), channel_id=1, source_target_pairs={{0,6},{2,0},{4,2},{6,4},{1,7},{3,1},{5,3},{7,5},{8,14},{10,8},{12,... | collective-permute-start | bytes 786440 | tf_op jit(solution)/shard_map/ppermute | solution.py:375
  83.0 11.4 %collective-permute-start.8 = (f32[256,256]{1,0:T(8,128)}, f32[256,256]{1,0:T(8,128)}, u32[]{:S(2)}, u32[]{:S(2)}) collective-permute-start(f32[256,256]{1,0:T(8,128)} %get-tuple-element.15), channel_id=1, source_target_pairs={{0,4},{2,6},{4,0},{6,2},{1,5},{3,7},{5,1},{7,3},{8,12},{10,14},{12... | collective-permute-start | bytes 786440 | tf_op jit(solution)/shard_map/ppermute | solution.py:375
  83.2 15.3 %collective-permute-start.7 = (f32[256,256]{1,0:T(8,128)}, f32[256,256]{1,0:T(8,128)}, u32[]{:S(2)}, u32[]{:S(2)}) collective-permute-start(f32[256,256]{1,0:T(8,128)} %get-tuple-element.16), channel_id=1, source_target_pairs={{0,2},{2,4},{4,6},{6,0},{1,3},{3,5},{5,7},{7,1},{8,10},{10,12},{12... | collective-permute-start | bytes 786440 | tf_op jit(solution)/shard_map/ppermute | solution.py:375
  100.9 20.0 %collective-permute-start.6 = (f32[2,2,256,256]{3,2,1,0:T(8,128)}, f32[2,2,256,256]{3,2,1,0:T(8,128)S(1)}, u32[]{:S(2)}, u32[]{:S(2)}) collective-permute-start(f32[2,2,256,256]{3,2,1,0:T(8,128)} %select_add_fusion), channel_id=1, source_target_pairs={{0,1},{1,2},{2,3},{3,4},{4,5},{5,6},{6,7},{8,9},{9,10},{10,11},{11... | collective-permute-start | bytes 3145736 | tf_op jit(solution)/shard_map/ppermute | solution.py:366
  103.0 3.3 %collective-permute-start.12 = (f32[64,256]{1,0:T(8,128)}, f32[64,256]{1,0:T(8,128)S(1)}, u32[]{:S(2)}, u32[]{:S(2)}) collective-permute-start(f32[64,256]{1,0:T(8,128)} %get-tuple-element.18), channel_id=1, source_target_pairs={{0,192},{64,0},{128,64},{192,128},{1,193},{65,1},{129,65},{193,129... | collective-permute-start | bytes 196616 | tf_op jit(solution)/shard_map/ppermute | solution.py:375
  104.4 4.8 %collective-permute-start.11 = (f32[64,256]{1,0:T(8,128)}, f32[64,256]{1,0:T(8,128)S(1)}, u32[]{:S(2)}, u32[]{:S(2)}) collective-permute-start(f32[64,256]{1,0:T(8,128)} %get-tuple-element.19), channel_id=1, source_target_pairs={{0,128},{64,192},{128,0},{192,64},{1,129},{65,193},{129,1},{193,65... | collective-permute-start | bytes 196616 | tf_op jit(solution)/shard_map/ppermute | solution.py:375
  105.3 4.7 %collective-permute-start.10 = (f32[64,256]{1,0:T(8,128)}, f32[64,256]{1,0:T(8,128)}, u32[]{:S(2)}, u32[]{:S(2)}) collective-permute-start(f32[64,256]{1,0:T(8,128)} %get-tuple-element.17), channel_id=1, source_target_pairs={{0,64},{64,128},{128,192},{192,0},{1,65},{65,129},{129,193},{193,1... | collective-permute-start | bytes 196616 | tf_op jit(solution)/shard_map/ppermute | solution.py:375
  120.9 4.5 %collective-permute-start.13 = (f32[64,256]{1,0:T(8,128)S(1)}, f32[64,256]{1,0:T(8,128)S(1)}, u32[]{:S(2)}, u32[]{:S(2)}) collective-permute-start(f32[64,256]{1,0:T(8,128)S(1)} %fusion.1), channel_id=1, source_target_pairs={{0,1},{1,0},{2,3},{3,2},{4,5},{5,4},{6,7},{7,6},{8,9},{9,8},{10,11... | collective-permute-start | bytes 196616 | tf_op jit(solution)/shard_map/ppermute | solution.py:408
  125.4 4.1 %collective-permute-start.14 = (f32[64,256]{1,0:T(8,128)S(1)}, f32[64,256]{1,0:T(8,128)S(1)}, u32[]{:S(2)}, u32[]{:S(2)}) collective-permute-start(f32[64,256]{1,0:T(8,128)S(1)} %add.205), channel_id=1, source_target_pairs={{0,16},{16,0},{32,48},{48,32},{1,17},{17,1},{33,49},{49,33},{2,18}... | collective-permute-start | bytes 196616 | tf_op jit(solution)/shard_map/ppermute | solution.py:408
  129.5 11.7 %collective-permute-start.15 = (f32[64,256]{1,0:T(8,128)S(1)}, f32[64,256]{1,0:T(8,128)S(1)}, u32[]{:S(2)}, u32[]{:S(2)}) collective-permute-start(f32[64,256]{1,0:T(8,128)S(1)} %add.206), channel_id=1, source_target_pairs={{0,32},{16,48},{32,0},{48,16},{1,33},{17,49},{33,1},{49,17},{2,34}... | collective-permute-start | bytes 196616 | tf_op jit(solution)/shard_map/ppermute | solution.py:408
  141.3 5.1 %collective-permute-start.16 = (f32[64,256]{1,0:T(8,128)S(1)}, f32[64,256]{1,0:T(8,128)S(1)}, u32[]{:S(2)}, u32[]{:S(2)}) collective-permute-start(f32[64,256]{1,0:T(8,128)S(1)} %get-tuple-element.11), channel_id=1, source_target_pairs={{0,64},{64,128},{128,192},{192,0},{1,65},{65,129},{129,193},{193,1... | collective-permute-start | bytes 196616 | tf_op jit(solution)/shard_map/ppermute | solution.py:375
  142.7 5.0 %collective-permute-start.17 = (f32[64,256]{1,0:T(8,128)S(1)}, f32[64,256]{1,0:T(8,128)S(1)}, u32[]{:S(2)}, u32[]{:S(2)}) collective-permute-start(f32[64,256]{1,0:T(8,128)S(1)} %get-tuple-element.11), channel_id=1, source_target_pairs={{0,128},{64,192},{128,0},{192,64},{1,129},{65,193},{129,1},{193,65... | collective-permute-start | bytes 196616 | tf_op jit(solution)/shard_map/ppermute | solution.py:375
  145.3 3.1 %collective-permute-start.18 = (f32[64,256]{1,0:T(8,128)S(1)}, f32[64,256]{1,0:T(8,128)S(1)}, u32[]{:S(2)}, u32[]{:S(2)}) collective-permute-start(f32[64,256]{1,0:T(8,128)S(1)} %get-tuple-element.11), channel_id=1, source_target_pairs={{0,192},{64,0},{128,64},{192,128},{1,193},{65,1},{129,65},{193,129... | collective-permute-start | bytes 196616 | tf_op jit(solution)/shard_map/ppermute | solution.py:375
  148.5 6.5 %collective-permute-start.19 = (f32[256,256]{1,0:T(8,128)S(1)}, f32[256,256]{1,0:T(8,128)S(1)}, u32[]{:S(2)}, u32[]{:S(2)}) collective-permute-start(f32[256,256]{1,0:T(8,128)S(1)} %bitcast.74), channel_id=1, source_target_pairs={{0,2},{2,4},{4,6},{6,0},{1,3},{3,5},{5,7},{7,1},{8,10},{10,12},{12... | collective-permute-start | bytes 786440 | tf_op jit(solution)/shard_map/ppermute | solution.py:375
  150.4 7.5 %collective-permute-start.20 = (f32[256,256]{1,0:T(8,128)S(1)}, f32[256,256]{1,0:T(8,128)S(1)}, u32[]{:S(2)}, u32[]{:S(2)}) collective-permute-start(f32[256,256]{1,0:T(8,128)S(1)} %bitcast.75), channel_id=1, source_target_pairs={{0,4},{2,6},{4,0},{6,2},{1,5},{3,7},{5,1},{7,3},{8,12},{10,14},{12... | collective-permute-start | bytes 786440 | tf_op jit(solution)/shard_map/ppermute | solution.py:375
  151.3 7.0 %collective-permute-start.21 = (f32[256,256]{1,0:T(8,128)S(1)}, f32[256,256]{1,0:T(8,128)S(1)}, u32[]{:S(2)}, u32[]{:S(2)}) collective-permute-start(f32[256,256]{1,0:T(8,128)S(1)} %bitcast.76), channel_id=1, source_target_pairs={{0,6},{2,0},{4,2},{6,4},{1,7},{3,1},{5,3},{7,5},{8,14},{10,8},{12,... | collective-permute-start | bytes 786440 | tf_op jit(solution)/shard_map/ppermute | solution.py:375
  158.4 10.5 %collective-permute-start.22 = (f32[1024,256]{1,0:T(8,128)S(1)}, f32[1024,256]{1,0:T(8,128)S(1)}, u32[]{:S(2)}, u32[]{:S(2)}) collective-permute-start(f32[1024,256]{1,0:T(8,128)S(1)} %bitcast.65), channel_id=1, source_target_pairs={{0,8},{8,0},{1,9},{9,1},{2,10},{10,2},{3,11},{11,3},{4,12},{12,4},... | collective-permute-start | bytes 3145736 | tf_op jit(solution)/shard_map/ppermute | solution.py:375
  (7 other events, 6.9 us)

commit v3 on v2

--- a/solution.py
+++ b/solution.py
@@ -1,3 +1,4 @@
+import functools
 import math
 
 import jax
@@ -205,51 +206,68 @@
     return a + c, b + d, a - c, b - d
 
 
-def main_kernel(
-    place, own, right, other, probes, amp, table, phases,
-    terms, grads,
-    obj, q1, op, mid, out, acc,
-):
+def field(ref, lead, row, q):
+    return quad(ref, lead + (0,), row, q), quad(ref, lead + (1,), row, q)
+
+
+def fold_pairs(pairs):
+    return fold4(*[v[0] for v in pairs]), fold4(*[v[1] for v in pairs])
+
+
+def window_of(place, mine, other):
+    y0, x0, odd = place[0], place[1], place[2]
+    scale = place[3].astype(F32)
+    rows = lax.broadcasted_iota(jnp.int32, (N, N), 0)
+    upper = jnp.where(rows >= y0, 1 - odd, odd) > 0
+    result = []
+    for p in range(2):
+        value = jnp.where(upper, mine[p] * scale, other[p])
+        value = pltpu.roll(pltpu.roll(value, lax.rem(N - y0, N), 0), lax.rem(N - x0, N), 1)
+        result.append(mirror(value))
+    return result
+
+
+def wrapped(place, value):
+    return pltpu.roll(pltpu.roll(mirror(value), place[0], 0), place[1], 1)
+
+
+def add_pair(total, value):
+    return total[0] + value[0], total[1] + value[1]
+
+
+def zeros():
+    return [(jnp.zeros((CH, H), F32), jnp.zeros((CH, H), F32))] * 4
+
+
+def first_kernel(place, mine, other, probes, table, q1, obj, op, mid, out):
     modes = probes.shape[0]
-    y0, x0, odd, live = place[0], place[1], place[2], place[3]
-    up = lax.rem(N - y0, N)
-    back = lax.rem(N - x0, N)
-    rows = lax.broadcasted_iota(jnp.int32, (N, N), 0)
-    mine = jnp.where(rows >= y0, 1 - odd, odd) > 0
-    beside = lax.broadcasted_iota(jnp.int32, (N, N), 1) < x0
-    scale = live.astype(F32)
-    for s in range(2):
-        window = []
-        for p in range(2):
-            value = jnp.where(beside, right[s, p], own[s, p]) * scale
-            value = jnp.where(mine, value, other[s, p])
-            value = pltpu.roll(pltpu.roll(value, up, 0), back, 1)
-            window.append(mirror(value))
-        if s == 1:
-            window = mul(window, (phases[0], phases[1]))
-        obj[s, 0], obj[s, 1] = window
-
-    def field(ref, lead, row, q):
-        return quad(ref, lead + (0,), row, q), quad(ref, lead + (1,), row, q)
-
-    def fold_pairs(pairs):
-        return fold4(*[v[0] for v in pairs]), fold4(*[v[1] for v in pairs])
-
+    obj[0], obj[1] = window_of(place, mine, other)
     for m in range(modes):
         for k in range(CHUNKS):
             row = k * CH
-            pairs = [mul(field(probes, (m,), row, q), field(obj, (0,), row, q)) for q in QUADS]
+            pairs = [mul(field(probes, (m,), row, q), field(obj, (), row, q)) for q in QUADS]
             store_right_prop(op, m, row, *fold_pairs(pairs))
     prop_products(op, mid, out, table, 0, modes)
     for m in range(modes):
         for k in range(CHUNKS):
             row = k * CH
             real, imag = load_prop(out, m, row)
-            pixels = list(zip(unfold4(*real), unfold4(*imag)))
-            for q, v in zip(QUADS, pixels):
+            for q, v in zip(QUADS, zip(unfold4(*real), unfold4(*imag))):
                 put(q1, (m, 0), row, q, v[0])
                 put(q1, (m, 1), row, q, v[1])
-            pairs = [mul(v, field(obj, (1,), row, q)) for q, v in zip(QUADS, pixels)]
+
+
+def second_kernel(
+    place, mine, other, q1, amplitude, table, phases, grads, back_send, back_keep,
+    obj, amp, op, mid, out,
+):
+    modes = q1.shape[0]
+    obj[0], obj[1] = mul(window_of(place, mine, other), (phases[0], phases[1]))
+    amp[...] = mirror(amplitude[0])
+    for m in range(modes):
+        for k in range(CHUNKS):
+            row = k * CH
+            pairs = [mul(field(q1, (m,), row, q), field(obj, (), row, q)) for q in QUADS]
             store_right_four(op, m, row, *fold_pairs(pairs))
     four_products(op, mid, out, table, modes)
     for k in range(CHUNKS):
@@ -260,7 +278,7 @@
             for i, v in enumerate(zip(unfold4(*real), unfold4(*imag))):
                 total[i] = total[i] + (v[0] * v[0] + v[1] * v[1])
         factor = [
-            1.0 - quad(amp, (0,), row, q) * lax.rsqrt(total[i] + 1.0) for i, q in enumerate(QUADS)
+            1.0 - quad(amp, (), row, q) * lax.rsqrt(total[i] + 1.0) for i, q in enumerate(QUADS)
         ]
         for m in range(modes):
             real, imag = load_four(out, m, row, 1)
@@ -272,92 +290,150 @@
     four_products(op, mid, out, table, modes)
     for k in range(CHUNKS):
         row = k * CH
-        total = [(jnp.zeros((CH, H), F32), jnp.zeros((CH, H), F32))] * 4
+        total = zeros()
         for m in range(modes):
             real, imag = load_four(out, m, row, -1)
             pairs = []
             for i, v in enumerate(zip(unfold4(*real), unfold4(*imag))):
                 q = QUADS[i]
-                g = mulc(field(q1, (m,), row, q), v)
-                total[i] = (total[i][0] + g[0], total[i][1] + g[1])
-                pairs.append(mulc(field(obj, (1,), row, q), v))
-            store_right_prop(op, m, row, *fold_pairs(pairs))
+                total[i] = add_pair(total[i], mulc(field(q1, (m,), row, q), v))
+                pairs.append(mulc(field(obj, (), row, q), v))
+            back = back_send if m < modes // 2 else back_keep
+            store_right_prop(back, m % (modes // 2), row, *fold_pairs(pairs))
         for i, q in enumerate(QUADS):
-            phase = (quad(phases, (0,), row, q), quad(phases, (1,), row, q))
-            g = mulc(phase, total[i])
-            put(acc, (1, 0), row, q, g[0])
-            put(acc, (1, 1), row, q, g[1])
-    prop_products(op, mid, out, table, 1, modes)
+            total[i] = mulc(field(phases, (), row, q), total[i])
+        for i, q in enumerate(QUADS):
+            put(grads, (0,), row, q, total[i][0])
+            put(grads, (1,), row, q, total[i][1])
+    for p in range(2):
+        grads[p] = wrapped(place, grads[p])
+
+
+def third_kernel(start, last, place, back, obj, probes, table, before, terms, grads, mid, out):
+    modes = terms.shape[0]
+    prop_products(back, mid, out, table, 1, modes)
     for k in range(CHUNKS):
         row = k * CH
-        total = [(jnp.zeros((CH, H), F32), jnp.zeros((CH, H), F32))] * 4
+        total = [field(before, (), row, q) for q in QUADS] if last else zeros()
         for m in range(modes):
             real, imag = load_prop(out, m, row)
             for i, v in enumerate(zip(unfold4(*real), unfold4(*imag))):
                 q = QUADS[i]
-                g = mulc(field(probes, (m,), row, q), v)
-                total[i] = (total[i][0] + g[0], total[i][1] + g[1])
-                t = mulc(field(obj, (0,), row, q), v)
-                put(terms, (m, 0), row, q, t[0])
-                put(terms, (m, 1), row, q, t[1])
+                total[i] = add_pair(total[i], mulc(field(probes, (start + m,), row, q), v))
+                term = mulc(field(obj, (), row, q), v)
+                put(terms, (m, 0), row, q, term[0])
+                put(terms, (m, 1), row, q, term[1])
         for i, q in enumerate(QUADS):
-            put(acc, (0, 0), row, q, total[i][0])
-            put(acc, (0, 1), row, q, total[i][1])
+            put(grads, (0,), row, q, total[i][0])
+            put(grads, (1,), row, q, total[i][1])
     for m in range(modes):
         for p in range(2):
             terms[m, p] = mirror(terms[m, p])
-    for s in range(2):
+    if last:
         for p in range(2):
-            grads[s, p] = pltpu.roll(pltpu.roll(mirror(acc[s, p]), y0, 0), x0, 1)
-
-
-def mirror_kernel(source, target):
+            grads[p] = wrapped(place, grads[p])
+
+
+def call(kernel, args, shapes, scratch, flops):
+    spec = pl.BlockSpec(memory_space=pltpu.VMEM)
+    return pl.pallas_call(
+        kernel,
+        in_specs=[pl.BlockSpec(memory_space=pltpu.SMEM)] + [spec] * (len(args) - 1),
+        out_specs=[spec] * len(shapes),
+        out_shape=[jax.ShapeDtypeStruct(shape, dtype) for shape, dtype in shapes],
+        scratch_shapes=[pltpu.VMEM(shape, dtype) for shape, dtype in scratch],
+        compiler_params=pltpu.CompilerParams(vmem_limit_bytes=32 * 1024 * 1024),
+        cost_estimate=pl.CostEstimate(flops=flops, bytes_accessed=4 << 20, transcendentals=0),
+    )(*args)
+
+
+def products_scratch(modes):
+    return [((2, 2 * N, modes * N), BF16), ((2, N, modes * N), F32)]
+
+
+def operand(modes):
+    return ((2, modes * N, 2 * N), BF16)
+
+
+def first(place, mine, other, probes, table):
+    modes = probes.shape[0]
+    return call(
+        first_kernel,
+        (place, mine, other, probes, table),
+        [(probes.shape, F32), ((2, N, N), F32)],
+        [operand(modes)] + products_scratch(modes),
+        3 << 30,
+    )
+
+
+def second(place, mine, other, q1, amplitude, table, phases):
+    modes = q1.shape[0]
+    return call(
+        second_kernel,
+        (place, mine, other, q1, amplitude, table, phases),
+        [((2, N, N), F32), operand(modes // 2), operand(modes // 2)],
+        [((2, N, N), F32), ((N, N), F32), operand(modes)] + products_scratch(modes),
+        6 << 30,
+    )
+
+
+def third(start, place, back, obj, probes, table, before):
+    modes = probes.shape[0] // 2
+    last = before is not None
+    return call(
+        functools.partial(third_kernel, start, last),
+        (place, back, obj, probes, table, before if last else place[None]),
+        [((modes, 2, N, N), F32), ((2, N, N), F32)],
+        products_scratch(modes),
+        2 << 30,
+    )
+
+
+def stage_kernel(core, source, table, phases, target, table_out, phases_out):
     target[0] = mirror(source[0])
 
-
-def mirrored(images):
-    return pl.pallas_call(
-        mirror_kernel,
-        grid=(images.shape[0],),
-        in_specs=[pl.BlockSpec((1, N, N), lambda i: (i, 0, 0))],
-        out_specs=pl.BlockSpec((1, N, N), lambda i: (i, 0, 0)),
-        out_shape=jax.ShapeDtypeStruct(images.shape, F32),
-    )(images)
-
-
-def compute(place, own, right, other, probes, amp):
+    @pl.when(pl.program_id(0) == 0)
+    def _():
+        table_out[...] = table[...]
+        phases_out[...] = phases[...]
+
+
+def staged(core, probes):
     table, phases = (jnp.asarray(v) for v in constants())
-    modes = probes.shape[0]
-    flip = mirrored(probes.reshape(-1, N, N)).reshape(probes.shape)
-    flip_amp = mirrored(amp)
-    vmem = pl.BlockSpec(memory_space=pltpu.VMEM)
-    return pl.pallas_call(
-        main_kernel,
-        in_specs=[pl.BlockSpec(memory_space=pltpu.SMEM)] + [vmem] * 7,
-        out_specs=[vmem, vmem],
+    images = probes.reshape(-1, N, N)
+    count = images.shape[0]
+    half = count // 2
+    whole = lambda value: pl.BlockSpec(value.shape, lambda i, core: (0,) * value.ndim)
+    flip, table, phases = pl.pallas_call(
+        stage_kernel,
+        grid_spec=pltpu.PrefetchScalarGridSpec(
+            num_scalar_prefetch=1,
+            grid=(count,),
+            in_specs=[
+                pl.BlockSpec((1, N, N), lambda i, core: ((i + half * (1 - core[0])) % count, 0, 0)),
+                whole(table),
+                whole(phases),
+            ],
+            out_specs=[
+                pl.BlockSpec((1, N, N), lambda i, core: (i, 0, 0)),
+                whole(table),
+                whole(phases),
+            ],
+        ),
         out_shape=[
-            jax.ShapeDtypeStruct(probes.shape, F32),
-            jax.ShapeDtypeStruct(own.shape, F32),
+            jax.ShapeDtypeStruct(images.shape, F32),
+            jax.ShapeDtypeStruct(table.shape, table.dtype),
+            jax.ShapeDtypeStruct(phases.shape, phases.dtype),
         ],
-        scratch_shapes=[
-            pltpu.VMEM((2, 2, N, N), F32),
-            pltpu.VMEM((modes, 2, N, N), F32),
-            pltpu.VMEM((2, modes * N, 2 * N), BF16),
-            pltpu.VMEM((2, 2 * N, modes * N), BF16),
-            pltpu.VMEM((2, N, modes * N), F32),
-            pltpu.VMEM((2, 2, N, N), F32),
-        ],
-        compiler_params=pltpu.CompilerParams(vmem_limit_bytes=48 * 1024 * 1024),
-        cost_estimate=pl.CostEstimate(
-            flops=12_000_000_000, bytes_accessed=12 << 20, transcendentals=0
-        ),
-    )(place, own, right, other, flip, flip_amp, table, phases)
+    )(core, images, table, phases)
+    return flip.reshape(probes.shape), table, phases
 
 
 POS = ("y", "zh", "core")
 TILE = ("x", "zl")
 ROWS = 32
 COLUMNS = 8
+MODES = 4
 
 
 def shifted(value, axes, steps):
@@ -403,15 +479,15 @@
     return whole
 
 
-def exchange_sum(value, axis, bit):
-    count = lax.axis_size(axis)
-    return value + lax.ppermute(value, axis, [(i, i ^ bit) for i in range(count)])
+def exchange(value, bits):
+    axes = ("zh", "zl")
+    count = math.prod(lax.axis_size(axis) for axis in axes)
+    return lax.ppermute(value, axes, [(i, i ^ bits) for i in range(count)])
 
 
 def spread(value, order):
-    value = exchange_sum(value, "zl", 1)
-    value = exchange_sum(value, "zh", 1)
-    value = exchange_sum(value, "zh", 2)
+    value = (value + exchange(value, 1)) + (exchange(value, 2) + exchange(value, 3))
+    value = value + exchange(value, 4)
     for axis in order[::-1] + ("core",):
         value = gather(value, axis).reshape(-1, N)
     return value
@@ -434,31 +510,51 @@
     col = lax.broadcasted_iota(jnp.int32, (N, N), 1)
     odd = lax.axis_index("zl")
     is_odd = odd == 1
-    first = (lax.axis_index(POS) == 0) & is_odd
+    first_row = (lax.axis_index(POS) == 0) & is_odd
     above = lax.ppermute(corners, POS, [(i, (i + 1) % ROWS) for i in range(ROWS)])
     yp, xp = [jnp.where(is_odd, above[0, i], corners[0, i]) for i in (0, 1)]
     yq, xq = [jnp.where(is_odd, corners[0, i], above[0, i]) for i in (0, 1)]
     amplitude = moved(amplitudes, 0, 1)
-    right = shifted(object_field, TILE, -1)
-    mixed = jnp.where(col < xq, right, object_field)
-    other = moved(mixed, -1, 1)
-    live = jnp.where(first, 0, 1)
+    live = jnp.where(first_row, 0, 1)
     place = jnp.stack([yp, xp, odd, live]).astype(jnp.int32)
-    terms, grads = compute(place, object_field, right, other, probe_modes, amplitude)
-    arrived = moved(grads, 1, -1)
-    partial = scatter_sum(pieces(terms, "core"), "core")
-    across = pieces(partial, "x")
+    flip, table, phases = staged(lax.axis_index("core").astype(jnp.int32).reshape(1), probe_modes)
+    mine, other = [], []
+    rights = [shifted(object_field[s], TILE, -1) for s in range(2)]
+    rights[0] = after(rights[0], flip)
+    for s in range(2):
+        mixed = jnp.where(col < xq, rights[s], object_field[s])
+        mine.append(jnp.where(col < xp, rights[s], object_field[s]))
+        other.append(moved(mixed, -1, 1))
+        if s == 0:
+            rights[1] = after(rights[1], mixed)
+
+    def split(grads, arrived):
+        kept = jnp.where(((row >= yp) != is_odd) & ~first_row, grads, 0.0)
+        taken = jnp.where((row < yq) != is_odd, arrived, 0.0)
+        leaving = jnp.where(col < xp, kept, 0.0) + jnp.where(col < xq, taken, 0.0)
+        staying = jnp.where(col >= xp, kept, 0.0) + jnp.where(col >= xq, taken, 0.0)
+        return staying, leaving
+
+    q1, obj = first(place, mine[0], other[0], flip, table)
+    grads1, back_send, back_keep = second(place, mine[1], other[1], q1, amplitude, table, phases)
+    arrived1 = moved(grads1, 1, -1)
+    send, part = third(0, place, back_send, obj, flip, table, None)
+    got = lax.ppermute(send, "core", [(0, 1), (1, 0)])
+    keep, grads0 = third(MODES // 2, place, back_keep, obj, flip, table, part)
+    arrived0 = moved(grads0, 1, -1)
+    across = pieces(keep + got, "x")
+    staying1, leaving1 = split(grads1, after(arrived1, *across))
+    received1 = shifted(leaving1, TILE, 1)
+    across[-1] = after(across[-1], leaving1)
     partial = scatter_sum(across, "x")
-    partial = scatter_sum(pieces(partial, "y"), "y")
-    arrived = after(arrived, *across)
-    kept = jnp.where(((row >= yp) != is_odd) & ~first, grads, 0.0)
-    taken = jnp.where((row < yq) != is_odd, arrived, 0.0)
-    leaving = jnp.where(col < xp, kept, 0.0) + jnp.where(col < xq, taken, 0.0)
-    staying = jnp.where(col >= xp, kept, 0.0) + jnp.where(col >= xq, taken, 0.0)
-    received = shifted(leaving, TILE, 1)
-    partial = after(partial, received)
-    object_grad = staying + received
-    probe_grad = spread(partial, ("x", "y")).reshape(terms.shape)
+    across = pieces(partial, "y")
+    staying0, leaving0 = split(grads0, after(arrived0, *across))
+    received0 = shifted(leaving0, TILE, 1)
+    across[-1] = after(across[-1], leaving0)
+    partial = scatter_sum(across, "y")
+    partial = after(partial, received0, received1)
+    object_grad = jnp.stack([staying0 + received0, staying1 + received1])
+    probe_grad = spread(partial, ("x", "y")).reshape(probe_modes.shape)
     return (object_grad, probe_grad)
 
 

time: 171 us -> 171 us (level)
  waiting for transfers between devices: 60.7 us -> 31.1 us
  starting transfers between devices: 60.2 us -> 87.8 us
    ppermute x2 -> x4, starting transfers between devices: 2.64 us -> 34.9 us  [shifted(): lax.ppermute(value, axes, [(source, source + steps) for source in range(f...]
    ppermute x2 -> x4, waiting for transfers between devices: 26.6 us -> 6.84 us  [shifted(): lax.ppermute(value, axes, [(source, source + steps) for source in range(f...]
    ppermute x3 -> x5, starting transfers between devices: 13.1 us -> 27.4 us  [moved(): return lax.ppermute(value, POS + TILE, pairs)]
    ppermute x14 -> x13, waiting for transfers between devices: 24.9 us -> 13.1 us  [ring(): lax.ppermute(value, axis, [(i, (i + step) % count) for i in range(count)])]
    ppermute x3 -> x5, starting transfers between devices: 14 us -> 4.38 us  [the longest x4 4.38 us: exchange(): return lax.ppermute(value, axes, [(i, i ^ bits) for i in range(count)])]
    ppermute x14 -> x13, starting transfers between devices: 26 us -> 16.6 us  [ring(): lax.ppermute(value, axis, [(i, (i + step) % count) for i in range(count)])]
    ppermute x3 -> x5, waiting for transfers between devices: 6.32 us -> 11.2 us  [the longest x4 11.2 us: exchange(): return lax.ppermute(value, axes, [(i, i ^ bits) for i in range(count)])]
    add x3 -> x2, other arithmetic: 3.71 us -> 0.09 us  [scatter_sum(): total = total + part]
  transfers between devices with their start and end apart: 23 -> 28, of which waited for: 17 -> 10; matrix products, arithmetic and copies ran while one was open for 5% -> 6% of each run, Pallas kernels for 5% -> 8%
where the time goes in v3:
time: 171 us; the launch traced here: 170 us
  starting transfers between devices  87.8 us (51%)
  waiting for transfers between devices  31.1 us (18%)
  Pallas kernels  23.3 us (14%)
  local copies, waits for them, and re-layouts  11.9 us (7%)
  other arithmetic  9.34 us (5%)
  between operations  6.35 us (4%)
    ppermute x4, starting transfers between devices, shifted(): lax.ppermute(value, axes, [(source, source + steps) for source in range(f...  34.9 us
    ppermute x5, starting transfers between devices, moved(): return lax.ppermute(value, POS + TILE, pairs)  27.4 us
    ppermute x13, starting transfers between devices, ring(): lax.ppermute(value, axis, [(i, (i + step) % count) for i in range(count)])  16.6 us
    pallas_call x4, Pallas kernels, call(): pl.pallas_call(kernel, in_specs=[pl.BlockSpec(memory_space=pltpu.SMEM)] +...  16.1 us
    ppermute x13, waiting for transfers between devices, ring(): lax.ppermute(value, axis, [(i, (i + step) % count) for i in range(count)])  13.1 us
    ppermute x4, waiting for transfers between devices, exchange(): return lax.ppermute(value, axes, [(i, i ^ bits) for i in range(count)])  11.2 us
    unnamed x30, local copies, waits for them, and re-layouts  7.55 us
    pallas_call x1, Pallas kernels, staged(): pl.pallas_call(stage_kernel, grid_spec=pltpu.PrefetchScalarGridSpec(num_s...  7.21 us
  transfers between devices with their start and end apart: 28, of which 10 were waited for; matrix products, arithmetic and copies ran while one was open for 6% of the time, Pallas kernels for 8%

profile of v3, /device:TPU:1, one launch (start us, length us, event | category | flops | bytes accessed | tf_op | source)
XLA Modules:
  0.0 169.9 jit_solution(8874668025939830749)
XLA Ops:
  3.3 4.5 %collective-permute-start = (s32[1,2]{1,0:T(1,128)S(1)}, s32[1,2]{1,0:T(1,128)S(1)}, u32[]{:S(2)}, u32[]{:S(2)}) collective-permute-start(s32[1,2]{1,0:T(1,128)S(1)} %copy-done.14), channel_id=1, source_target_pairs={{0,8},{8,16},{16,24},{24,32},{32,40},{40,48},{48,56},{56,64},{64,7... | collective-permute-start | bytes 32 | tf_op jit(solution)/shard_map/ppermute | solution.py:514
  9.0 7.2 %shard_map.77 = (f32[8,256,256]{2,1,0:T(8,128)}, bf16[5,2,256,256]{3,2,1,0:T(8,128)(2,1)}, f32[2,256,256]{2,1,0:T(8,128)}) custom-call(s32[1]{0:T(128)} %bitcast.10.core, f32[8,256,256]{2,1,0:T(8,128)} %bitcast.79, bf16[5,2,256,256]{3,2,1,0:T(8,128)(2,1)} %constant.160.clone.table, f32[2,256,256]{2,1,0:T(8,128)} %constant.161.clone.phases), custom_call_target="tpu_custom_call" | custom-call | tf_op jit(solution)/shard_map/pallas_call | solution.py:407
  20.8 2.2 %broadcast_select_fusion.2 = (f32[2,256,256]{2,1,0:T(8,128)S(1)}, f32[2,256,256]{2,1,0:T(8,128)}) fusion(f32[2,256,256]{2,1,0:T(8,128)} %copy-done.11, pred[256]{0:T(512)(128)(4,1)S(1)} %get-tuple-element.65, f32[2,2,256,256]{3,2,1,0:T(8,128)} %param.6, pred[256]{0:T(512)(128)(4,1)S(1)} %get-tuple-element.64), kind=kLoop, calls=%fused_computation.20 | loop fusion | flops 262144 | bytes 2097664 | tf_op jit(solution)/shard_map/jit(_where)/select_n | solution.py:526
  23.0 3.8 %collective-permute-start.4 = (f32[2,256,256]{2,1,0:T(8,128)}, f32[2,256,256]{2,1,0:T(8,128)}, u32[]{:S(2)}, u32[]{:S(2)}) collective-permute-start(f32[2,256,256]{2,1,0:T(8,128)} %get-tuple-element.43), channel_id=1, source_target_pairs={{1,9},{3,11},{5,13},{7,15},{8,0},{9,17},{10,2},{11,19},{12,4},{13,... | collective-permute-start | bytes 1572872 | tf_op jit(solution)/shard_map/ppermute | solution.py:505
  31.1 8.2 %collective-permute-start.3 = (f32[2,256,256]{2,1,0:T(8,128)S(1)}, f32[2,256,256]{2,1,0:T(8,128)S(1)}, u32[]{:S(2)}, u32[]{:S(2)}) collective-permute-start(f32[2,256,256]{2,1,0:T(8,128)S(1)} %get-tuple-element.44), channel_id=1, source_target_pairs={{1,9},{3,11},{5,13},{7,15},{8,0},{9,17},{10,2},{11,19},{12,4},{13,... | collective-permute-start | bytes 1572872 | tf_op jit(solution)/shard_map/ppermute | solution.py:505
  39.5 3.9 %shard_map.78 = (f32[4,2,256,256]{3,2,1,0:T(8,128)S(1)}, f32[2,256,256]{2,1,0:T(8,128)S(1)}) custom-call(s32[4]{0:T(128)S(1)} %pad_add_fusion.place, f32[2,256,256]{2,1,0:T(8,128)S(1)} %get-tuple-element.42.mine, f32[2,256,256]{2,1,0:T(8,128)} %collective-permute-done.4.other, f32[4,2,256,256]{3,2,1,0:T(8,128)S(1)} %bitcast.72, ...), custom_call_target="tpu_custom_call" | custom-call | flops 3221225472 | bytes 4194304 | tf_op jit(solution)/shard_map/pallas_call | solution.py:339
  43.5 6.7 %shard_map.79 = (f32[2,256,256]{2,1,0:T(8,128)S(1)}, bf16[2,512,512]{2,1,0:T(8,128)(2,1)S(1)}, bf16[2,512,512]{2,1,0:T(8,128)(2,1)S(1)}) custom-call(s32[4]{0:T(128)S(1)} %pad_add_fusion.place, f32[2,256,256]{2,1,0:T(8,128)S(1)} %get-tuple-element.45.mine, f32[2,256,256]{2,1,0:T(8,128)S(1)} %collective-permute-done.3.other, ...), custom_call_target="tpu_custom_call" | custom-call | flops 6442450944 | bytes 4194304 | tf_op jit(solution)/shard_map/pallas_call | solution.py:339
  50.3 3.1 %shard_map.80 = (f32[2,2,256,256]{3,2,1,0:T(8,128)}, f32[2,256,256]{2,1,0:T(8,128)S(1)}) custom-call(s32[4]{0:T(128)S(1)} %pad_add_fusion.place, bf16[2,512,512]{2,1,0:T(8,128)(2,1)S(1)} %get-tuple-element.29.back, f32[2,256,256]{2,1,0:T(8,128)S(1)} %get-tuple-element.28.obj, f32[4,2,256,256]{3,2,1,0:T(8,128)S(1)} %bitcast.73, ...), custom_call_target="tpu_custom_call" | custom-call | flops 2147483648 | bytes 4194304 | tf_op jit(solution)/shard_map/pallas_call | solution.py:339
  54.2 11.9 %collective-permute-start.8 = (f32[2,256,256]{2,1,0:T(8,128)S(1)}, f32[2,256,256]{2,1,0:T(8,128)}, u32[]{:S(2)}, u32[]{:S(2)}) collective-permute-start(f32[2,256,256]{2,1,0:T(8,128)S(1)} %get-tuple-element.34), channel_id=1, source_target_pairs={{0,8},{1,249},{2,10},{3,251},{4,12},{5,253},{6,14},{7,255},{8,16},... | collective-permute-start | bytes 1572872 | tf_op jit(solution)/shard_map/ppermute | solution.py:505
  72.1 2.3 %shard_map.81 = (f32[2,2,256,256]{3,2,1,0:T(8,128)S(1)}, f32[2,256,256]{2,1,0:T(8,128)S(1)}) custom-call(s32[4]{0:T(128)S(1)} %pad_add_fusion.place, bf16[2,512,512]{2,1,0:T(8,128)(2,1)S(1)} %copy-done.5, f32[2,256,256]{2,1,0:T(8,128)S(1)} %copy-done.7, f32[4,2,256,256]{3,2,1,0:T(8,128)S(1)} %bitcast.74, bf16[5,2,256,256]{3,2,1,0:T(8,128)(2,1)S(1)} %copy-done.2, ...), custom_call_target="tpu_custom_call" | custom-call | flops 2147483648 | bytes 4194304 | tf_op jit(solution)/shard_map/pallas_call | solution.py:339
  80.7 23.7 %collective-permute-start.13 = (f32[2,256,256]{2,1,0:T(8,128)S(1)}, f32[2,256,256]{2,1,0:T(8,128)S(1)}, u32[]{:S(2)}, u32[]{:S(2)}) collective-permute-start(f32[2,256,256]{2,1,0:T(8,128)S(1)} %select_add_fusion.1), channel_id=1, source_target_pairs={{0,1},{1,2},{2,3},{3,4},{4,5},{5,6},{6,7},{8,9},{9,10},{10,11},{11... | collective-permute-start | bytes 1572872 | tf_op jit(solution)/shard_map/ppermute | solution.py:442
  104.7 8.7 %collective-permute-start.12 = (f32[2,256,256]{2,1,0:T(8,128)S(1)}, f32[2,256,256]{2,1,0:T(8,128)S(1)}, u32[]{:S(2)}, u32[]{:S(2)}) collective-permute-start(f32[2,256,256]{2,1,0:T(8,128)S(1)} %select_add_fusion), channel_id=1, source_target_pairs={{0,1},{1,2},{2,3},{3,4},{4,5},{5,6},{6,7},{8,9},{9,10},{10,11},{11... | collective-permute-start | bytes 1572872 | tf_op jit(solution)/shard_map/ppermute | solution.py:442
  113.6 2.6 %collective-permute-start.16 = (f32[64,256]{1,0:T(8,128)S(1)}, f32[64,256]{1,0:T(8,128)S(1)}, u32[]{:S(2)}, u32[]{:S(2)}) collective-permute-start(f32[64,256]{1,0:T(8,128)S(1)} %get-tuple-element.53), channel_id=1, source_target_pairs={{0,192},{64,0},{128,64},{192,128},{1,193},{65,1},{129,65},{193,129... | collective-permute-start | bytes 196616 | tf_op jit(solution)/shard_map/ppermute | solution.py:451
  116.2 2.7 %collective-permute-done.14 = f32[64,256]{1,0:T(8,128)S(1)} collective-permute-done((f32[64,256]{1,0:T(8,128)S(1)}, f32[64,256]{1,0:T(8,128)S(1)}, u32[]{:S(2)}, u32[]{:S(2)}) %collective-permute-start.14) | collective-permute-done | bytes 65568 | tf_op jit(solution)/shard_map/ppermute | solution.py:451
  119.5 6.8 %collective-permute-done.12 = f32[2,256,256]{2,1,0:T(8,128)S(1)} collective-permute-done((f32[2,256,256]{2,1,0:T(8,128)S(1)}, f32[2,256,256]{2,1,0:T(8,128)S(1)}, u32[]{:S(2)}, u32[]{:S(2)}) %collective-permute-start.12) | collective-permute-done | bytes 524320 | tf_op jit(solution)/shard_map/ppermute | solution.py:442
  126.3 2.2 %collective-permute-start.17 = (f32[64,256]{1,0:T(8,128)S(1)}, f32[64,256]{1,0:T(8,128)S(1)}, u32[]{:S(2)}, u32[]{:S(2)}) collective-permute-start(f32[64,256]{1,0:T(8,128)S(1)} %add_add_fusion.2), channel_id=1, source_target_pairs={{0,1},{1,0},{16,17},{17,16},{32,33},{33,32},{48,49},{49,48},{2,3},... | collective-permute-start | bytes 196616 | tf_op jit(solution)/shard_map/ppermute | solution.py:485
  130.6 4.2 %collective-permute-done.18 = f32[64,256]{1,0:T(8,128)S(1)} collective-permute-done((f32[64,256]{1,0:T(8,128)S(1)}, f32[64,256]{1,0:T(8,128)S(1)}, u32[]{:S(2)}, u32[]{:S(2)}) %collective-permute-start.18) | collective-permute-done | bytes 65568 | tf_op jit(solution)/shard_map/ppermute | solution.py:485
  134.9 7.0 %collective-permute-done.20 = f32[64,256]{1,0:T(8,128)S(1)} collective-permute-done((f32[64,256]{1,0:T(8,128)S(1)}, f32[64,256]{1,0:T(8,128)S(1)}, u32[]{:S(2)}, u32[]{:S(2)}) %collective-permute-start.20) | collective-permute-done | bytes 65568 | tf_op jit(solution)/shard_map/ppermute | solution.py:485
  142.1 2.6 %collective-permute-start.23 = (f32[64,256]{1,0:T(8,128)S(1)}, f32[64,256]{1,0:T(8,128)S(1)}, u32[]{:S(2)}, u32[]{:S(2)}) collective-permute-start(f32[64,256]{1,0:T(8,128)S(1)} %get-tuple-element.41), channel_id=1, source_target_pairs={{0,192},{64,0},{128,64},{192,128},{1,193},{65,1},{129,65},{193,129... | collective-permute-start | bytes 196616 | tf_op jit(solution)/shard_map/ppermute | solution.py:451
  144.7 2.3 %collective-permute-done.21 = f32[64,256]{1,0:T(8,128)S(1)} collective-permute-done((f32[64,256]{1,0:T(8,128)S(1)}, f32[64,256]{1,0:T(8,128)S(1)}, u32[]{:S(2)}, u32[]{:S(2)}) %collective-permute-start.21) | collective-permute-done | bytes 65568 | tf_op jit(solution)/shard_map/ppermute | solution.py:451
  147.7 3.1 %collective-permute-start.25 = (f32[256,256]{1,0:T(8,128)S(1)}, f32[256,256]{1,0:T(8,128)S(1)}, u32[]{:S(2)}, u32[]{:S(2)}) collective-permute-start(f32[256,256]{1,0:T(8,128)S(1)} %bitcast.82), channel_id=1, source_target_pairs={{0,4},{2,6},{4,0},{6,2},{1,5},{3,7},{5,1},{7,3},{8,12},{10,14},{12... | collective-permute-start | bytes 786440 | tf_op jit(solution)/shard_map/ppermute | solution.py:451
  150.9 3.2 %collective-permute-done.24 = f32[256,256]{1,0:T(8,128)S(1)} collective-permute-done((f32[256,256]{1,0:T(8,128)S(1)}, f32[256,256]{1,0:T(8,128)S(1)}, u32[]{:S(2)}, u32[]{:S(2)}) %collective-permute-start.24) | collective-permute-done | bytes 262176 | tf_op jit(solution)/shard_map/ppermute | solution.py:451
  154.2 3.3 %collective-permute-done.25 = f32[256,256]{1,0:T(8,128)S(1)} collective-permute-done((f32[256,256]{1,0:T(8,128)S(1)}, f32[256,256]{1,0:T(8,128)S(1)}, u32[]{:S(2)}, u32[]{:S(2)}) %collective-permute-start.25) | collective-permute-done | bytes 262176 | tf_op jit(solution)/shard_map/ppermute | solution.py:451
  158.0 6.3 %collective-permute-start.27 = (f32[1024,256]{1,0:T(8,128)S(1)}, f32[1024,256]{1,0:T(8,128)}, u32[]{:S(2)}, u32[]{:S(2)}) collective-permute-start(f32[1024,256]{1,0:T(8,128)S(1)} %bitcast.76), channel_id=1, source_target_pairs={{0,8},{8,0},{1,9},{9,1},{2,10},{10,2},{3,11},{11,3},{4,12},{12,4},... | collective-permute-start | bytes 3145736 | tf_op jit(solution)/shard_map/ppermute | solution.py:451
  (100 shorter events, 31.0 us)
Async XLA Ops:
  1.9 18.1 %collective-permute-start.2 = (f32[2,256,256]{2,1,0:T(8,128)S(1)}, f32[2,256,256]{2,1,0:T(8,128)S(1)}, u32[]{:S(2)}, u32[]{:S(2)}) collective-permute-start(f32[2,256,256]{2,1,0:T(8,128)S(1)} %get-tuple-element.50), channel_id=1, source_target_pairs={{1,0},{2,1},{3,2},{4,3},{5,4},{6,5},{7,6},{9,8},{10,9},{11,10},{12... | collective-permute-start | bytes 1572872 | tf_op jit(solution)/shard_map/ppermute | solution.py:442
  3.3 13.6 %collective-permute-start = (s32[1,2]{1,0:T(1,128)S(1)}, s32[1,2]{1,0:T(1,128)S(1)}, u32[]{:S(2)}, u32[]{:S(2)}) collective-permute-start(s32[1,2]{1,0:T(1,128)S(1)} %copy-done.14), channel_id=1, source_target_pairs={{0,8},{8,16},{16,24},{24,32},{32,40},{40,48},{48,56},{56,64},{64,7... | collective-permute-start | bytes 32 | tf_op jit(solution)/shard_map/ppermute | solution.py:514
  7.7 22.0 %collective-permute-start.1 = (f32[2,256,256]{2,1,0:T(8,128)S(1)}, f32[2,256,256]{2,1,0:T(8,128)}, u32[]{:S(2)}, u32[]{:S(2)}) collective-permute-start(f32[2,256,256]{2,1,0:T(8,128)S(1)} %get-tuple-element.51), channel_id=1, source_target_pairs={{1,0},{2,1},{3,2},{4,3},{5,4},{6,5},{7,6},{9,8},{10,9},{11,10},{12... | collective-permute-start | bytes 1572872 | tf_op jit(solution)/shard_map/ppermute | solution.py:442
  23.0 16.5 %collective-permute-start.4 = (f32[2,256,256]{2,1,0:T(8,128)}, f32[2,256,256]{2,1,0:T(8,128)}, u32[]{:S(2)}, u32[]{:S(2)}) collective-permute-start(f32[2,256,256]{2,1,0:T(8,128)} %get-tuple-element.43), channel_id=1, source_target_pairs={{1,9},{3,11},{5,13},{7,15},{8,0},{9,17},{10,2},{11,19},{12,4},{13,... | collective-permute-start | bytes 1572872 | tf_op jit(solution)/shard_map/ppermute | solution.py:505
  26.9 16.6 %collective-permute-start.5 = (f32[1,256,256]{2,1,0:T(8,128)}, f32[1,256,256]{2,1,0:T(8,128)S(1)}, u32[]{:S(2)}, u32[]{:S(2)}) collective-permute-start(f32[1,256,256]{2,1,0:T(8,128)} %param.8), channel_id=1, source_target_pairs={{0,0},{1,9},{2,2},{3,11},{4,4},{5,13},{6,6},{7,15},{8,8},{9,17},{1... | collective-permute-start | bytes 786440 | tf_op jit(solution)/shard_map/ppermute | solution.py:505
  31.1 12.3 %collective-permute-start.3 = (f32[2,256,256]{2,1,0:T(8,128)S(1)}, f32[2,256,256]{2,1,0:T(8,128)S(1)}, u32[]{:S(2)}, u32[]{:S(2)}) collective-permute-start(f32[2,256,256]{2,1,0:T(8,128)S(1)} %get-tuple-element.44), channel_id=1, source_target_pairs={{1,9},{3,11},{5,13},{7,15},{8,0},{9,17},{10,2},{11,19},{12,4},{13,... | collective-permute-start | bytes 1572872 | tf_op jit(solution)/shard_map/ppermute | solution.py:505
  54.2 22.2 %collective-permute-start.7 = (f32[2,2,256,256]{3,2,1,0:T(8,128)}, f32[2,2,256,256]{3,2,1,0:T(8,128)}, u32[]{:S(2)}, u32[]{:S(2)}) collective-permute-start(f32[2,2,256,256]{3,2,1,0:T(8,128)} %get-tuple-element.33), channel_id=1, source_target_pairs={{0,8},{8,0},{1,9},{9,1},{2,10},{10,2},{3,11},{11,3},{4,12},{12,4},... | collective-permute-start | bytes 3145736 | tf_op jit(solution)/shard_map/ppermute | solution.py:542
  54.2 25.3 %collective-permute-start.8 = (f32[2,256,256]{2,1,0:T(8,128)S(1)}, f32[2,256,256]{2,1,0:T(8,128)}, u32[]{:S(2)}, u32[]{:S(2)}) collective-permute-start(f32[2,256,256]{2,1,0:T(8,128)S(1)} %get-tuple-element.34), channel_id=1, source_target_pairs={{0,8},{1,249},{2,10},{3,251},{4,12},{5,253},{6,14},{7,255},{8,16},... | collective-permute-start | bytes 1572872 | tf_op jit(solution)/shard_map/ppermute | solution.py:505
  74.4 30.1 %collective-permute-start.6 = (f32[2,256,256]{2,1,0:T(8,128)S(1)}, f32[2,256,256]{2,1,0:T(8,128)S(1)}, u32[]{:S(2)}, u32[]{:S(2)}) collective-permute-start(f32[2,256,256]{2,1,0:T(8,128)S(1)} %get-tuple-element.31), channel_id=1, source_target_pairs={{0,8},{1,249},{2,10},{3,251},{4,12},{5,253},{6,14},{7,255},{8,16},... | collective-permute-start | bytes 1572872 | tf_op jit(solution)/shard_map/ppermute | solution.py:505
  77.8 26.6 %collective-permute-start.10 = (f32[256,256]{1,0:T(8,128)S(1)}, f32[256,256]{1,0:T(8,128)S(1)}, u32[]{:S(2)}, u32[]{:S(2)}) collective-permute-start(f32[256,256]{1,0:T(8,128)S(1)} %get-tuple-element.48), channel_id=1, source_target_pairs={{0,4},{2,6},{4,0},{6,2},{1,5},{3,7},{5,1},{7,3},{8,12},{10,14},{12... | collective-permute-start | bytes 786440 | tf_op jit(solution)/shard_map/ppermute | solution.py:451
  77.9 26.5 %collective-permute-start.11 = (f32[256,256]{1,0:T(8,128)S(1)}, f32[256,256]{1,0:T(8,128)S(1)}, u32[]{:S(2)}, u32[]{:S(2)}) collective-permute-start(f32[256,256]{1,0:T(8,128)S(1)} %get-tuple-element.47), channel_id=1, source_target_pairs={{0,6},{2,0},{4,2},{6,4},{1,7},{3,1},{5,3},{7,5},{8,14},{10,8},{12,... | collective-permute-start | bytes 786440 | tf_op jit(solution)/shard_map/ppermute | solution.py:451
  78.0 26.4 %collective-permute-start.9 = (f32[256,256]{1,0:T(8,128)S(1)}, f32[256,256]{1,0:T(8,128)S(1)}, u32[]{:S(2)}, u32[]{:S(2)}) collective-permute-start(f32[256,256]{1,0:T(8,128)S(1)} %get-tuple-element.49), channel_id=1, source_target_pairs={{0,2},{2,4},{4,6},{6,0},{1,3},{3,5},{5,7},{7,1},{8,10},{10,12},{12... | collective-permute-start | bytes 786440 | tf_op jit(solution)/shard_map/ppermute | solution.py:451
  80.7 38.7 %collective-permute-start.13 = (f32[2,256,256]{2,1,0:T(8,128)S(1)}, f32[2,256,256]{2,1,0:T(8,128)S(1)}, u32[]{:S(2)}, u32[]{:S(2)}) collective-permute-start(f32[2,256,256]{2,1,0:T(8,128)S(1)} %select_add_fusion.1), channel_id=1, source_target_pairs={{0,1},{1,2},{2,3},{3,4},{4,5},{5,6},{6,7},{8,9},{9,10},{10,11},{11... | collective-permute-start | bytes 1572872 | tf_op jit(solution)/shard_map/ppermute | solution.py:442
  104.7 21.5 %collective-permute-start.12 = (f32[2,256,256]{2,1,0:T(8,128)S(1)}, f32[2,256,256]{2,1,0:T(8,128)S(1)}, u32[]{:S(2)}, u32[]{:S(2)}) collective-permute-start(f32[2,256,256]{2,1,0:T(8,128)S(1)} %select_add_fusion), channel_id=1, source_target_pairs={{0,1},{1,2},{2,3},{3,4},{4,5},{5,6},{6,7},{8,9},{9,10},{10,11},{11... | collective-permute-start | bytes 1572872 | tf_op jit(solution)/shard_map/ppermute | solution.py:442
  113.4 5.4 %collective-permute-start.14 = (f32[64,256]{1,0:T(8,128)S(1)}, f32[64,256]{1,0:T(8,128)S(1)}, u32[]{:S(2)}, u32[]{:S(2)}) collective-permute-start(f32[64,256]{1,0:T(8,128)S(1)} %get-tuple-element.55), channel_id=1, source_target_pairs={{0,64},{64,128},{128,192},{192,0},{1,65},{65,129},{129,193},{193,1... | collective-permute-start | bytes 196616 | tf_op jit(solution)/shard_map/ppermute | solution.py:451
  113.6 5.8 %collective-permute-start.16 = (f32[64,256]{1,0:T(8,128)S(1)}, f32[64,256]{1,0:T(8,128)S(1)}, u32[]{:S(2)}, u32[]{:S(2)}) collective-permute-start(f32[64,256]{1,0:T(8,128)S(1)} %get-tuple-element.53), channel_id=1, source_target_pairs={{0,192},{64,0},{128,64},{192,128},{1,193},{65,1},{129,65},{193,129... | collective-permute-start | bytes 196616 | tf_op jit(solution)/shard_map/ppermute | solution.py:451
  128.5 6.3 %collective-permute-start.18 = (f32[64,256]{1,0:T(8,128)S(1)}, f32[64,256]{1,0:T(8,128)S(1)}, u32[]{:S(2)}, u32[]{:S(2)}) collective-permute-start(f32[64,256]{1,0:T(8,128)S(1)} %add_add_fusion.2), channel_id=1, source_target_pairs={{0,16},{1,17},{16,0},{17,1},{32,48},{33,49},{48,32},{49,33},{2,18}... | collective-permute-start | bytes 196616 | tf_op jit(solution)/shard_map/ppermute | solution.py:485
  128.5 6.3 %collective-permute-start.19 = (f32[64,256]{1,0:T(8,128)S(1)}, f32[64,256]{1,0:T(8,128)S(1)}, u32[]{:S(2)}, u32[]{:S(2)}) collective-permute-start(f32[64,256]{1,0:T(8,128)S(1)} %add_add_fusion.2), channel_id=1, source_target_pairs={{0,17},{1,16},{16,1},{17,0},{32,49},{33,48},{48,33},{49,32},{2,19}... | collective-permute-start | bytes 196616 | tf_op jit(solution)/shard_map/ppermute | solution.py:485
  134.8 7.1 %collective-permute-start.20 = (f32[64,256]{1,0:T(8,128)S(1)}, f32[64,256]{1,0:T(8,128)S(1)}, u32[]{:S(2)}, u32[]{:S(2)}) collective-permute-start(f32[64,256]{1,0:T(8,128)S(1)} %add_add_fusion.1), channel_id=1, source_target_pairs={{0,32},{1,33},{16,48},{17,49},{32,0},{33,1},{48,16},{49,17},{2,34}... | collective-permute-start | bytes 196616 | tf_op jit(solution)/shard_map/ppermute | solution.py:485
  142.1 5.5 %collective-permute-start.23 = (f32[64,256]{1,0:T(8,128)S(1)}, f32[64,256]{1,0:T(8,128)S(1)}, u32[]{:S(2)}, u32[]{:S(2)}) collective-permute-start(f32[64,256]{1,0:T(8,128)S(1)} %get-tuple-element.41), channel_id=1, source_target_pairs={{0,192},{64,0},{128,64},{192,128},{1,193},{65,1},{129,65},{193,129... | collective-permute-start | bytes 196616 | tf_op jit(solution)/shard_map/ppermute | solution.py:451
  147.7 6.5 %collective-permute-start.24 = (f32[256,256]{1,0:T(8,128)S(1)}, f32[256,256]{1,0:T(8,128)S(1)}, u32[]{:S(2)}, u32[]{:S(2)}) collective-permute-start(f32[256,256]{1,0:T(8,128)S(1)} %bitcast.81), channel_id=1, source_target_pairs={{0,2},{2,4},{4,6},{6,0},{1,3},{3,5},{5,7},{7,1},{8,10},{10,12},{12... | collective-permute-start | bytes 786440 | tf_op jit(solution)/shard_map/ppermute | solution.py:451
  147.7 9.7 %collective-permute-start.25 = (f32[256,256]{1,0:T(8,128)S(1)}, f32[256,256]{1,0:T(8,128)S(1)}, u32[]{:S(2)}, u32[]{:S(2)}) collective-permute-start(f32[256,256]{1,0:T(8,128)S(1)} %bitcast.82), channel_id=1, source_target_pairs={{0,4},{2,6},{4,0},{6,2},{1,5},{3,7},{5,1},{7,3},{8,12},{10,14},{12... | collective-permute-start | bytes 786440 | tf_op jit(solution)/shard_map/ppermute | solution.py:451
  150.8 7.1 %collective-permute-start.26 = (f32[256,256]{1,0:T(8,128)S(1)}, f32[256,256]{1,0:T(8,128)S(1)}, u32[]{:S(2)}, u32[]{:S(2)}) collective-permute-start(f32[256,256]{1,0:T(8,128)S(1)} %bitcast.83), channel_id=1, source_target_pairs={{0,6},{2,0},{4,2},{6,4},{1,7},{3,1},{5,3},{7,5},{8,14},{10,8},{12,... | collective-permute-start | bytes 786440 | tf_op jit(solution)/shard_map/ppermute | solution.py:451
  158.0 9.2 %collective-permute-start.27 = (f32[1024,256]{1,0:T(8,128)S(1)}, f32[1024,256]{1,0:T(8,128)}, u32[]{:S(2)}, u32[]{:S(2)}) collective-permute-start(f32[1024,256]{1,0:T(8,128)S(1)} %bitcast.76), channel_id=1, source_target_pairs={{0,8},{8,0},{1,9},{9,1},{2,10},{10,2},{3,11},{11,3},{4,12},{12,4},... | collective-permute-start | bytes 3145736 | tf_op jit(solution)/shard_map/ppermute | solution.py:451
  (19 other events, 112.3 us)

commit v4 on v3

--- a/solution.py
+++ b/solution.py
@@ -334,7 +334,7 @@
             grads[p] = wrapped(place, grads[p])
 
 
-def call(kernel, args, shapes, scratch, flops):
+def call(kernel, args, shapes, scratch, flops, mib):
     spec = pl.BlockSpec(memory_space=pltpu.VMEM)
     return pl.pallas_call(
         kernel,
@@ -342,7 +342,7 @@
         out_specs=[spec] * len(shapes),
         out_shape=[jax.ShapeDtypeStruct(shape, dtype) for shape, dtype in shapes],
         scratch_shapes=[pltpu.VMEM(shape, dtype) for shape, dtype in scratch],
-        compiler_params=pltpu.CompilerParams(vmem_limit_bytes=32 * 1024 * 1024),
+        compiler_params=pltpu.CompilerParams(vmem_limit_bytes=mib << 20),
         cost_estimate=pl.CostEstimate(flops=flops, bytes_accessed=4 << 20, transcendentals=0),
     )(*args)
 
@@ -363,6 +363,7 @@
         [(probes.shape, F32), ((2, N, N), F32)],
         [operand(modes)] + products_scratch(modes),
         3 << 30,
+        20,
     )
 
 
@@ -374,6 +375,7 @@
         [((2, N, N), F32), operand(modes // 2), operand(modes // 2)],
         [((2, N, N), F32), ((N, N), F32), operand(modes)] + products_scratch(modes),
         6 << 30,
+        24,
     )
 
 
@@ -386,6 +388,7 @@
         [((modes, 2, N, N), F32), ((2, N, N), F32)],
         products_scratch(modes),
         2 << 30,
+        14,
     )
 
 
@@ -469,10 +472,10 @@
     return lax.optimization_barrier((value,) + others)[0]
 
 
-def gather(value, axis):
+def gather(value, axis, *beside):
     count, me = lax.axis_size(axis), lax.axis_index(axis)
     whole = jnp.zeros((count,) + value.shape, value.dtype)
-    whole = lax.dynamic_update_index_in_dim(whole, value, me, 0)
+    whole = after(lax.dynamic_update_index_in_dim(whole, value, me, 0), *beside)
     for step in range(1, count):
         part = ring(value, axis, step)
         whole = lax.dynamic_update_index_in_dim(whole, part, (me + count - step) % count, 0)
@@ -485,12 +488,28 @@
     return lax.ppermute(value, axes, [(i, i ^ bits) for i in range(count)])
 
 
-def spread(value, order):
+def summed_over_z(value):
     value = (value + exchange(value, 1)) + (exchange(value, 2) + exchange(value, 3))
-    value = value + exchange(value, 4)
-    for axis in order[::-1] + ("core",):
-        value = gather(value, axis).reshape(-1, N)
-    return value
+    return value + exchange(value, 4)
+
+
+def place_kernel(index, source, *refs):
+    target, semaphore = refs[-2:]
+    copy = pltpu.make_async_copy(source, target.at[index[0]], semaphore)
+    copy.start()
+    copy.wait()
+
+
+def placed(index, value, whole):
+    anywhere = pl.BlockSpec(memory_space=pl.ANY)
+    return pl.pallas_call(
+        place_kernel,
+        in_specs=[pl.BlockSpec(memory_space=pltpu.SMEM)] + [anywhere] * (1 if whole is None else 2),
+        out_specs=anywhere,
+        out_shape=jax.ShapeDtypeStruct((2,) + value.shape, value.dtype),
+        scratch_shapes=[pltpu.SemaphoreType.DMA],
+        input_output_aliases={} if whole is None else {2: 0},
+    )(index, value, *([] if whole is None else [whole]))
 
 
 def moved(value, even, odd):
@@ -519,14 +538,12 @@
     place = jnp.stack([yp, xp, odd, live]).astype(jnp.int32)
     flip, table, phases = staged(lax.axis_index("core").astype(jnp.int32).reshape(1), probe_modes)
     mine, other = [], []
-    rights = [shifted(object_field[s], TILE, -1) for s in range(2)]
-    rights[0] = after(rights[0], flip)
+    right = after(shifted(object_field, TILE, -1), flip)
     for s in range(2):
-        mixed = jnp.where(col < xq, rights[s], object_field[s])
-        mine.append(jnp.where(col < xp, rights[s], object_field[s]))
+        mixed = jnp.where(col < xq, right[s], object_field[s])
+        mine.append(jnp.where(col < xp, right[s], object_field[s]))
         other.append(moved(mixed, -1, 1))
-        if s == 0:
-            rights[1] = after(rights[1], mixed)
+        right = after(right, mixed)
 
     def split(grads, arrived):
         kept = jnp.where(((row >= yp) != is_odd) & ~first_row, grads, 0.0)
@@ -554,7 +571,12 @@
     partial = scatter_sum(across, "y")
     partial = after(partial, received0, received1)
     object_grad = jnp.stack([staying0 + received0, staying1 + received1])
-    probe_grad = spread(partial, ("x", "y")).reshape(probe_modes.shape)
+    total = gather(summed_over_z(partial), "y").reshape(-1, N)
+    total = gather(total, "x", object_grad).reshape(-1, N)
+    core = lax.axis_index("core").astype(jnp.int32).reshape(1)
+    whole = placed(core, total, None)
+    opposite = lax.ppermute(total, "core", [(0, 1), (1, 0)])
+    probe_grad = placed(1 - core, opposite, whole).reshape(probe_modes.shape)
     return (object_grad, probe_grad)
 
 

time: 171 us -> 242 us (1.42)
  Pallas kernels: 23.3 us -> 88.9 us
  waiting for transfers between devices: 31.1 us -> 60.3 us
  starting transfers between devices: 87.8 us -> 69.2 us
  local copies, waits for them, and re-layouts: 11.9 us -> 7.14 us
    pallas_call x0 -> x2, Pallas kernels: none -> 65.7 us  [placed(): pl.pallas_call(place_kernel, in_specs=[pl.BlockSpec(memory_space=pltpu.SM...]
    ppermute x4 -> x3, starting transfers between devices: 34.9 us -> 7.39 us  [shifted(): lax.ppermute(value, axes, [(source, source + steps) for source in range(f...]
    ppermute x13 -> x12, waiting for transfers between devices: 13.1 us -> 36.6 us  [ring(): lax.ppermute(value, axis, [(i, (i + step) % count) for i in range(count)])]
    ppermute x5, starting transfers between devices: 27.4 us -> 16.8 us  [moved(): return lax.ppermute(value, POS + TILE, pairs)]
    ppermute x13 -> x12, starting transfers between devices: 16.6 us -> 25.5 us  [ring(): lax.ppermute(value, axis, [(i, (i + step) % count) for i in range(count)])]
    ppermute x0 -> x1, starting transfers between devices: none -> 6.66 us  [per_device(): opposite = lax.ppermute(total, 'core', [(0, 1), (1, 0)])]
    ppermute x5, waiting for transfers between devices: 0.01 us -> 6.12 us  [moved(): return lax.ppermute(value, POS + TILE, pairs)]
    ppermute x4, waiting for transfers between devices: 11.2 us -> 6.17 us  [exchange(): return lax.ppermute(value, axes, [(i, i ^ bits) for i in range(count)])]
  transfers between devices with their start and end apart: 28 -> 27, of which waited for: 10 -> 16; matrix products, arithmetic and copies ran while one was open for 6% -> 4% of each run, Pallas kernels for 8% -> 19%
where the time goes in v4:
time: 242 us; the launch traced here: 241 us
  Pallas kernels  88.9 us (37%)
  starting transfers between devices  69.2 us (29%)
  waiting for transfers between devices  60.3 us (25%)
  other arithmetic  9.24 us (4%)
  local copies, waits for them, and re-layouts  7.14 us (3%)
  between operations  6.27 us (3%)
    pallas_call x2, Pallas kernels, placed(): pl.pallas_call(place_kernel, in_specs=[pl.BlockSpec(memory_space=pltpu.SM...  65.7 us
    ppermute x12, waiting for transfers between devices, ring(): lax.ppermute(value, axis, [(i, (i + step) % count) for i in range(count)])  36.6 us
    ppermute x12, starting transfers between devices, ring(): lax.ppermute(value, axis, [(i, (i + step) % count) for i in range(count)])  25.5 us
    ppermute x5, starting transfers between devices, moved(): return lax.ppermute(value, POS + TILE, pairs)  16.8 us
    pallas_call x4, Pallas kernels, call(): pl.pallas_call(kernel, in_specs=[pl.BlockSpec(memory_space=pltpu.SMEM)] +...  15.9 us
    ppermute x3, waiting for transfers between devices, shifted(): lax.ppermute(value, axes, [(source, source + steps) for source in range(f...  11.5 us
    ppermute x4, starting transfers between devices, exchange(): return lax.ppermute(value, axes, [(i, i ^ bits) for i in range(count)])  8.35 us
    ppermute x3, starting transfers between devices, shifted(): lax.ppermute(value, axes, [(source, source + steps) for source in range(f...  7.39 us
  transfers between devices with their start and end apart: 27, of which 16 were waited for; matrix products, arithmetic and copies ran while one was open for 4% of the time, Pallas kernels for 19%

profile of v4, /device:TPU:1, one launch (start us, length us, event | category | flops | bytes accessed | tf_op | source)
XLA Modules:
  0.0 241.1 jit_solution(15452545340475090700)
XLA Ops:
  1.9 4.5 %collective-permute-start = (s32[1,2]{1,0:T(1,128)}, s32[1,2]{1,0:T(1,128)S(1)}, u32[]{:S(2)}, u32[]{:S(2)}) collective-permute-start(s32[1,2]{1,0:T(1,128)} %param.9), channel_id=1, source_target_pairs={{0,8},{8,16},{16,24},{24,32},{32,40},{40,48},{48,56},{56,64},{64,7... | collective-permute-start | bytes 32 | tf_op jit(solution)/shard_map/ppermute | solution.py:533
  6.4 7.2 %shard_map.77 = (f32[8,256,256]{2,1,0:T(8,128)}, bf16[5,2,256,256]{3,2,1,0:T(8,128)(2,1)}, f32[2,256,256]{2,1,0:T(8,128)}) custom-call(s32[1]{0:T(128)} %bitcast.8.core.index, f32[8,256,256]{2,1,0:T(8,128)} %bitcast.74, bf16[5,2,256,256]{3,2,1,0:T(8,128)(2,1)} %constant.146.clone.table, f32[2,256,256]{2,1,0:T(8,128)} %constant.147.clone.phases), custom_call_target="tpu_custom_call" | custom-call | tf_op jit(solution)/shard_map/pallas_call | solution.py:410
  17.5 8.7 %collective-permute-done.1 = f32[2,2,256,256]{3,2,1,0:T(8,128)S(1)} collective-permute-done((f32[2,2,256,256]{3,2,1,0:T(8,128)}, f32[2,2,256,256]{3,2,1,0:T(8,128)S(1)}, u32[]{:S(2)}, u32[]{:S(2)}) %collective-permute-start.1) | collective-permute-done | bytes 1048608 | tf_op jit(solution)/shard_map/ppermute | solution.py:445
  29.4 5.0 %collective-permute-start.3 = (f32[2,256,256]{2,1,0:T(8,128)}, f32[2,256,256]{2,1,0:T(8,128)S(1)}, u32[]{:S(2)}, u32[]{:S(2)}) collective-permute-start(f32[2,256,256]{2,1,0:T(8,128)} %get-tuple-element.45), channel_id=1, source_target_pairs={{1,9},{3,11},{5,13},{7,15},{8,0},{9,17},{10,2},{11,19},{12,4},{13,... | collective-permute-start | bytes 1572872 | tf_op jit(solution)/shard_map/ppermute | solution.py:524
  40.8 3.6 %collective-permute-done.3.other = f32[2,256,256]{2,1,0:T(8,128)S(1)} collective-permute-done((f32[2,256,256]{2,1,0:T(8,128)}, f32[2,256,256]{2,1,0:T(8,128)S(1)}, u32[]{:S(2)}, u32[]{:S(2)}) %collective-permute-start.3) | collective-permute-done | bytes 524320 | tf_op jit(solution)/shard_map/ppermute | solution.py:524
  44.4 3.4 %shard_map.78 = (f32[4,2,256,256]{3,2,1,0:T(8,128)S(1)}, f32[2,256,256]{2,1,0:T(8,128)S(1)}) custom-call(s32[4]{0:T(128)S(1)} %pad_add_fusion.place, f32[2,256,256]{2,1,0:T(8,128)S(1)} %get-tuple-element.44.mine, f32[2,256,256]{2,1,0:T(8,128)S(1)} %collective-permute-done.3.other, f32[4,2,256,256]{3,2,1,0:T(8,128)S(1)} %bitcast.67, ...), custom_call_target="tpu_custom_call" | custom-call | flops 3221225472 | bytes 4194304 | tf_op jit(solution)/shard_map/pallas_call | solution.py:339
  47.9 2.5 %collective-permute-done.2.other = f32[2,256,256]{2,1,0:T(8,128)S(1)} collective-permute-done((f32[2,256,256]{2,1,0:T(8,128)S(1)}, f32[2,256,256]{2,1,0:T(8,128)S(1)}, u32[]{:S(2)}, u32[]{:S(2)}) %collective-permute-start.2) | collective-permute-done | bytes 524320 | tf_op jit(solution)/shard_map/ppermute | solution.py:524
  50.3 6.9 %shard_map.79 = (f32[2,256,256]{2,1,0:T(8,128)S(1)}, bf16[2,512,512]{2,1,0:T(8,128)(2,1)S(1)}, bf16[2,512,512]{2,1,0:T(8,128)(2,1)S(1)}) custom-call(s32[4]{0:T(128)S(1)} %pad_add_fusion.place, f32[2,256,256]{2,1,0:T(8,128)S(1)} %get-tuple-element.47.mine, f32[2,256,256]{2,1,0:T(8,128)S(1)} %collective-permute-done.2.other, ...), custom_call_target="tpu_custom_call" | custom-call | flops 6442450944 | bytes 4194304 | tf_op jit(solution)/shard_map/pallas_call | solution.py:339
  57.3 3.2 %shard_map.80 = (f32[2,2,256,256]{3,2,1,0:T(8,128)}, f32[2,256,256]{2,1,0:T(8,128)S(1)}) custom-call(s32[4]{0:T(128)S(1)} %pad_add_fusion.place, bf16[2,512,512]{2,1,0:T(8,128)(2,1)S(1)} %get-tuple-element.30.back, f32[2,256,256]{2,1,0:T(8,128)S(1)} %get-tuple-element.29.obj, f32[4,2,256,256]{3,2,1,0:T(8,128)S(1)} %bitcast.68, ...), custom_call_target="tpu_custom_call" | custom-call | flops 2147483648 | bytes 4194304 | tf_op jit(solution)/shard_map/pallas_call | solution.py:339
  60.5 6.3 %collective-permute-start.7 = (f32[2,256,256]{2,1,0:T(8,128)S(1)}, f32[2,256,256]{2,1,0:T(8,128)}, u32[]{:S(2)}, u32[]{:S(2)}) collective-permute-start(f32[2,256,256]{2,1,0:T(8,128)S(1)} %get-tuple-element.35), channel_id=1, source_target_pairs={{0,8},{1,249},{2,10},{3,251},{4,12},{5,253},{6,14},{7,255},{8,16},... | collective-permute-start | bytes 1572872 | tf_op jit(solution)/shard_map/ppermute | solution.py:524
  77.6 8.2 %collective-permute-start.10 = (f32[256,256]{1,0:T(8,128)S(1)}, f32[256,256]{1,0:T(8,128)S(1)}, u32[]{:S(2)}, u32[]{:S(2)}) collective-permute-start(f32[256,256]{1,0:T(8,128)S(1)} %get-tuple-element.49), channel_id=1, source_target_pairs={{0,6},{2,0},{4,2},{6,4},{1,7},{3,1},{5,3},{7,5},{8,14},{10,8},{12,... | collective-permute-start | bytes 786440 | tf_op jit(solution)/shard_map/ppermute | solution.py:454
  88.4 4.8 %collective-permute-start.12 = (f32[2,256,256]{2,1,0:T(8,128)S(1)}, f32[2,256,256]{2,1,0:T(8,128)S(1)}, u32[]{:S(2)}, u32[]{:S(2)}) collective-permute-start(f32[2,256,256]{2,1,0:T(8,128)S(1)} %select_add_fusion.1), channel_id=1, source_target_pairs={{0,1},{1,2},{2,3},{3,4},{4,5},{5,6},{6,7},{8,9},{9,10},{10,11},{11... | collective-permute-start | bytes 1572872 | tf_op jit(solution)/shard_map/ppermute | solution.py:445
  93.2 3.4 %collective-permute-done.10 = f32[256,256]{1,0:T(8,128)S(1)} collective-permute-done((f32[256,256]{1,0:T(8,128)S(1)}, f32[256,256]{1,0:T(8,128)S(1)}, u32[]{:S(2)}, u32[]{:S(2)}) %collective-permute-start.10) | collective-permute-done | bytes 262176 | tf_op jit(solution)/shard_map/ppermute | solution.py:454
  96.7 22.7 %collective-permute-done.9 = f32[256,256]{1,0:T(8,128)S(1)} collective-permute-done((f32[256,256]{1,0:T(8,128)S(1)}, f32[256,256]{1,0:T(8,128)S(1)}, u32[]{:S(2)}, u32[]{:S(2)}) %collective-permute-start.9) | collective-permute-done | bytes 262176 | tf_op jit(solution)/shard_map/ppermute | solution.py:454
  121.7 2.9 %collective-permute-start.14 = (f32[64,256]{1,0:T(8,128)S(1)}, f32[64,256]{1,0:T(8,128)S(1)}, u32[]{:S(2)}, u32[]{:S(2)}) collective-permute-start(f32[64,256]{1,0:T(8,128)S(1)} %get-tuple-element.54), channel_id=1, source_target_pairs={{0,128},{64,192},{128,0},{192,64},{1,129},{65,193},{129,1},{193,65... | collective-permute-start | bytes 196616 | tf_op jit(solution)/shard_map/ppermute | solution.py:454
  128.6 2.8 %collective-permute-done.11 = f32[2,256,256]{2,1,0:T(8,128)S(1)} collective-permute-done((f32[2,256,256]{2,1,0:T(8,128)S(1)}, f32[2,256,256]{2,1,0:T(8,128)S(1)}, u32[]{:S(2)}, u32[]{:S(2)}) %collective-permute-start.11) | collective-permute-done | bytes 524320 | tf_op jit(solution)/shard_map/ppermute | solution.py:445
  135.7 3.1 %collective-permute-done.17 = f32[64,256]{1,0:T(8,128)S(1)} collective-permute-done((f32[64,256]{1,0:T(8,128)S(1)}, f32[64,256]{1,0:T(8,128)S(1)}, u32[]{:S(2)}, u32[]{:S(2)}) %collective-permute-start.17) | collective-permute-done | bytes 65568 | tf_op jit(solution)/shard_map/ppermute | solution.py:488
  138.8 4.1 %collective-permute-start.19 = (f32[64,256]{1,0:T(8,128)S(1)}, f32[64,256]{1,0:T(8,128)S(1)}, u32[]{:S(2)}, u32[]{:S(2)}) collective-permute-start(f32[64,256]{1,0:T(8,128)S(1)} %add_add_fusion.1), channel_id=1, source_target_pairs={{0,32},{1,33},{16,48},{17,49},{32,0},{33,1},{48,16},{49,17},{2,34}... | collective-permute-start | bytes 196616 | tf_op jit(solution)/shard_map/ppermute | solution.py:488
  142.8 3.1 %collective-permute-done.19 = f32[64,256]{1,0:T(8,128)S(1)} collective-permute-done((f32[64,256]{1,0:T(8,128)S(1)}, f32[64,256]{1,0:T(8,128)S(1)}, u32[]{:S(2)}, u32[]{:S(2)}) %collective-permute-start.19) | collective-permute-done | bytes 65568 | tf_op jit(solution)/shard_map/ppermute | solution.py:488
  146.5 3.5 %collective-permute-start.21 = (f32[64,256]{1,0:T(8,128)S(1)}, f32[64,256]{1,0:T(8,128)S(1)}, u32[]{:S(2)}, u32[]{:S(2)}) collective-permute-start(f32[64,256]{1,0:T(8,128)S(1)} %get-tuple-element.43), channel_id=1, source_target_pairs={{0,128},{64,192},{128,0},{192,64},{1,129},{65,193},{129,1},{193,65... | collective-permute-start | bytes 196616 | tf_op jit(solution)/shard_map/ppermute | solution.py:454
  157.5 3.4 %collective-permute-start.24 = (f32[256,256]{1,0:T(8,128)S(1)}, f32[256,256]{1,0:T(8,128)S(1)}, u32[]{:S(2)}, u32[]{:S(2)}) collective-permute-start(f32[256,256]{1,0:T(8,128)S(1)} %bitcast.77), channel_id=1, source_target_pairs={{0,4},{2,6},{4,0},{6,2},{1,5},{3,7},{5,1},{7,3},{8,12},{10,14},{12... | collective-permute-start | bytes 786440 | tf_op jit(solution)/shard_map/ppermute | solution.py:454
  167.5 6.7 %collective-permute-start.26 = (f32[1024,256]{1,0:T(8,128)S(1)}, f32[1024,256]{1,0:T(8,128)S(1)}, u32[]{:S(2)}, u32[]{:S(2)}) collective-permute-start(f32[1024,256]{1,0:T(8,128)S(1)} %bitcast.72), channel_id=1, source_target_pairs={{0,8},{8,0},{1,9},{9,1},{2,10},{10,2},{3,11},{11,3},{4,12},{12,4},... | collective-permute-start | bytes 3145736 | tf_op jit(solution)/shard_map/ppermute | solution.py:578
  174.1 32.9 %shard_map.82.refs_0_ = f32[2,1024,256]{2,1,0:T(8,128)} custom-call(s32[1]{0:T(128)} %bitcast.8.core.index, f32[1024,256]{1,0:T(8,128)} %bitcast.73), custom_call_target="tpu_custom_call" | custom-call | tf_op jit(solution)/shard_map/pallas_call | solution.py:505
  208.0 32.9 %shard_map.83 = f32[2,1024,256]{2,1,0:T(8,128)} custom-call(s32[1]{0:T(128)S(6)} %sub.2.index, f32[1024,256]{1,0:T(8,128)} %copy-done.10, f32[2,1024,256]{2,1,0:T(8,128)} %shard_map.82.refs_0_), custom_call_target="tpu_custom_call", output_to_operand_aliasing={{}: (2, {})} | custom-call | tf_op jit(solution)/shard_map/pallas_call | solution.py:505
  (90 shorter events, 49.1 us)
Async XLA Ops:
  0.6 25.5 %collective-permute-start.1 = (f32[2,2,256,256]{3,2,1,0:T(8,128)}, f32[2,2,256,256]{3,2,1,0:T(8,128)S(1)}, u32[]{:S(2)}, u32[]{:S(2)}) collective-permute-start(f32[2,2,256,256]{3,2,1,0:T(8,128)} %param.6), channel_id=1, source_target_pairs={{1,0},{2,1},{3,2},{4,3},{5,4},{6,5},{7,6},{9,8},{10,9},{11,10},{12... | collective-permute-start | bytes 3145736 | tf_op jit(solution)/shard_map/ppermute | solution.py:445
  1.9 12.3 %collective-permute-start = (s32[1,2]{1,0:T(1,128)}, s32[1,2]{1,0:T(1,128)S(1)}, u32[]{:S(2)}, u32[]{:S(2)}) collective-permute-start(s32[1,2]{1,0:T(1,128)} %param.9), channel_id=1, source_target_pairs={{0,8},{8,16},{16,24},{24,32},{32,40},{40,48},{48,56},{56,64},{64,7... | collective-permute-start | bytes 32 | tf_op jit(solution)/shard_map/ppermute | solution.py:533
  29.4 15.0 %collective-permute-start.3 = (f32[2,256,256]{2,1,0:T(8,128)}, f32[2,256,256]{2,1,0:T(8,128)S(1)}, u32[]{:S(2)}, u32[]{:S(2)}) collective-permute-start(f32[2,256,256]{2,1,0:T(8,128)} %get-tuple-element.45), channel_id=1, source_target_pairs={{1,9},{3,11},{5,13},{7,15},{8,0},{9,17},{10,2},{11,19},{12,4},{13,... | collective-permute-start | bytes 1572872 | tf_op jit(solution)/shard_map/ppermute | solution.py:524
  34.5 13.4 %collective-permute-start.4 = (f32[1,256,256]{2,1,0:T(8,128)}, f32[1,256,256]{2,1,0:T(8,128)S(1)}, u32[]{:S(2)}, u32[]{:S(2)}) collective-permute-start(f32[1,256,256]{2,1,0:T(8,128)} %param.8), channel_id=1, source_target_pairs={{0,0},{1,9},{2,2},{3,11},{4,4},{5,13},{6,6},{7,15},{8,8},{9,17},{1... | collective-permute-start | bytes 786440 | tf_op jit(solution)/shard_map/ppermute | solution.py:524
  38.7 11.7 %collective-permute-start.2 = (f32[2,256,256]{2,1,0:T(8,128)S(1)}, f32[2,256,256]{2,1,0:T(8,128)S(1)}, u32[]{:S(2)}, u32[]{:S(2)}) collective-permute-start(f32[2,256,256]{2,1,0:T(8,128)S(1)} %get-tuple-element.46), channel_id=1, source_target_pairs={{1,9},{3,11},{5,13},{7,15},{8,0},{9,17},{10,2},{11,19},{12,4},{13,... | collective-permute-start | bytes 1572872 | tf_op jit(solution)/shard_map/ppermute | solution.py:524
  60.5 15.5 %collective-permute-start.6 = (f32[2,2,256,256]{3,2,1,0:T(8,128)}, f32[2,2,256,256]{3,2,1,0:T(8,128)}, u32[]{:S(2)}, u32[]{:S(2)}) collective-permute-start(f32[2,2,256,256]{3,2,1,0:T(8,128)} %get-tuple-element.34), channel_id=1, source_target_pairs={{0,8},{8,0},{1,9},{9,1},{2,10},{10,2},{3,11},{11,3},{4,12},{12,4},... | collective-permute-start | bytes 3145736 | tf_op jit(solution)/shard_map/ppermute | solution.py:559
  60.5 26.7 %collective-permute-start.7 = (f32[2,256,256]{2,1,0:T(8,128)S(1)}, f32[2,256,256]{2,1,0:T(8,128)}, u32[]{:S(2)}, u32[]{:S(2)}) collective-permute-start(f32[2,256,256]{2,1,0:T(8,128)S(1)} %get-tuple-element.35), channel_id=1, source_target_pairs={{0,8},{1,249},{2,10},{3,251},{4,12},{5,253},{6,14},{7,255},{8,16},... | collective-permute-start | bytes 1572872 | tf_op jit(solution)/shard_map/ppermute | solution.py:524
  74.1 45.4 %collective-permute-start.5 = (f32[2,256,256]{2,1,0:T(8,128)S(1)}, f32[2,256,256]{2,1,0:T(8,128)S(1)}, u32[]{:S(2)}, u32[]{:S(2)}) collective-permute-start(f32[2,256,256]{2,1,0:T(8,128)S(1)} %get-tuple-element.32), channel_id=1, source_target_pairs={{0,8},{1,249},{2,10},{3,251},{4,12},{5,253},{6,14},{7,255},{8,16},... | collective-permute-start | bytes 1572872 | tf_op jit(solution)/shard_map/ppermute | solution.py:524
  77.6 19.1 %collective-permute-start.10 = (f32[256,256]{1,0:T(8,128)S(1)}, f32[256,256]{1,0:T(8,128)S(1)}, u32[]{:S(2)}, u32[]{:S(2)}) collective-permute-start(f32[256,256]{1,0:T(8,128)S(1)} %get-tuple-element.49), channel_id=1, source_target_pairs={{0,6},{2,0},{4,2},{6,4},{1,7},{3,1},{5,3},{7,5},{8,14},{10,8},{12,... | collective-permute-start | bytes 786440 | tf_op jit(solution)/shard_map/ppermute | solution.py:454
  85.8 10.9 %collective-permute-start.8 = (f32[256,256]{1,0:T(8,128)S(1)}, f32[256,256]{1,0:T(8,128)S(1)}, u32[]{:S(2)}, u32[]{:S(2)}) collective-permute-start(f32[256,256]{1,0:T(8,128)S(1)} %get-tuple-element.51), channel_id=1, source_target_pairs={{0,2},{2,4},{4,6},{6,0},{1,3},{3,5},{5,7},{7,1},{8,10},{10,12},{12... | collective-permute-start | bytes 786440 | tf_op jit(solution)/shard_map/ppermute | solution.py:454
  85.8 33.6 %collective-permute-start.9 = (f32[256,256]{1,0:T(8,128)S(1)}, f32[256,256]{1,0:T(8,128)S(1)}, u32[]{:S(2)}, u32[]{:S(2)}) collective-permute-start(f32[256,256]{1,0:T(8,128)S(1)} %get-tuple-element.50), channel_id=1, source_target_pairs={{0,4},{2,6},{4,0},{6,2},{1,5},{3,7},{5,1},{7,3},{8,12},{10,14},{12... | collective-permute-start | bytes 786440 | tf_op jit(solution)/shard_map/ppermute | solution.py:454
  88.4 40.2 %collective-permute-start.12 = (f32[2,256,256]{2,1,0:T(8,128)S(1)}, f32[2,256,256]{2,1,0:T(8,128)S(1)}, u32[]{:S(2)}, u32[]{:S(2)}) collective-permute-start(f32[2,256,256]{2,1,0:T(8,128)S(1)} %select_add_fusion.1), channel_id=1, source_target_pairs={{0,1},{1,2},{2,3},{3,4},{4,5},{5,6},{6,7},{8,9},{9,10},{10,11},{11... | collective-permute-start | bytes 1572872 | tf_op jit(solution)/shard_map/ppermute | solution.py:445
  119.7 11.7 %collective-permute-start.11 = (f32[2,256,256]{2,1,0:T(8,128)S(1)}, f32[2,256,256]{2,1,0:T(8,128)S(1)}, u32[]{:S(2)}, u32[]{:S(2)}) collective-permute-start(f32[2,256,256]{2,1,0:T(8,128)S(1)} %select_add_fusion), channel_id=1, source_target_pairs={{0,1},{1,2},{2,3},{3,4},{4,5},{5,6},{6,7},{8,9},{9,10},{10,11},{11... | collective-permute-start | bytes 1572872 | tf_op jit(solution)/shard_map/ppermute | solution.py:445
  121.0 4.4 %collective-permute-start.13 = (f32[64,256]{1,0:T(8,128)S(1)}, f32[64,256]{1,0:T(8,128)S(1)}, u32[]{:S(2)}, u32[]{:S(2)}) collective-permute-start(f32[64,256]{1,0:T(8,128)S(1)} %get-tuple-element.55), channel_id=1, source_target_pairs={{0,64},{64,128},{128,192},{192,0},{1,65},{65,129},{129,193},{193,1... | collective-permute-start | bytes 196616 | tf_op jit(solution)/shard_map/ppermute | solution.py:454
  121.7 5.3 %collective-permute-start.14 = (f32[64,256]{1,0:T(8,128)S(1)}, f32[64,256]{1,0:T(8,128)S(1)}, u32[]{:S(2)}, u32[]{:S(2)}) collective-permute-start(f32[64,256]{1,0:T(8,128)S(1)} %get-tuple-element.54), channel_id=1, source_target_pairs={{0,128},{64,192},{128,0},{192,64},{1,129},{65,193},{129,1},{193,65... | collective-permute-start | bytes 196616 | tf_op jit(solution)/shard_map/ppermute | solution.py:454
  133.6 5.1 %collective-permute-start.17 = (f32[64,256]{1,0:T(8,128)S(1)}, f32[64,256]{1,0:T(8,128)S(1)}, u32[]{:S(2)}, u32[]{:S(2)}) collective-permute-start(f32[64,256]{1,0:T(8,128)S(1)} %add_add_fusion.2), channel_id=1, source_target_pairs={{0,16},{1,17},{16,0},{17,1},{32,48},{33,49},{48,32},{49,33},{2,18}... | collective-permute-start | bytes 196616 | tf_op jit(solution)/shard_map/ppermute | solution.py:488
  133.6 5.1 %collective-permute-start.18 = (f32[64,256]{1,0:T(8,128)S(1)}, f32[64,256]{1,0:T(8,128)S(1)}, u32[]{:S(2)}, u32[]{:S(2)}) collective-permute-start(f32[64,256]{1,0:T(8,128)S(1)} %add_add_fusion.2), channel_id=1, source_target_pairs={{0,17},{1,16},{16,1},{17,0},{32,49},{33,48},{48,33},{49,32},{2,19}... | collective-permute-start | bytes 196616 | tf_op jit(solution)/shard_map/ppermute | solution.py:488
  138.8 7.2 %collective-permute-start.19 = (f32[64,256]{1,0:T(8,128)S(1)}, f32[64,256]{1,0:T(8,128)S(1)}, u32[]{:S(2)}, u32[]{:S(2)}) collective-permute-start(f32[64,256]{1,0:T(8,128)S(1)} %add_add_fusion.1), channel_id=1, source_target_pairs={{0,32},{1,33},{16,48},{17,49},{32,0},{33,1},{48,16},{49,17},{2,34}... | collective-permute-start | bytes 196616 | tf_op jit(solution)/shard_map/ppermute | solution.py:488
  146.0 4.5 %collective-permute-start.20 = (f32[64,256]{1,0:T(8,128)S(1)}, f32[64,256]{1,0:T(8,128)S(1)}, u32[]{:S(2)}, u32[]{:S(2)}) collective-permute-start(f32[64,256]{1,0:T(8,128)S(1)} %get-tuple-element.43), channel_id=1, source_target_pairs={{0,64},{64,128},{128,192},{192,0},{1,65},{65,129},{129,193},{193,1... | collective-permute-start | bytes 196616 | tf_op jit(solution)/shard_map/ppermute | solution.py:454
  146.5 5.9 %collective-permute-start.21 = (f32[64,256]{1,0:T(8,128)S(1)}, f32[64,256]{1,0:T(8,128)S(1)}, u32[]{:S(2)}, u32[]{:S(2)}) collective-permute-start(f32[64,256]{1,0:T(8,128)S(1)} %get-tuple-element.43), channel_id=1, source_target_pairs={{0,128},{64,192},{128,0},{192,64},{1,129},{65,193},{129,1},{193,65... | collective-permute-start | bytes 196616 | tf_op jit(solution)/shard_map/ppermute | solution.py:454
  153.1 10.0 %collective-permute-start.23 = (f32[256,256]{1,0:T(8,128)S(1)}, f32[256,256]{1,0:T(8,128)S(1)}, u32[]{:S(2)}, u32[]{:S(2)}) collective-permute-start(f32[256,256]{1,0:T(8,128)S(1)} %bitcast.76), channel_id=1, source_target_pairs={{0,2},{2,4},{4,6},{6,0},{1,3},{3,5},{5,7},{7,1},{8,10},{10,12},{12... | collective-permute-start | bytes 786440 | tf_op jit(solution)/shard_map/ppermute | solution.py:454
  157.5 7.7 %collective-permute-start.24 = (f32[256,256]{1,0:T(8,128)S(1)}, f32[256,256]{1,0:T(8,128)S(1)}, u32[]{:S(2)}, u32[]{:S(2)}) collective-permute-start(f32[256,256]{1,0:T(8,128)S(1)} %bitcast.77), channel_id=1, source_target_pairs={{0,4},{2,6},{4,0},{6,2},{1,5},{3,7},{5,1},{7,3},{8,12},{10,14},{12... | collective-permute-start | bytes 786440 | tf_op jit(solution)/shard_map/ppermute | solution.py:454
  160.9 6.5 %collective-permute-start.25 = (f32[256,256]{1,0:T(8,128)S(1)}, f32[256,256]{1,0:T(8,128)S(1)}, u32[]{:S(2)}, u32[]{:S(2)}) collective-permute-start(f32[256,256]{1,0:T(8,128)S(1)} %bitcast.78), channel_id=1, source_target_pairs={{0,6},{2,0},{4,2},{6,4},{1,7},{3,1},{5,3},{7,5},{8,14},{10,8},{12,... | collective-permute-start | bytes 786440 | tf_op jit(solution)/shard_map/ppermute | solution.py:454
  167.5 39.5 %collective-permute-start.26 = (f32[1024,256]{1,0:T(8,128)S(1)}, f32[1024,256]{1,0:T(8,128)S(1)}, u32[]{:S(2)}, u32[]{:S(2)}) collective-permute-start(f32[1024,256]{1,0:T(8,128)S(1)} %bitcast.72), channel_id=1, source_target_pairs={{0,8},{8,0},{1,9},{9,1},{2,10},{10,2},{3,11},{11,3},{4,12},{12,4},... | collective-permute-start | bytes 3145736 | tf_op jit(solution)/shard_map/ppermute | solution.py:578
  (15 other events, 79.5 us)

commit v5 on v4

--- a/solution.py
+++ b/solution.py
@@ -258,7 +258,8 @@
 
 
 def second_kernel(
-    place, mine, other, q1, amplitude, table, phases, grads, back_send, back_keep,
+    place, mine, other, q1, amplitude, table, phases, probes, first_obj,
+    grads1, grads0, send, keep,
     obj, amp, op, mid, out,
 ):
     modes = q1.shape[0]
@@ -298,40 +299,36 @@
                 q = QUADS[i]
                 total[i] = add_pair(total[i], mulc(field(q1, (m,), row, q), v))
                 pairs.append(mulc(field(obj, (), row, q), v))
-            back = back_send if m < modes // 2 else back_keep
-            store_right_prop(back, m % (modes // 2), row, *fold_pairs(pairs))
+            store_right_prop(op, m, row, *fold_pairs(pairs))
         for i, q in enumerate(QUADS):
             total[i] = mulc(field(phases, (), row, q), total[i])
         for i, q in enumerate(QUADS):
-            put(grads, (0,), row, q, total[i][0])
-            put(grads, (1,), row, q, total[i][1])
-    for p in range(2):
-        grads[p] = wrapped(place, grads[p])
-
-
-def third_kernel(start, last, place, back, obj, probes, table, before, terms, grads, mid, out):
-    modes = terms.shape[0]
-    prop_products(back, mid, out, table, 1, modes)
+            put(grads1, (0,), row, q, total[i][0])
+            put(grads1, (1,), row, q, total[i][1])
+    prop_products(op, mid, out, table, 1, modes)
+    half = modes // 2
     for k in range(CHUNKS):
         row = k * CH
-        total = [field(before, (), row, q) for q in QUADS] if last else zeros()
+        total = zeros()
         for m in range(modes):
             real, imag = load_prop(out, m, row)
+            terms = send if m < half else keep
             for i, v in enumerate(zip(unfold4(*real), unfold4(*imag))):
                 q = QUADS[i]
-                total[i] = add_pair(total[i], mulc(field(probes, (start + m,), row, q), v))
-                term = mulc(field(obj, (), row, q), v)
-                put(terms, (m, 0), row, q, term[0])
-                put(terms, (m, 1), row, q, term[1])
+                total[i] = add_pair(total[i], mulc(field(probes, (m,), row, q), v))
+                term = mulc(field(first_obj, (), row, q), v)
+                put(terms, (m % half, 0), row, q, term[0])
+                put(terms, (m % half, 1), row, q, term[1])
         for i, q in enumerate(QUADS):
-            put(grads, (0,), row, q, total[i][0])
-            put(grads, (1,), row, q, total[i][1])
-    for m in range(modes):
-        for p in range(2):
-            terms[m, p] = mirror(terms[m, p])
-    if last:
-        for p in range(2):
-            grads[p] = wrapped(place, grads[p])
+            put(grads0, (0,), row, q, total[i][0])
+            put(grads0, (1,), row, q, total[i][1])
+    for terms in (send, keep):
+        for m in range(half):
+            for p in range(2):
+                terms[m, p] = mirror(terms[m, p])
+    for p in range(2):
+        grads1[p] = wrapped(place, grads1[p])
+        grads0[p] = wrapped(place, grads0[p])
 
 
 def call(kernel, args, shapes, scratch, flops, mib):
@@ -367,28 +364,16 @@
     )
 
 
-def second(place, mine, other, q1, amplitude, table, phases):
+def second(place, mine, other, q1, amplitude, table, phases, probes, first_obj):
     modes = q1.shape[0]
+    field_shape, terms_shape = ((2, N, N), F32), ((modes // 2, 2, N, N), F32)
     return call(
         second_kernel,
-        (place, mine, other, q1, amplitude, table, phases),
-        [((2, N, N), F32), operand(modes // 2), operand(modes // 2)],
-        [((2, N, N), F32), ((N, N), F32), operand(modes)] + products_scratch(modes),
-        6 << 30,
-        24,
-    )
-
-
-def third(start, place, back, obj, probes, table, before):
-    modes = probes.shape[0] // 2
-    last = before is not None
-    return call(
-        functools.partial(third_kernel, start, last),
-        (place, back, obj, probes, table, before if last else place[None]),
-        [((modes, 2, N, N), F32), ((2, N, N), F32)],
-        products_scratch(modes),
-        2 << 30,
-        14,
+        (place, mine, other, q1, amplitude, table, phases, probes, first_obj),
+        [field_shape, field_shape, terms_shape, terms_shape],
+        [field_shape, ((N, N), F32), operand(modes)] + products_scratch(modes),
+        9 << 30,
+        26,
     )
 
 
@@ -504,7 +489,8 @@
     anywhere = pl.BlockSpec(memory_space=pl.ANY)
     return pl.pallas_call(
         place_kernel,
-        in_specs=[pl.BlockSpec(memory_space=pltpu.SMEM)] + [anywhere] * (1 if whole is None else 2),
+        in_specs=[pl.BlockSpec(memory_space=pltpu.SMEM), pl.BlockSpec(memory_space=pltpu.VMEM)]
+        + [anywhere] * (0 if whole is None else 1),
         out_specs=anywhere,
         out_shape=jax.ShapeDtypeStruct((2,) + value.shape, value.dtype),
         scratch_shapes=[pltpu.SemaphoreType.DMA],
@@ -533,17 +519,13 @@
     above = lax.ppermute(corners, POS, [(i, (i + 1) % ROWS) for i in range(ROWS)])
     yp, xp = [jnp.where(is_odd, above[0, i], corners[0, i]) for i in (0, 1)]
     yq, xq = [jnp.where(is_odd, corners[0, i], above[0, i]) for i in (0, 1)]
-    amplitude = moved(amplitudes, 0, 1)
     live = jnp.where(first_row, 0, 1)
     place = jnp.stack([yp, xp, odd, live]).astype(jnp.int32)
     flip, table, phases = staged(lax.axis_index("core").astype(jnp.int32).reshape(1), probe_modes)
-    mine, other = [], []
-    right = after(shifted(object_field, TILE, -1), flip)
-    for s in range(2):
-        mixed = jnp.where(col < xq, right[s], object_field[s])
-        mine.append(jnp.where(col < xp, right[s], object_field[s]))
-        other.append(moved(mixed, -1, 1))
-        right = after(right, mixed)
+    right = after(shifted(after(object_field, above), TILE, -1), flip)
+    mixed = jnp.where(col < xq, right, object_field)
+    mine = jnp.where(col < xp, right, object_field)
+    other = [moved(mixed[s], -1, 1) for s in range(2)]
 
     def split(grads, arrived):
         kept = jnp.where(((row >= yp) != is_odd) & ~first_row, grads, 0.0)
@@ -552,31 +534,30 @@
         staying = jnp.where(col >= xp, kept, 0.0) + jnp.where(col >= xq, taken, 0.0)
         return staying, leaving
 
+    amplitude = moved(after(amplitudes, mixed), 0, 1)
     q1, obj = first(place, mine[0], other[0], flip, table)
-    grads1, back_send, back_keep = second(place, mine[1], other[1], q1, amplitude, table, phases)
+    grads1, grads0, send, keep = second(
+        place, mine[1], other[1], q1, amplitude, table, phases, flip, obj
+    )
+    swap = [(0, 1), (1, 0)]
     arrived1 = moved(grads1, 1, -1)
-    send, part = third(0, place, back_send, obj, flip, table, None)
-    got = lax.ppermute(send, "core", [(0, 1), (1, 0)])
-    keep, grads0 = third(MODES // 2, place, back_keep, obj, flip, table, part)
-    arrived0 = moved(grads0, 1, -1)
-    across = pieces(keep + got, "x")
+    across = pieces(keep + lax.ppermute(send, "core", swap), "y")
     staying1, leaving1 = split(grads1, after(arrived1, *across))
     received1 = shifted(leaving1, TILE, 1)
     across[-1] = after(across[-1], leaving1)
-    partial = scatter_sum(across, "x")
-    across = pieces(partial, "y")
-    staying0, leaving0 = split(grads0, after(arrived0, *across))
-    received0 = shifted(leaving0, TILE, 1)
-    across[-1] = after(across[-1], leaving0)
-    partial = scatter_sum(across, "y")
-    partial = after(partial, received0, received1)
-    object_grad = jnp.stack([staying0 + received0, staying1 + received1])
-    total = gather(summed_over_z(partial), "y").reshape(-1, N)
-    total = gather(total, "x", object_grad).reshape(-1, N)
+    partial = after(scatter_sum(across, "y"), received1)
+    total = summed_over_z(scatter_sum(pieces(partial, "x"), "x"))
+    grads0 = after(grads0, total)
+    arrived0 = moved(grads0, 1, -1)
+    total = gather(total, "x").reshape(-1, N)
+    staying0, leaving0 = split(grads0, arrived0)
+    received0 = shifted(after(leaving0, total), TILE, 1)
+    total = after(gather(total, "y", leaving0).reshape(-1, N), received0)
     core = lax.axis_index("core").astype(jnp.int32).reshape(1)
     whole = placed(core, total, None)
-    opposite = lax.ppermute(total, "core", [(0, 1), (1, 0)])
-    probe_grad = placed(1 - core, opposite, whole).reshape(probe_modes.shape)
+    probe_grad = placed(1 - core, lax.ppermute(total, "core", swap), whole)
+    probe_grad = probe_grad.reshape(probe_modes.shape)
+    object_grad = jnp.stack([staying0 + received0, staying1 + received1])
     return (object_grad, probe_grad)
 
 

time: 242 us -> 167 us (0.69)
  Pallas kernels: 88.9 us -> 25.9 us
  waiting for transfers between devices: 60.3 us -> 48.5 us
  starting transfers between devices: 69.2 us -> 73.3 us
  other arithmetic: 9.24 us -> 6.64 us
  local copies, waits for them, and re-layouts: 7.14 us -> 4.58 us
    pallas_call x2, Pallas kernels: 65.7 us -> 4.4 us  [placed(): pl.pallas_call(place_kernel, in_specs=[pl.BlockSpec(memory_space=pltpu.SM...]
    ppermute x12, waiting for transfers between devices: 36.6 us -> 22.3 us  [ring(): lax.ppermute(value, axis, [(i, (i + step) % count) for i in range(count)])]
    ppermute x3, starting transfers between devices: 7.39 us -> 17.3 us  [shifted(): lax.ppermute(value, axes, [(source, source + steps) for source in range(f...]
    ppermute x5, starting transfers between devices: 16.8 us -> 25.5 us  [moved(): return lax.ppermute(value, POS + TILE, pairs)]
    ppermute x12, starting transfers between devices: 25.5 us -> 18.2 us  [ring(): lax.ppermute(value, axis, [(i, (i + step) % count) for i in range(count)])]
    unnamed x24 -> x16, local copies, waits for them, and re-layouts: 5.56 us -> 0.03 us
    ppermute x2, starting transfers between devices: 6.66 us -> 1.49 us  [the longest x1 1.49 us: per_device(): probe_grad = placed(1 - core, lax.ppermute(total, 'core', swap), whole)]
    select_n x2 -> x1, other arithmetic: 3.66 us -> 1.11 us  [per_device(): mixed = jnp.where(col < xq, right, object_field)]
  transfers between devices with their start and end apart: 27 -> 27, of which waited for: 16 -> 16; matrix products, arithmetic and copies ran while one was open for 4% -> 5% of each run, Pallas kernels for 19% -> 8%
where the time goes in v5:
time: 167 us; the launch traced here: 165 us
  starting transfers between devices  73.3 us (44%)
  waiting for transfers between devices  48.5 us (29%)
  Pallas kernels  25.9 us (16%)
  other arithmetic  6.64 us (4%)
  between operations  6.09 us (4%)
  local copies, waits for them, and re-layouts  4.58 us (3%)
    ppermute x5, starting transfers between devices, moved(): return lax.ppermute(value, POS + TILE, pairs)  25.5 us
    ppermute x12, waiting for transfers between devices, ring(): lax.ppermute(value, axis, [(i, (i + step) % count) for i in range(count)])  22.3 us
    ppermute x12, starting transfers between devices, ring(): lax.ppermute(value, axis, [(i, (i + step) % count) for i in range(count)])  18.2 us
    ppermute x3, starting transfers between devices, shifted(): lax.ppermute(value, axes, [(source, source + steps) for source in range(f...  17.3 us
    pallas_call x2, Pallas kernels, call(): pl.pallas_call(kernel, in_specs=[pl.BlockSpec(memory_space=pltpu.SMEM)] +...  14.3 us
    ppermute x3, waiting for transfers between devices, shifted(): lax.ppermute(value, axes, [(source, source + steps) for source in range(f...  9.43 us
    ppermute x5, waiting for transfers between devices, moved(): return lax.ppermute(value, POS + TILE, pairs)  8.3 us
    ppermute x4, waiting for transfers between devices, exchange(): return lax.ppermute(value, axes, [(i, i ^ bits) for i in range(count)])  7.61 us
  transfers between devices with their start and end apart: 27, of which 16 were waited for; matrix products, arithmetic and copies ran while one was open for 5% of the time, Pallas kernels for 8%

profile of v5, /device:TPU:1, one launch (start us, length us, event | category | flops | bytes accessed | tf_op | source)
XLA Modules:
  0.0 165.0 jit_solution(18313988844841352527)
XLA Ops:
  0.6 4.5 %collective-permute-start = (s32[1,2]{1,0:T(1,128)}, s32[1,2]{1,0:T(1,128)S(1)}, u32[]{:S(2)}, u32[]{:S(2)}) collective-permute-start(s32[1,2]{1,0:T(1,128)} %param.9), channel_id=1, source_target_pairs={{0,8},{8,16},{16,24},{24,32},{32,40},{40,48},{48,56},{56,64},{64,7... | collective-permute-start | bytes 32 | tf_op jit(solution)/shard_map/ppermute | solution.py:519
  7.3 7.2 %shard_map.77 = (f32[8,256,256]{2,1,0:T(8,128)}, bf16[5,2,256,256]{3,2,1,0:T(8,128)(2,1)}, f32[2,256,256]{2,1,0:T(8,128)}) custom-call(s32[1]{0:T(128)} %bitcast.8.core.index, f32[8,256,256]{2,1,0:T(8,128)} %bitcast.71, bf16[5,2,256,256]{3,2,1,0:T(8,128)(2,1)} %constant.146.clone.table, f32[2,256,256]{2,1,0:T(8,128)} %constant.147.clone.phases), custom_call_target="tpu_custom_call" | custom-call | tf_op jit(solution)/shard_map/pallas_call | solution.py:395
  18.1 9.2 %collective-permute-done.1 = f32[2,2,256,256]{3,2,1,0:T(8,128)S(1)} collective-permute-done((f32[2,2,256,256]{3,2,1,0:T(8,128)}, f32[2,2,256,256]{3,2,1,0:T(8,128)S(1)}, u32[]{:S(2)}, u32[]{:S(2)}) %collective-permute-start.1) | collective-permute-done | bytes 1048608 | tf_op jit(solution)/shard_map/ppermute | solution.py:430
  29.4 8.6 %collective-permute-start.3 = (f32[2,256,256]{2,1,0:T(8,128)}, f32[2,256,256]{2,1,0:T(8,128)}, u32[]{:S(2)}, u32[]{:S(2)}) collective-permute-start(f32[2,256,256]{2,1,0:T(8,128)} %get-tuple-element.48), channel_id=1, source_target_pairs={{1,9},{3,11},{5,13},{7,15},{8,0},{9,17},{10,2},{11,19},{12,4},{13,... | collective-permute-start | bytes 1572872 | tf_op jit(solution)/shard_map/ppermute | solution.py:510
  44.2 4.0 %collective-permute-done.3.other = f32[2,256,256]{2,1,0:T(8,128)} collective-permute-done((f32[2,256,256]{2,1,0:T(8,128)}, f32[2,256,256]{2,1,0:T(8,128)}, u32[]{:S(2)}, u32[]{:S(2)}) %collective-permute-start.3) | collective-permute-done | bytes 524320 | tf_op jit(solution)/shard_map/ppermute | solution.py:510
  48.2 4.0 %shard_map.78 = (f32[4,2,256,256]{3,2,1,0:T(8,128)S(1)}, f32[2,256,256]{2,1,0:T(8,128)S(1)}) custom-call(s32[4]{0:T(128)S(1)} %pad_add_fusion.place, f32[2,256,256]{2,1,0:T(8,128)S(1)} %get-tuple-element.50.mine, f32[2,256,256]{2,1,0:T(8,128)} %collective-permute-done.3.other, f32[4,2,256,256]{3,2,1,0:T(8,128)S(1)} %bitcast.65, ...), custom_call_target="tpu_custom_call" | custom-call | flops 3221225472 | bytes 4194304 | tf_op jit(solution)/shard_map/pallas_call | solution.py:336
  53.7 10.3 %shard_map.79 = (f32[2,256,256]{2,1,0:T(8,128)S(1)}, f32[2,256,256]{2,1,0:T(8,128)S(1)}, f32[2,2,256,256]{3,2,1,0:T(8,128)}, f32[2,2,256,256]{3,2,1,0:T(8,128)S(1)}) custom-call(s32[4]{0:T(128)S(1)} %pad_add_fusion.place, f32[2,256,256]{2,1,0:T(8,128)S(1)} %get-tuple-element.51.mine, f32[2,256,256]{2,1,0:T(8,128)S(1)} %collective-permute-done.2.other, ...), custom_call_target="tpu_custom_call" | custom-call | flops 9663676416 | bytes 4194304 | tf_op jit(solution)/shard_map/pallas_call | solution.py:336
  64.0 6.0 %collective-permute-start.6 = (f32[2,256,256]{2,1,0:T(8,128)S(1)}, f32[2,256,256]{2,1,0:T(8,128)S(1)}, u32[]{:S(2)}, u32[]{:S(2)}) collective-permute-start(f32[2,256,256]{2,1,0:T(8,128)S(1)} %get-tuple-element.32), channel_id=1, source_target_pairs={{0,8},{1,249},{2,10},{3,251},{4,12},{5,253},{6,14},{7,255},{8,16},... | collective-permute-start | bytes 1572872 | tf_op jit(solution)/shard_map/ppermute | solution.py:510
  73.5 2.6 %collective-permute-done.6 = f32[2,256,256]{2,1,0:T(8,128)S(1)} collective-permute-done((f32[2,256,256]{2,1,0:T(8,128)S(1)}, f32[2,256,256]{2,1,0:T(8,128)S(1)}, u32[]{:S(2)}, u32[]{:S(2)}) %collective-permute-start.6) | collective-permute-done | bytes 524320 | tf_op jit(solution)/shard_map/ppermute | solution.py:510
  76.3 9.5 %collective-permute-start.10 = (f32[2,256,256]{2,1,0:T(8,128)S(1)}, f32[2,256,256]{2,1,0:T(8,128)S(1)}, u32[]{:S(2)}, u32[]{:S(2)}) collective-permute-start(f32[2,256,256]{2,1,0:T(8,128)S(1)} %select_add_fusion.1), channel_id=1, source_target_pairs={{0,1},{1,2},{2,3},{3,4},{4,5},{5,6},{6,7},{8,9},{9,10},{10,11},{11... | collective-permute-start | bytes 1572872 | tf_op jit(solution)/shard_map/ppermute | solution.py:430
  86.0 2.6 %collective-permute-start.8 = (f32[256,256]{1,0:T(8,128)S(1)}, f32[256,256]{1,0:T(8,128)}, u32[]{:S(2)}, u32[]{:S(2)}) collective-permute-start(f32[256,256]{1,0:T(8,128)S(1)} %get-tuple-element.46), channel_id=1, source_target_pairs={{0,128},{64,192},{128,0},{192,64},{1,129},{65,193},{129,1},{193,65... | collective-permute-start | bytes 786440 | tf_op jit(solution)/shard_map/ppermute | solution.py:439
  89.7 11.0 %collective-permute-done.7 = f32[256,256]{1,0:T(8,128)} collective-permute-done((f32[256,256]{1,0:T(8,128)}, f32[256,256]{1,0:T(8,128)}, u32[]{:S(2)}, u32[]{:S(2)}) %collective-permute-start.7) | collective-permute-done | bytes 262176 | tf_op jit(solution)/shard_map/ppermute | solution.py:439
  105.7 2.0 %collective-permute-start.13 = (f32[64,256]{1,0:T(8,128)S(1)}, f32[64,256]{1,0:T(8,128)S(1)}, u32[]{:S(2)}, u32[]{:S(2)}) collective-permute-start(f32[64,256]{1,0:T(8,128)S(1)} %get-tuple-element.53), channel_id=1, source_target_pairs={{0,6},{2,0},{4,2},{6,4},{1,7},{3,1},{5,3},{7,5},{8,14},{10,8},{12,... | collective-permute-start | bytes 196616 | tf_op jit(solution)/shard_map/ppermute | solution.py:439
  110.8 2.5 %collective-permute-start.16 = (f32[64,256]{1,0:T(8,128)S(1)}, f32[64,256]{1,0:T(8,128)S(1)}, u32[]{:S(2)}, u32[]{:S(2)}) collective-permute-start(f32[64,256]{1,0:T(8,128)S(1)} %fusion.1), channel_id=1, source_target_pairs={{0,17},{1,16},{16,1},{17,0},{32,49},{33,48},{48,33},{49,32},{2,19}... | collective-permute-start | bytes 196616 | tf_op jit(solution)/shard_map/ppermute | solution.py:473
  113.9 2.6 %collective-permute-done.16 = f32[64,256]{1,0:T(8,128)S(1)} collective-permute-done((f32[64,256]{1,0:T(8,128)S(1)}, f32[64,256]{1,0:T(8,128)S(1)}, u32[]{:S(2)}, u32[]{:S(2)}) %collective-permute-start.16) | collective-permute-done | bytes 65568 | tf_op jit(solution)/shard_map/ppermute | solution.py:473
  116.5 2.7 %collective-permute-start.17 = (f32[64,256]{1,0:T(8,128)S(1)}, f32[64,256]{1,0:T(8,128)S(1)}, u32[]{:S(2)}, u32[]{:S(2)}) collective-permute-start(f32[64,256]{1,0:T(8,128)S(1)} %add_add_fusion.1), channel_id=1, source_target_pairs={{0,32},{1,33},{16,48},{17,49},{32,0},{33,1},{48,16},{49,17},{2,34}... | collective-permute-start | bytes 196616 | tf_op jit(solution)/shard_map/ppermute | solution.py:473
  119.2 4.5 %collective-permute-done.17 = f32[64,256]{1,0:T(8,128)S(1)} collective-permute-done((f32[64,256]{1,0:T(8,128)S(1)}, f32[64,256]{1,0:T(8,128)S(1)}, u32[]{:S(2)}, u32[]{:S(2)}) %collective-permute-start.17) | collective-permute-done | bytes 65568 | tf_op jit(solution)/shard_map/ppermute | solution.py:473
  123.8 3.7 %collective-permute-start.20 = (f32[64,256]{1,0:T(8,128)S(1)}, f32[64,256]{1,0:T(8,128)S(1)}, u32[]{:S(2)}, u32[]{:S(2)}) collective-permute-start(f32[64,256]{1,0:T(8,128)S(1)} %get-tuple-element.41), channel_id=1, source_target_pairs={{0,4},{2,6},{4,0},{6,2},{1,5},{3,7},{5,1},{7,3},{8,12},{10,14},{12... | collective-permute-start | bytes 196616 | tf_op jit(solution)/shard_map/ppermute | solution.py:439
  127.5 7.4 %collective-permute-start.18 = (f32[2,256,256]{2,1,0:T(8,128)S(1)}, f32[2,256,256]{2,1,0:T(8,128)S(1)}, u32[]{:S(2)}, u32[]{:S(2)}) collective-permute-start(f32[2,256,256]{2,1,0:T(8,128)S(1)} %get-tuple-element.36), channel_id=1, source_target_pairs={{0,8},{1,249},{2,10},{3,251},{4,12},{5,253},{6,14},{7,255},{8,16},... | collective-permute-start | bytes 1572872 | tf_op jit(solution)/shard_map/ppermute | solution.py:510
  135.0 2.4 %collective-permute-start.23 = (f32[256,256]{1,0:T(8,128)S(1)}, f32[256,256]{1,0:T(8,128)S(1)}, u32[]{:S(2)}, u32[]{:S(2)}) collective-permute-start(f32[256,256]{1,0:T(8,128)S(1)} %bitcast.74), channel_id=1, source_target_pairs={{0,64},{64,128},{128,192},{192,0},{1,65},{65,129},{129,193},{193,1... | collective-permute-start | bytes 786440 | tf_op jit(solution)/shard_map/ppermute | solution.py:439
  141.1 6.5 %collective-permute-start.22 = (f32[2,256,256]{2,1,0:T(8,128)S(1)}, f32[2,256,256]{2,1,0:T(8,128)}, u32[]{:S(2)}, u32[]{:S(2)}) collective-permute-start(f32[2,256,256]{2,1,0:T(8,128)S(1)} %select_add_fusion), channel_id=1, source_target_pairs={{0,1},{1,2},{2,3},{3,4},{4,5},{5,6},{6,7},{8,9},{9,10},{10,11},{11... | collective-permute-start | bytes 1572872 | tf_op jit(solution)/shard_map/ppermute | solution.py:430
  148.4 7.6 %collective-permute-done.24 = f32[256,256]{1,0:T(8,128)S(1)} collective-permute-done((f32[256,256]{1,0:T(8,128)S(1)}, f32[256,256]{1,0:T(8,128)S(1)}, u32[]{:S(2)}, u32[]{:S(2)}) %collective-permute-start.24) | collective-permute-done | bytes 262176 | tf_op jit(solution)/shard_map/ppermute | solution.py:439
  157.8 2.2 %shard_map.80.refs_0_ = f32[2,1024,256]{2,1,0:T(8,128)} custom-call(s32[1]{0:T(128)} %bitcast.8.core.index, f32[1024,256]{1,0:T(8,128)} %bitcast.70), custom_call_target="tpu_custom_call" | custom-call | tf_op jit(solution)/shard_map/pallas_call | solution.py:490
  162.6 2.2 %shard_map.81 = f32[2,1024,256]{2,1,0:T(8,128)} custom-call(s32[1]{0:T(128)S(6)} %sub.2.index, f32[1024,256]{1,0:T(8,128)} %collective-permute-done.26.source, f32[2,1024,256]{2,1,0:T(8,128)} %shard_map.80.refs_0_), custom_call_target="tpu_custom_call", output_to_operand_aliasing={{}: (2, {})} | custom-call | tf_op jit(solution)/shard_map/pallas_call | solution.py:490
  (80 shorter events, 33.2 us)
Async XLA Ops:
  0.6 5.3 %collective-permute-start = (s32[1,2]{1,0:T(1,128)}, s32[1,2]{1,0:T(1,128)S(1)}, u32[]{:S(2)}, u32[]{:S(2)}) collective-permute-start(s32[1,2]{1,0:T(1,128)} %param.9), channel_id=1, source_target_pairs={{0,8},{8,16},{16,24},{24,32},{32,40},{40,48},{48,56},{56,64},{64,7... | collective-permute-start | bytes 32 | tf_op jit(solution)/shard_map/ppermute | solution.py:519
  6.0 21.3 %collective-permute-start.1 = (f32[2,2,256,256]{3,2,1,0:T(8,128)}, f32[2,2,256,256]{3,2,1,0:T(8,128)S(1)}, u32[]{:S(2)}, u32[]{:S(2)}) collective-permute-start(f32[2,2,256,256]{3,2,1,0:T(8,128)} %param.6), channel_id=1, source_target_pairs={{1,0},{2,1},{3,2},{4,3},{5,4},{6,5},{7,6},{9,8},{10,9},{11,10},{12... | collective-permute-start | bytes 3145736 | tf_op jit(solution)/shard_map/ppermute | solution.py:430
  29.4 18.8 %collective-permute-start.3 = (f32[2,256,256]{2,1,0:T(8,128)}, f32[2,256,256]{2,1,0:T(8,128)}, u32[]{:S(2)}, u32[]{:S(2)}) collective-permute-start(f32[2,256,256]{2,1,0:T(8,128)} %get-tuple-element.48), channel_id=1, source_target_pairs={{1,9},{3,11},{5,13},{7,15},{8,0},{9,17},{10,2},{11,19},{12,4},{13,... | collective-permute-start | bytes 1572872 | tf_op jit(solution)/shard_map/ppermute | solution.py:510
  39.4 14.4 %collective-permute-start.2 = (f32[2,256,256]{2,1,0:T(8,128)}, f32[2,256,256]{2,1,0:T(8,128)S(1)}, u32[]{:S(2)}, u32[]{:S(2)}) collective-permute-start(f32[2,256,256]{2,1,0:T(8,128)} %get-tuple-element.49), channel_id=1, source_target_pairs={{1,9},{3,11},{5,13},{7,15},{8,0},{9,17},{10,2},{11,19},{12,4},{13,... | collective-permute-start | bytes 1572872 | tf_op jit(solution)/shard_map/ppermute | solution.py:510
  41.3 11.0 %collective-permute-start.4 = (f32[1,256,256]{2,1,0:T(8,128)}, f32[1,256,256]{2,1,0:T(8,128)S(1)}, u32[]{:S(2)}, u32[]{:S(2)}) collective-permute-start(f32[1,256,256]{2,1,0:T(8,128)} %param.8), channel_id=1, source_target_pairs={{0,0},{1,9},{2,2},{3,11},{4,4},{5,13},{6,6},{7,15},{8,8},{9,17},{1... | collective-permute-start | bytes 786440 | tf_op jit(solution)/shard_map/ppermute | solution.py:510
  64.0 7.3 %collective-permute-start.5 = (f32[2,2,256,256]{3,2,1,0:T(8,128)}, f32[2,2,256,256]{3,2,1,0:T(8,128)}, u32[]{:S(2)}, u32[]{:S(2)}) collective-permute-start(f32[2,2,256,256]{3,2,1,0:T(8,128)} %get-tuple-element.31), channel_id=1, source_target_pairs={{0,8},{8,0},{1,9},{9,1},{2,10},{10,2},{3,11},{11,3},{4,12},{12,4},... | collective-permute-start | bytes 3145736 | tf_op jit(solution)/shard_map/ppermute | solution.py:544
  64.0 12.1 %collective-permute-start.6 = (f32[2,256,256]{2,1,0:T(8,128)S(1)}, f32[2,256,256]{2,1,0:T(8,128)S(1)}, u32[]{:S(2)}, u32[]{:S(2)}) collective-permute-start(f32[2,256,256]{2,1,0:T(8,128)S(1)} %get-tuple-element.32), channel_id=1, source_target_pairs={{0,8},{1,249},{2,10},{3,251},{4,12},{5,253},{6,14},{7,255},{8,16},... | collective-permute-start | bytes 1572872 | tf_op jit(solution)/shard_map/ppermute | solution.py:510
  76.3 26.4 %collective-permute-start.10 = (f32[2,256,256]{2,1,0:T(8,128)S(1)}, f32[2,256,256]{2,1,0:T(8,128)S(1)}, u32[]{:S(2)}, u32[]{:S(2)}) collective-permute-start(f32[2,256,256]{2,1,0:T(8,128)S(1)} %select_add_fusion.1), channel_id=1, source_target_pairs={{0,1},{1,2},{2,3},{3,4},{4,5},{5,6},{6,7},{8,9},{9,10},{10,11},{11... | collective-permute-start | bytes 1572872 | tf_op jit(solution)/shard_map/ppermute | solution.py:430
  85.8 14.9 %collective-permute-start.7 = (f32[256,256]{1,0:T(8,128)}, f32[256,256]{1,0:T(8,128)}, u32[]{:S(2)}, u32[]{:S(2)}) collective-permute-start(f32[256,256]{1,0:T(8,128)} %get-tuple-element.47), channel_id=1, source_target_pairs={{0,64},{64,128},{128,192},{192,0},{1,65},{65,129},{129,193},{193,1... | collective-permute-start | bytes 786440 | tf_op jit(solution)/shard_map/ppermute | solution.py:439
  86.0 14.7 %collective-permute-start.8 = (f32[256,256]{1,0:T(8,128)S(1)}, f32[256,256]{1,0:T(8,128)}, u32[]{:S(2)}, u32[]{:S(2)}) collective-permute-start(f32[256,256]{1,0:T(8,128)S(1)} %get-tuple-element.46), channel_id=1, source_target_pairs={{0,128},{64,192},{128,0},{192,64},{1,129},{65,193},{129,1},{193,65... | collective-permute-start | bytes 786440 | tf_op jit(solution)/shard_map/ppermute | solution.py:439
  88.6 12.9 %collective-permute-start.9 = (f32[256,256]{1,0:T(8,128)S(1)}, f32[256,256]{1,0:T(8,128)}, u32[]{:S(2)}, u32[]{:S(2)}) collective-permute-start(f32[256,256]{1,0:T(8,128)S(1)} %get-tuple-element.45), channel_id=1, source_target_pairs={{0,192},{64,0},{128,64},{192,128},{1,193},{65,1},{129,65},{193,129... | collective-permute-start | bytes 786440 | tf_op jit(solution)/shard_map/ppermute | solution.py:439
  102.8 4.9 %collective-permute-start.11 = (f32[64,256]{1,0:T(8,128)S(1)}, f32[64,256]{1,0:T(8,128)S(1)}, u32[]{:S(2)}, u32[]{:S(2)}) collective-permute-start(f32[64,256]{1,0:T(8,128)S(1)} %get-tuple-element.52), channel_id=1, source_target_pairs={{0,2},{2,4},{4,6},{6,0},{1,3},{3,5},{5,7},{7,1},{8,10},{10,12},{12... | collective-permute-start | bytes 196616 | tf_op jit(solution)/shard_map/ppermute | solution.py:439
  104.0 4.7 %collective-permute-start.12 = (f32[64,256]{1,0:T(8,128)S(1)}, f32[64,256]{1,0:T(8,128)S(1)}, u32[]{:S(2)}, u32[]{:S(2)}) collective-permute-start(f32[64,256]{1,0:T(8,128)S(1)} %get-tuple-element.54), channel_id=1, source_target_pairs={{0,4},{2,6},{4,0},{6,2},{1,5},{3,7},{5,1},{7,3},{8,12},{10,14},{12... | collective-permute-start | bytes 196616 | tf_op jit(solution)/shard_map/ppermute | solution.py:439
  110.8 5.7 %collective-permute-start.16 = (f32[64,256]{1,0:T(8,128)S(1)}, f32[64,256]{1,0:T(8,128)S(1)}, u32[]{:S(2)}, u32[]{:S(2)}) collective-permute-start(f32[64,256]{1,0:T(8,128)S(1)} %fusion.1), channel_id=1, source_target_pairs={{0,17},{1,16},{16,1},{17,0},{32,49},{33,48},{48,33},{49,32},{2,19}... | collective-permute-start | bytes 196616 | tf_op jit(solution)/shard_map/ppermute | solution.py:473
  116.5 7.2 %collective-permute-start.17 = (f32[64,256]{1,0:T(8,128)S(1)}, f32[64,256]{1,0:T(8,128)S(1)}, u32[]{:S(2)}, u32[]{:S(2)}) collective-permute-start(f32[64,256]{1,0:T(8,128)S(1)} %add_add_fusion.1), channel_id=1, source_target_pairs={{0,32},{1,33},{16,48},{17,49},{32,0},{33,1},{48,16},{49,17},{2,34}... | collective-permute-start | bytes 196616 | tf_op jit(solution)/shard_map/ppermute | solution.py:473
  123.7 11.2 %collective-permute-start.19 = (f32[64,256]{1,0:T(8,128)S(1)}, f32[64,256]{1,0:T(8,128)S(1)}, u32[]{:S(2)}, u32[]{:S(2)}) collective-permute-start(f32[64,256]{1,0:T(8,128)S(1)} %get-tuple-element.41), channel_id=1, source_target_pairs={{0,2},{2,4},{4,6},{6,0},{1,3},{3,5},{5,7},{7,1},{8,10},{10,12},{12... | collective-permute-start | bytes 196616 | tf_op jit(solution)/shard_map/ppermute | solution.py:439
  123.8 11.1 %collective-permute-start.20 = (f32[64,256]{1,0:T(8,128)S(1)}, f32[64,256]{1,0:T(8,128)S(1)}, u32[]{:S(2)}, u32[]{:S(2)}) collective-permute-start(f32[64,256]{1,0:T(8,128)S(1)} %get-tuple-element.41), channel_id=1, source_target_pairs={{0,4},{2,6},{4,0},{6,2},{1,5},{3,7},{5,1},{7,3},{8,12},{10,14},{12... | collective-permute-start | bytes 196616 | tf_op jit(solution)/shard_map/ppermute | solution.py:439
  127.5 7.5 %collective-permute-start.21 = (f32[64,256]{1,0:T(8,128)S(1)}, f32[64,256]{1,0:T(8,128)S(1)}, u32[]{:S(2)}, u32[]{:S(2)}) collective-permute-start(f32[64,256]{1,0:T(8,128)S(1)} %get-tuple-element.41), channel_id=1, source_target_pairs={{0,6},{2,0},{4,2},{6,4},{1,7},{3,1},{5,3},{7,5},{8,14},{10,8},{12,... | collective-permute-start | bytes 196616 | tf_op jit(solution)/shard_map/ppermute | solution.py:439
  127.5 13.5 %collective-permute-start.18 = (f32[2,256,256]{2,1,0:T(8,128)S(1)}, f32[2,256,256]{2,1,0:T(8,128)S(1)}, u32[]{:S(2)}, u32[]{:S(2)}) collective-permute-start(f32[2,256,256]{2,1,0:T(8,128)S(1)} %get-tuple-element.36), channel_id=1, source_target_pairs={{0,8},{1,249},{2,10},{3,251},{4,12},{5,253},{6,14},{7,255},{8,16},... | collective-permute-start | bytes 1572872 | tf_op jit(solution)/shard_map/ppermute | solution.py:510
  135.0 13.5 %collective-permute-start.23 = (f32[256,256]{1,0:T(8,128)S(1)}, f32[256,256]{1,0:T(8,128)S(1)}, u32[]{:S(2)}, u32[]{:S(2)}) collective-permute-start(f32[256,256]{1,0:T(8,128)S(1)} %bitcast.74), channel_id=1, source_target_pairs={{0,64},{64,128},{128,192},{192,0},{1,65},{65,129},{129,193},{193,1... | collective-permute-start | bytes 786440 | tf_op jit(solution)/shard_map/ppermute | solution.py:439
  137.3 18.7 %collective-permute-start.24 = (f32[256,256]{1,0:T(8,128)S(1)}, f32[256,256]{1,0:T(8,128)S(1)}, u32[]{:S(2)}, u32[]{:S(2)}) collective-permute-start(f32[256,256]{1,0:T(8,128)S(1)} %bitcast.75), channel_id=1, source_target_pairs={{0,128},{64,192},{128,0},{192,64},{1,129},{65,193},{129,1},{193,65... | collective-permute-start | bytes 786440 | tf_op jit(solution)/shard_map/ppermute | solution.py:439
  139.2 16.9 %collective-permute-start.25 = (f32[256,256]{1,0:T(8,128)S(1)}, f32[256,256]{1,0:T(8,128)S(1)}, u32[]{:S(2)}, u32[]{:S(2)}) collective-permute-start(f32[256,256]{1,0:T(8,128)S(1)} %bitcast.76), channel_id=1, source_target_pairs={{0,192},{64,0},{128,64},{192,128},{1,193},{65,1},{129,65},{193,129... | collective-permute-start | bytes 786440 | tf_op jit(solution)/shard_map/ppermute | solution.py:439
  141.1 15.2 %collective-permute-start.22 = (f32[2,256,256]{2,1,0:T(8,128)S(1)}, f32[2,256,256]{2,1,0:T(8,128)}, u32[]{:S(2)}, u32[]{:S(2)}) collective-permute-start(f32[2,256,256]{2,1,0:T(8,128)S(1)} %select_add_fusion), channel_id=1, source_target_pairs={{0,1},{1,2},{2,3},{3,4},{4,5},{5,6},{6,7},{8,9},{9,10},{10,11},{11... | collective-permute-start | bytes 1572872 | tf_op jit(solution)/shard_map/ppermute | solution.py:430
  156.4 6.2 %collective-permute-start.26 = (f32[1024,256]{1,0:T(8,128)S(1)}, f32[1024,256]{1,0:T(8,128)}, u32[]{:S(2)}, u32[]{:S(2)}) collective-permute-start(f32[1024,256]{1,0:T(8,128)S(1)} %bitcast.69), channel_id=1, source_target_pairs={{0,8},{8,0},{1,9},{9,1},{2,10},{10,2},{3,11},{11,3},{4,12},{12,4},... | collective-permute-start | bytes 3145736 | tf_op jit(solution)/shard_map/ppermute | solution.py:558
  (11 other events, 129.4 us)

commit v6 on v5

--- a/solution.py
+++ b/solution.py
@@ -259,7 +259,7 @@
 
 def second_kernel(
     place, mine, other, q1, amplitude, table, phases, probes, first_obj,
-    grads1, grads0, send, keep,
+    grads, send, keep,
     obj, amp, op, mid, out,
 ):
     modes = q1.shape[0]
@@ -303,8 +303,8 @@
         for i, q in enumerate(QUADS):
             total[i] = mulc(field(phases, (), row, q), total[i])
         for i, q in enumerate(QUADS):
-            put(grads1, (0,), row, q, total[i][0])
-            put(grads1, (1,), row, q, total[i][1])
+            put(grads, (1, 0), row, q, total[i][0])
+            put(grads, (1, 1), row, q, total[i][1])
     prop_products(op, mid, out, table, 1, modes)
     half = modes // 2
     for k in range(CHUNKS):
@@ -320,15 +320,15 @@
                 put(terms, (m % half, 0), row, q, term[0])
                 put(terms, (m % half, 1), row, q, term[1])
         for i, q in enumerate(QUADS):
-            put(grads0, (0,), row, q, total[i][0])
-            put(grads0, (1,), row, q, total[i][1])
+            put(grads, (0, 0), row, q, total[i][0])
+            put(grads, (0, 1), row, q, total[i][1])
     for terms in (send, keep):
         for m in range(half):
             for p in range(2):
                 terms[m, p] = mirror(terms[m, p])
-    for p in range(2):
-        grads1[p] = wrapped(place, grads1[p])
-        grads0[p] = wrapped(place, grads0[p])
+    for s in range(2):
+        for p in range(2):
+            grads[s, p] = wrapped(place, grads[s, p])
 
 
 def call(kernel, args, shapes, scratch, flops, mib):
@@ -370,7 +370,7 @@
     return call(
         second_kernel,
         (place, mine, other, q1, amplitude, table, phases, probes, first_obj),
-        [field_shape, field_shape, terms_shape, terms_shape],
+        [((2, 2, N, N), F32), terms_shape, terms_shape],
         [field_shape, ((N, N), F32), operand(modes)] + products_scratch(modes),
         9 << 30,
         26,
@@ -464,7 +464,7 @@
     for step in range(1, count):
         part = ring(value, axis, step)
         whole = lax.dynamic_update_index_in_dim(whole, part, (me + count - step) % count, 0)
-    return whole
+    return whole.reshape(-1, N)
 
 
 def exchange(value, bits):
@@ -478,11 +478,24 @@
     return value + exchange(value, 4)
 
 
+COPIES = 8
+
+
 def place_kernel(index, source, *refs):
-    target, semaphore = refs[-2:]
-    copy = pltpu.make_async_copy(source, target.at[index[0]], semaphore)
-    copy.start()
-    copy.wait()
+    target, semaphores = refs[-2:]
+    rows = source.shape[0] // COPIES
+    copies = [
+        pltpu.make_async_copy(
+            source.at[pl.ds(i * rows, rows)],
+            target.at[index[0], pl.ds(i * rows, rows)],
+            semaphores.at[i],
+        )
+        for i in range(COPIES)
+    ]
+    for copy in copies:
+        copy.start()
+    for copy in copies:
+        copy.wait()
 
 
 def placed(index, value, whole):
@@ -493,7 +506,7 @@
         + [anywhere] * (0 if whole is None else 1),
         out_specs=anywhere,
         out_shape=jax.ShapeDtypeStruct((2,) + value.shape, value.dtype),
-        scratch_shapes=[pltpu.SemaphoreType.DMA],
+        scratch_shapes=[pltpu.SemaphoreType.DMA((COPIES,))],
         input_output_aliases={} if whole is None else {2: 0},
     )(index, value, *([] if whole is None else [whole]))
 
@@ -523,8 +536,9 @@
     place = jnp.stack([yp, xp, odd, live]).astype(jnp.int32)
     flip, table, phases = staged(lax.axis_index("core").astype(jnp.int32).reshape(1), probe_modes)
     right = after(shifted(after(object_field, above), TILE, -1), flip)
-    mixed = jnp.where(col < xq, right, object_field)
-    mine = jnp.where(col < xp, right, object_field)
+    mine, mixed = [
+        [jnp.where(col < x, right[s], object_field[s]) for s in range(2)] for x in (xp, xq)
+    ]
     other = [moved(mixed[s], -1, 1) for s in range(2)]
 
     def split(grads, arrived):
@@ -534,30 +548,27 @@
         staying = jnp.where(col >= xp, kept, 0.0) + jnp.where(col >= xq, taken, 0.0)
         return staying, leaving
 
-    amplitude = moved(after(amplitudes, mixed), 0, 1)
+    amplitude = moved(after(amplitudes, *mixed), 0, 1)
     q1, obj = first(place, mine[0], other[0], flip, table)
-    grads1, grads0, send, keep = second(
+    grads, send, keep = second(
         place, mine[1], other[1], q1, amplitude, table, phases, flip, obj
     )
     swap = [(0, 1), (1, 0)]
-    arrived1 = moved(grads1, 1, -1)
+    arrived = moved(grads, 1, -1)
     across = pieces(keep + lax.ppermute(send, "core", swap), "y")
-    staying1, leaving1 = split(grads1, after(arrived1, *across))
-    received1 = shifted(leaving1, TILE, 1)
-    across[-1] = after(across[-1], leaving1)
-    partial = after(scatter_sum(across, "y"), received1)
-    total = summed_over_z(scatter_sum(pieces(partial, "x"), "x"))
-    grads0 = after(grads0, total)
-    arrived0 = moved(grads0, 1, -1)
-    total = gather(total, "x").reshape(-1, N)
-    staying0, leaving0 = split(grads0, arrived0)
-    received0 = shifted(after(leaving0, total), TILE, 1)
-    total = after(gather(total, "y", leaving0).reshape(-1, N), received0)
+    across = pieces(after(scatter_sum(across, "y"), arrived), "x")
+    staying, leaving = split(grads, arrived)
+    across[-1] = after(across[-1], leaving)
+    total = summed_over_z(scatter_sum(across, "x"))
+    total = gather(total, "x")
+    received = shifted(after(leaving, total), TILE, 1)
+    total = gather(total, "y", received)
+    object_grad = staying + received
+    total = after(total, object_grad)
     core = lax.axis_index("core").astype(jnp.int32).reshape(1)
     whole = placed(core, total, None)
     probe_grad = placed(1 - core, lax.ppermute(total, "core", swap), whole)
     probe_grad = probe_grad.reshape(probe_modes.shape)
-    object_grad = jnp.stack([staying0 + received0, staying1 + received1])
     return (object_grad, probe_grad)
 
 

time: 167 us -> 181 us (1.084)
  the two profiles are of different devices: /device:TPU:1 before, /device:TPU:5 now
where the time goes in v6:
time: 181 us
  starting transfers between devices  81.7 us (45%)
  waiting for transfers between devices  50.5 us (28%)
  Pallas kernels  26.3 us (15%)
  other arithmetic  8.69 us (5%)
  local copies, waits for them, and re-layouts  6.83 us (4%)
  between operations  6.52 us (4%)
    ppermute x1, starting transfers between devices, per_device(): probe_grad = placed(1 - core, lax.ppermute(total, 'core', swap), whole)  29.6 us
    ppermute x12, waiting for transfers between devices, ring(): lax.ppermute(value, axis, [(i, (i + step) % count) for i in range(count)])  22.7 us
    ppermute x4, starting transfers between devices, moved(): return lax.ppermute(value, POS + TILE, pairs)  17.9 us
    ppermute x2, waiting for transfers between devices, shifted(): lax.ppermute(value, axes, [(source, source + steps) for source in range(f...  17.7 us
    pallas_call x2, Pallas kernels, call(): pl.pallas_call(kernel, in_specs=[pl.BlockSpec(memory_space=pltpu.SMEM)] +...  14.6 us
    ppermute x12, starting transfers between devices, ring(): lax.ppermute(value, axis, [(i, (i + step) % count) for i in range(count)])  14.4 us
    ppermute x4, starting transfers between devices, exchange(): return lax.ppermute(value, axes, [(i, i ^ bits) for i in range(count)])  10.7 us
    pallas_call x1, Pallas kernels, staged(): pl.pallas_call(stage_kernel, grid_spec=pltpu.PrefetchScalarGridSpec(num_s...  7.21 us
  transfers between devices with their start and end apart: 25, of which 13 were waited for; matrix products, arithmetic and copies ran while one was open for 3% of the time, Pallas kernels for 8%

profile of v6, /device:TPU:5, one launch (start us, length us, event | category | flops | bytes accessed | tf_op | source)
XLA Modules:
  0.0 180.5 jit_solution(10705365635991817958)
XLA Ops:
  0.6 3.6 %collective-permute-start = (s32[1,2]{1,0:T(1,128)}, s32[1,2]{1,0:T(1,128)S(1)}, u32[]{:S(2)}, u32[]{:S(2)}) collective-permute-start(s32[1,2]{1,0:T(1,128)} %param.9), channel_id=1, source_target_pairs={{0,8},{8,16},{16,24},{24,32},{32,40},{40,48},{48,56},{56,64},{64,7... | collective-permute-start | bytes 32 | tf_op jit(solution)/shard_map/ppermute | solution.py:532
  5.1 3.5 %collective-permute-start.1 = (f32[2,2,256,256]{3,2,1,0:T(8,128)}, f32[2,2,256,256]{3,2,1,0:T(8,128)S(1)}, u32[]{:S(2)}, u32[]{:S(2)}) collective-permute-start(f32[2,2,256,256]{3,2,1,0:T(8,128)} %param.6), channel_id=1, source_target_pairs={{1,0},{2,1},{3,2},{4,3},{5,4},{6,5},{7,6},{9,8},{10,9},{11,10},{12... | collective-permute-start | bytes 3145736 | tf_op jit(solution)/shard_map/ppermute | solution.py:430
  8.6 7.2 %shard_map.77 = (f32[8,256,256]{2,1,0:T(8,128)}, bf16[5,2,256,256]{3,2,1,0:T(8,128)(2,1)}, f32[2,256,256]{2,1,0:T(8,128)}) custom-call(s32[1]{0:T(128)} %bitcast.8.core.index, f32[8,256,256]{2,1,0:T(8,128)} %bitcast.72, bf16[5,2,256,256]{3,2,1,0:T(8,128)(2,1)} %constant.146.clone.table, f32[2,256,256]{2,1,0:T(8,128)} %constant.147.clone.phases), custom_call_target="tpu_custom_call" | custom-call | tf_op jit(solution)/shard_map/pallas_call | solution.py:395
  19.8 6.7 %collective-permute-done.1 = f32[2,2,256,256]{3,2,1,0:T(8,128)S(1)} collective-permute-done((f32[2,2,256,256]{3,2,1,0:T(8,128)}, f32[2,2,256,256]{3,2,1,0:T(8,128)S(1)}, u32[]{:S(2)}, u32[]{:S(2)}) %collective-permute-start.1) | collective-permute-done | bytes 1048608 | tf_op jit(solution)/shard_map/ppermute | solution.py:430
  27.4 2.6 %bitcast_select_fusion = (f32[2,256,256]{2,1,0:T(8,128)S(1)}, f32[2,256,256]{2,1,0:T(8,128)}, f32[2,256,256]{2,1,0:T(8,128)S(1)}, f32[2,256,256]{2,1,0:T(8,128)S(1)}) fusion(f32[2,2,256,256]{3,2,1,0:T(8,128)} %param.6, f32[2,2,256,256]{3,2,1,0:T(8,128)} %copy-done.7, pred[256]{0:T(512)(128)(4,1)S(1)} %get-tuple-element.55, pred[256]{0:T(512)(128)(4,1)S(1)} %get-tuple-element.56), kind=kLoop, calls=%fused_computation.2 | loop fusion | flops 524288 | bytes 4194816 | tf_op jit(solution)/shard_map/jit(_where)/select_n | solution.py:540
  30.1 8.4 %collective-permute-start.3 = (f32[2,256,256]{2,1,0:T(8,128)S(1)}, f32[2,256,256]{2,1,0:T(8,128)}, u32[]{:S(2)}, u32[]{:S(2)}) collective-permute-start(f32[2,256,256]{2,1,0:T(8,128)S(1)} %get-tuple-element.36), channel_id=1, source_target_pairs={{1,9},{3,11},{5,13},{7,15},{8,0},{9,17},{10,2},{11,19},{12,4},{13,... | collective-permute-start | bytes 1572872 | tf_op jit(solution)/shard_map/ppermute | solution.py:523
  43.5 5.0 %collective-permute-done.3.other = f32[2,256,256]{2,1,0:T(8,128)} collective-permute-done((f32[2,256,256]{2,1,0:T(8,128)S(1)}, f32[2,256,256]{2,1,0:T(8,128)}, u32[]{:S(2)}, u32[]{:S(2)}) %collective-permute-start.3) | collective-permute-done | bytes 524320 | tf_op jit(solution)/shard_map/ppermute | solution.py:523
  50.1 4.1 %shard_map.78 = (f32[4,2,256,256]{3,2,1,0:T(8,128)S(1)}, f32[2,256,256]{2,1,0:T(8,128)S(1)}) custom-call(s32[4]{0:T(128)S(1)} %pad_add_fusion.place, f32[2,256,256]{2,1,0:T(8,128)S(1)} %get-tuple-element.41.mine, f32[2,256,256]{2,1,0:T(8,128)} %collective-permute-done.3.other, f32[4,2,256,256]{3,2,1,0:T(8,128)S(1)} %bitcast.65, ...), custom_call_target="tpu_custom_call" | custom-call | flops 3221225472 | bytes 4194304 | tf_op jit(solution)/shard_map/pallas_call | solution.py:336
  54.2 10.5 %shard_map.79 = (f32[2,2,256,256]{3,2,1,0:T(8,128)S(1)}, f32[2,2,256,256]{3,2,1,0:T(8,128)}, f32[2,2,256,256]{3,2,1,0:T(8,128)S(1)}) custom-call(s32[4]{0:T(128)S(1)} %pad_add_fusion.place, f32[2,256,256]{2,1,0:T(8,128)S(1)} %get-tuple-element.40.mine, f32[2,256,256]{2,1,0:T(8,128)S(1)} %collective-permute-done.2.other, ...), custom_call_target="tpu_custom_call" | custom-call | flops 9663676416 | bytes 4194304 | tf_op jit(solution)/shard_map/pallas_call | solution.py:336
  64.7 6.0 %collective-permute-start.5 = (f32[2,2,256,256]{3,2,1,0:T(8,128)S(1)}, f32[2,2,256,256]{3,2,1,0:T(8,128)}, u32[]{:S(2)}, u32[]{:S(2)}) collective-permute-start(f32[2,2,256,256]{3,2,1,0:T(8,128)S(1)} %get-tuple-element.26), channel_id=1, source_target_pairs={{0,8},{1,249},{2,10},{3,251},{4,12},{5,253},{6,14},{7,255},{8,16},... | collective-permute-start | bytes 3145736 | tf_op jit(solution)/shard_map/ppermute | solution.py:523
  75.2 2.6 %collective-permute-start.8 = (f32[256,256]{1,0:T(8,128)S(1)}, f32[256,256]{1,0:T(8,128)S(1)}, u32[]{:S(2)}, u32[]{:S(2)}) collective-permute-start(f32[256,256]{1,0:T(8,128)S(1)} %get-tuple-element.44), channel_id=1, source_target_pairs={{0,128},{64,192},{128,0},{192,64},{1,129},{65,193},{129,1},{193,65... | collective-permute-start | bytes 786440 | tf_op jit(solution)/shard_map/ppermute | solution.py:439
  80.3 8.6 %collective-permute-done.7 = f32[256,256]{1,0:T(8,128)S(1)} collective-permute-done((f32[256,256]{1,0:T(8,128)}, f32[256,256]{1,0:T(8,128)S(1)}, u32[]{:S(2)}, u32[]{:S(2)}) %collective-permute-start.7) | collective-permute-done | bytes 262176 | tf_op jit(solution)/shard_map/ppermute | solution.py:439
  88.8 8.7 %collective-permute-done.8 = f32[256,256]{1,0:T(8,128)S(1)} collective-permute-done((f32[256,256]{1,0:T(8,128)S(1)}, f32[256,256]{1,0:T(8,128)S(1)}, u32[]{:S(2)}, u32[]{:S(2)}) %collective-permute-start.8) | collective-permute-done | bytes 262176 | tf_op jit(solution)/shard_map/ppermute | solution.py:439
  103.8 3.4 %collective-permute-start.15 = (f32[64,256]{1,0:T(8,128)S(1)}, f32[64,256]{1,0:T(8,128)S(1)}, u32[]{:S(2)}, u32[]{:S(2)}) collective-permute-start(f32[64,256]{1,0:T(8,128)S(1)} %add_add_fusion.2), channel_id=1, source_target_pairs={{0,17},{1,16},{16,1},{17,0},{32,49},{33,48},{48,33},{49,32},{2,19}... | collective-permute-start | bytes 196616 | tf_op jit(solution)/shard_map/ppermute | solution.py:473
  107.8 2.0 %collective-permute-done.15 = f32[64,256]{1,0:T(8,128)S(1)} collective-permute-done((f32[64,256]{1,0:T(8,128)S(1)}, f32[64,256]{1,0:T(8,128)S(1)}, u32[]{:S(2)}, u32[]{:S(2)}) %collective-permute-start.15) | collective-permute-done | bytes 65568 | tf_op jit(solution)/shard_map/ppermute | solution.py:473
  109.8 7.1 %collective-permute-start.16 = (f32[64,256]{1,0:T(8,128)S(1)}, f32[64,256]{1,0:T(8,128)S(1)}, u32[]{:S(2)}, u32[]{:S(2)}) collective-permute-start(f32[64,256]{1,0:T(8,128)S(1)} %add_add_fusion.1), channel_id=1, source_target_pairs={{0,32},{1,33},{16,48},{17,49},{32,0},{33,1},{48,16},{49,17},{2,34}... | collective-permute-start | bytes 196616 | tf_op jit(solution)/shard_map/ppermute | solution.py:473
  118.6 2.1 %collective-permute-start.17 = (f32[64,256]{1,0:T(8,128)S(1)}, f32[64,256]{1,0:T(8,128)S(1)}, u32[]{:S(2)}, u32[]{:S(2)}) collective-permute-start(f32[64,256]{1,0:T(8,128)S(1)} %get-tuple-element.35), channel_id=1, source_target_pairs={{0,2},{2,4},{4,6},{6,0},{1,3},{3,5},{5,7},{7,1},{8,10},{10,12},{12... | collective-permute-start | bytes 196616 | tf_op jit(solution)/shard_map/ppermute | solution.py:439
  122.1 3.2 %collective-permute-done.18 = f32[64,256]{1,0:T(8,128)S(1)} collective-permute-done((f32[64,256]{1,0:T(8,128)S(1)}, f32[64,256]{1,0:T(8,128)S(1)}, u32[]{:S(2)}, u32[]{:S(2)}) %collective-permute-start.18) | collective-permute-done | bytes 65568 | tf_op jit(solution)/shard_map/ppermute | solution.py:439
  127.5 3.5 %collective-permute-start.22 = (f32[256,256]{1,0:T(8,128)S(1)}, f32[256,256]{1,0:T(8,128)S(1)}, u32[]{:S(2)}, u32[]{:S(2)}) collective-permute-start(f32[256,256]{1,0:T(8,128)S(1)} %bitcast.75), channel_id=1, source_target_pairs={{0,128},{64,192},{128,0},{192,64},{1,129},{65,193},{129,1},{193,65... | collective-permute-start | bytes 786440 | tf_op jit(solution)/shard_map/ppermute | solution.py:439
  131.1 11.1 %collective-permute-done.20 = f32[2,2,256,256]{3,2,1,0:T(8,128)S(1)} collective-permute-done((f32[2,2,256,256]{3,2,1,0:T(8,128)S(1)}, f32[2,2,256,256]{3,2,1,0:T(8,128)S(1)}, u32[]{:S(2)}, u32[]{:S(2)}) %collective-permute-start.20) | collective-permute-done | bytes 1048608 | tf_op jit(solution)/shard_map/ppermute | solution.py:430
  142.3 2.9 %add_add_fusion = f32[2,2,256,256]{3,2,1,0:T(8,128)} fusion(f32[2,2,256,256]{3,2,1,0:T(8,128)S(1)} %collective-permute-done.20, f32[2,2,256,256]{3,2,1,0:T(8,128)} %collective-permute-done.5, f32[2,2,256,256]{3,2,1,0:T(8,128)S(1)} %get-tuple-element.26, pred[256]{0:T(512)(128)(4,1)S(1)} %get-tuple-element.53, pred[256]{0:T(512)(128)(4,1)S(1)} %get-tuple-element.54, ...), kind=kLoop, calls=%fused_computation.1 | loop fusion | flops 1572864 | bytes 4195328 | tf_op jit(solution)/shard_map/add | solution.py:566
  145.2 29.6 %collective-permute-start.24 = (f32[1024,256]{1,0:T(8,128)S(1)}, f32[1024,256]{1,0:T(8,128)S(1)}, u32[]{:S(2)}, u32[]{:S(2)}) collective-permute-start(f32[1024,256]{1,0:T(8,128)S(1)} %bitcast.70), channel_id=1, source_target_pairs={{0,8},{8,0},{1,9},{9,1},{2,10},{10,2},{3,11},{11,3},{4,12},{12,4},... | collective-permute-start | bytes 3145736 | tf_op jit(solution)/shard_map/ppermute | solution.py:570
  174.8 2.2 %shard_map.80.refs_0_ = f32[2,1024,256]{2,1,0:T(8,128)} custom-call(s32[1]{0:T(128)} %bitcast.8.core.index, f32[1024,256]{1,0:T(8,128)} %bitcast.71), custom_call_target="tpu_custom_call" | custom-call | tf_op jit(solution)/shard_map/pallas_call | solution.py:503
  178.1 2.2 %shard_map.81 = f32[2,1024,256]{2,1,0:T(8,128)} custom-call(s32[1]{0:T(128)S(6)} %sub.2.index, f32[1024,256]{1,0:T(8,128)} %copy-done.8, f32[2,1024,256]{2,1,0:T(8,128)} %shard_map.80.refs_0_), custom_call_target="tpu_custom_call", output_to_operand_aliasing={{}: (2, {})} | custom-call | tf_op jit(solution)/shard_map/pallas_call | solution.py:503
  (76 shorter events, 27.0 us)
Async XLA Ops:
  0.6 4.5 %collective-permute-start = (s32[1,2]{1,0:T(1,128)}, s32[1,2]{1,0:T(1,128)S(1)}, u32[]{:S(2)}, u32[]{:S(2)}) collective-permute-start(s32[1,2]{1,0:T(1,128)} %param.9), channel_id=1, source_target_pairs={{0,8},{8,16},{16,24},{24,32},{32,40},{40,48},{48,56},{56,64},{64,7... | collective-permute-start | bytes 32 | tf_op jit(solution)/shard_map/ppermute | solution.py:532
  5.1 21.3 %collective-permute-start.1 = (f32[2,2,256,256]{3,2,1,0:T(8,128)}, f32[2,2,256,256]{3,2,1,0:T(8,128)S(1)}, u32[]{:S(2)}, u32[]{:S(2)}) collective-permute-start(f32[2,2,256,256]{3,2,1,0:T(8,128)} %param.6), channel_id=1, source_target_pairs={{1,0},{2,1},{3,2},{4,3},{5,4},{6,5},{7,6},{9,8},{10,9},{11,10},{12... | collective-permute-start | bytes 3145736 | tf_op jit(solution)/shard_map/ppermute | solution.py:430
  30.1 18.4 %collective-permute-start.3 = (f32[2,256,256]{2,1,0:T(8,128)S(1)}, f32[2,256,256]{2,1,0:T(8,128)}, u32[]{:S(2)}, u32[]{:S(2)}) collective-permute-start(f32[2,256,256]{2,1,0:T(8,128)S(1)} %get-tuple-element.36), channel_id=1, source_target_pairs={{1,9},{3,11},{5,13},{7,15},{8,0},{9,17},{10,2},{11,19},{12,4},{13,... | collective-permute-start | bytes 1572872 | tf_op jit(solution)/shard_map/ppermute | solution.py:523
  38.5 15.7 %collective-permute-start.2 = (f32[2,256,256]{2,1,0:T(8,128)}, f32[2,256,256]{2,1,0:T(8,128)S(1)}, u32[]{:S(2)}, u32[]{:S(2)}) collective-permute-start(f32[2,256,256]{2,1,0:T(8,128)} %get-tuple-element.37), channel_id=1, source_target_pairs={{1,9},{3,11},{5,13},{7,15},{8,0},{9,17},{10,2},{11,19},{12,4},{13,... | collective-permute-start | bytes 1572872 | tf_op jit(solution)/shard_map/ppermute | solution.py:523
  41.9 12.3 %collective-permute-start.4 = (f32[1,256,256]{2,1,0:T(8,128)}, f32[1,256,256]{2,1,0:T(8,128)S(1)}, u32[]{:S(2)}, u32[]{:S(2)}) collective-permute-start(f32[1,256,256]{2,1,0:T(8,128)} %param.8), channel_id=1, source_target_pairs={{0,0},{1,9},{2,2},{3,11},{4,4},{5,13},{6,6},{7,15},{8,8},{9,17},{1... | collective-permute-start | bytes 786440 | tf_op jit(solution)/shard_map/ppermute | solution.py:523
  64.7 6.0 %collective-permute-start.6 = (f32[2,2,256,256]{3,2,1,0:T(8,128)}, f32[2,2,256,256]{3,2,1,0:T(8,128)S(1)}, u32[]{:S(2)}, u32[]{:S(2)}) collective-permute-start(f32[2,2,256,256]{3,2,1,0:T(8,128)} %get-tuple-element.28), channel_id=1, source_target_pairs={{0,8},{8,0},{1,9},{9,1},{2,10},{10,2},{3,11},{11,3},{4,12},{12,4},... | collective-permute-start | bytes 3145736 | tf_op jit(solution)/shard_map/ppermute | solution.py:558
  64.7 32.9 %collective-permute-start.5 = (f32[2,2,256,256]{3,2,1,0:T(8,128)S(1)}, f32[2,2,256,256]{3,2,1,0:T(8,128)}, u32[]{:S(2)}, u32[]{:S(2)}) collective-permute-start(f32[2,2,256,256]{3,2,1,0:T(8,128)S(1)} %get-tuple-element.26), channel_id=1, source_target_pairs={{0,8},{1,249},{2,10},{3,251},{4,12},{5,253},{6,14},{7,255},{8,16},... | collective-permute-start | bytes 3145736 | tf_op jit(solution)/shard_map/ppermute | solution.py:523
  74.0 14.9 %collective-permute-start.7 = (f32[256,256]{1,0:T(8,128)}, f32[256,256]{1,0:T(8,128)S(1)}, u32[]{:S(2)}, u32[]{:S(2)}) collective-permute-start(f32[256,256]{1,0:T(8,128)} %get-tuple-element.42), channel_id=1, source_target_pairs={{0,64},{64,128},{128,192},{192,0},{1,65},{65,129},{129,193},{193,1... | collective-permute-start | bytes 786440 | tf_op jit(solution)/shard_map/ppermute | solution.py:439
  75.2 22.3 %collective-permute-start.8 = (f32[256,256]{1,0:T(8,128)S(1)}, f32[256,256]{1,0:T(8,128)S(1)}, u32[]{:S(2)}, u32[]{:S(2)}) collective-permute-start(f32[256,256]{1,0:T(8,128)S(1)} %get-tuple-element.44), channel_id=1, source_target_pairs={{0,128},{64,192},{128,0},{192,64},{1,129},{65,193},{129,1},{193,65... | collective-permute-start | bytes 786440 | tf_op jit(solution)/shard_map/ppermute | solution.py:439
  77.9 19.7 %collective-permute-start.9 = (f32[256,256]{1,0:T(8,128)S(1)}, f32[256,256]{1,0:T(8,128)S(1)}, u32[]{:S(2)}, u32[]{:S(2)}) collective-permute-start(f32[256,256]{1,0:T(8,128)S(1)} %get-tuple-element.43), channel_id=1, source_target_pairs={{0,192},{64,0},{128,64},{192,128},{1,193},{65,1},{129,65},{193,129... | collective-permute-start | bytes 786440 | tf_op jit(solution)/shard_map/ppermute | solution.py:439
  97.6 3.9 %collective-permute-start.10 = (f32[64,256]{1,0:T(8,128)S(1)}, f32[64,256]{1,0:T(8,128)S(1)}, u32[]{:S(2)}, u32[]{:S(2)}) collective-permute-start(f32[64,256]{1,0:T(8,128)S(1)} %get-tuple-element.45), channel_id=1, source_target_pairs={{0,2},{2,4},{4,6},{6,0},{1,3},{3,5},{5,7},{7,1},{8,10},{10,12},{12... | collective-permute-start | bytes 196616 | tf_op jit(solution)/shard_map/ppermute | solution.py:439
  98.6 4.6 %collective-permute-start.11 = (f32[64,256]{1,0:T(8,128)S(1)}, f32[64,256]{1,0:T(8,128)S(1)}, u32[]{:S(2)}, u32[]{:S(2)}) collective-permute-start(f32[64,256]{1,0:T(8,128)S(1)} %get-tuple-element.47), channel_id=1, source_target_pairs={{0,4},{2,6},{4,0},{6,2},{1,5},{3,7},{5,1},{7,3},{8,12},{10,14},{12... | collective-permute-start | bytes 196616 | tf_op jit(solution)/shard_map/ppermute | solution.py:439
  99.2 4.4 %collective-permute-start.12 = (f32[64,256]{1,0:T(8,128)S(1)}, f32[64,256]{1,0:T(8,128)S(1)}, u32[]{:S(2)}, u32[]{:S(2)}) collective-permute-start(f32[64,256]{1,0:T(8,128)S(1)} %get-tuple-element.46), channel_id=1, source_target_pairs={{0,6},{2,0},{4,2},{6,4},{1,7},{3,1},{5,3},{7,5},{8,14},{10,8},{12,... | collective-permute-start | bytes 196616 | tf_op jit(solution)/shard_map/ppermute | solution.py:439
  103.6 3.6 %collective-permute-start.13 = (f32[64,256]{1,0:T(8,128)S(1)}, f32[64,256]{1,0:T(8,128)S(1)}, u32[]{:S(2)}, u32[]{:S(2)}) collective-permute-start(f32[64,256]{1,0:T(8,128)S(1)} %add_add_fusion.2), channel_id=1, source_target_pairs={{0,1},{1,0},{16,17},{17,16},{32,33},{33,32},{48,49},{49,48},{2,3},... | collective-permute-start | bytes 196616 | tf_op jit(solution)/shard_map/ppermute | solution.py:473
  103.7 4.1 %collective-permute-start.14 = (f32[64,256]{1,0:T(8,128)S(1)}, f32[64,256]{1,0:T(8,128)S(1)}, u32[]{:S(2)}, u32[]{:S(2)}) collective-permute-start(f32[64,256]{1,0:T(8,128)S(1)} %add_add_fusion.2), channel_id=1, source_target_pairs={{0,16},{1,17},{16,0},{17,1},{32,48},{33,49},{48,32},{49,33},{2,18}... | collective-permute-start | bytes 196616 | tf_op jit(solution)/shard_map/ppermute | solution.py:473
  103.8 6.0 %collective-permute-start.15 = (f32[64,256]{1,0:T(8,128)S(1)}, f32[64,256]{1,0:T(8,128)S(1)}, u32[]{:S(2)}, u32[]{:S(2)}) collective-permute-start(f32[64,256]{1,0:T(8,128)S(1)} %add_add_fusion.2), channel_id=1, source_target_pairs={{0,17},{1,16},{16,1},{17,0},{32,49},{33,48},{48,33},{49,32},{2,19}... | collective-permute-start | bytes 196616 | tf_op jit(solution)/shard_map/ppermute | solution.py:473
  109.8 8.8 %collective-permute-start.16 = (f32[64,256]{1,0:T(8,128)S(1)}, f32[64,256]{1,0:T(8,128)S(1)}, u32[]{:S(2)}, u32[]{:S(2)}) collective-permute-start(f32[64,256]{1,0:T(8,128)S(1)} %add_add_fusion.1), channel_id=1, source_target_pairs={{0,32},{1,33},{16,48},{17,49},{32,0},{33,1},{48,16},{49,17},{2,34}... | collective-permute-start | bytes 196616 | tf_op jit(solution)/shard_map/ppermute | solution.py:473
  120.8 4.6 %collective-permute-start.18 = (f32[64,256]{1,0:T(8,128)S(1)}, f32[64,256]{1,0:T(8,128)S(1)}, u32[]{:S(2)}, u32[]{:S(2)}) collective-permute-start(f32[64,256]{1,0:T(8,128)S(1)} %get-tuple-element.35), channel_id=1, source_target_pairs={{0,4},{2,6},{4,0},{6,2},{1,5},{3,7},{5,1},{7,3},{8,12},{10,14},{12... | collective-permute-start | bytes 196616 | tf_op jit(solution)/shard_map/ppermute | solution.py:439
  120.8 4.6 %collective-permute-start.19 = (f32[64,256]{1,0:T(8,128)S(1)}, f32[64,256]{1,0:T(8,128)S(1)}, u32[]{:S(2)}, u32[]{:S(2)}) collective-permute-start(f32[64,256]{1,0:T(8,128)S(1)} %get-tuple-element.35), channel_id=1, source_target_pairs={{0,6},{2,0},{4,2},{6,4},{1,7},{3,1},{5,3},{7,5},{8,14},{10,8},{12,... | collective-permute-start | bytes 196616 | tf_op jit(solution)/shard_map/ppermute | solution.py:439
  125.4 16.7 %collective-permute-start.20 = (f32[2,2,256,256]{3,2,1,0:T(8,128)S(1)}, f32[2,2,256,256]{3,2,1,0:T(8,128)S(1)}, u32[]{:S(2)}, u32[]{:S(2)}) collective-permute-start(f32[2,2,256,256]{3,2,1,0:T(8,128)S(1)} %select_add_fusion), channel_id=1, source_target_pairs={{0,1},{1,2},{2,3},{3,4},{4,5},{5,6},{6,7},{8,9},{9,10},{10,11},{11... | collective-permute-start | bytes 3145736 | tf_op jit(solution)/shard_map/ppermute | solution.py:430
  127.3 14.8 %collective-permute-start.21 = (f32[256,256]{1,0:T(8,128)S(1)}, f32[256,256]{1,0:T(8,128)S(1)}, u32[]{:S(2)}, u32[]{:S(2)}) collective-permute-start(f32[256,256]{1,0:T(8,128)S(1)} %bitcast.74), channel_id=1, source_target_pairs={{0,64},{64,128},{128,192},{192,0},{1,65},{65,129},{129,193},{193,1... | collective-permute-start | bytes 786440 | tf_op jit(solution)/shard_map/ppermute | solution.py:439
  127.5 14.7 %collective-permute-start.22 = (f32[256,256]{1,0:T(8,128)S(1)}, f32[256,256]{1,0:T(8,128)S(1)}, u32[]{:S(2)}, u32[]{:S(2)}) collective-permute-start(f32[256,256]{1,0:T(8,128)S(1)} %bitcast.75), channel_id=1, source_target_pairs={{0,128},{64,192},{128,0},{192,64},{1,129},{65,193},{129,1},{193,65... | collective-permute-start | bytes 786440 | tf_op jit(solution)/shard_map/ppermute | solution.py:439
  131.0 11.3 %collective-permute-start.23 = (f32[256,256]{1,0:T(8,128)S(1)}, f32[256,256]{1,0:T(8,128)S(1)}, u32[]{:S(2)}, u32[]{:S(2)}) collective-permute-start(f32[256,256]{1,0:T(8,128)S(1)} %bitcast.76), channel_id=1, source_target_pairs={{0,192},{64,0},{128,64},{192,128},{1,193},{65,1},{129,65},{193,129... | collective-permute-start | bytes 786440 | tf_op jit(solution)/shard_map/ppermute | solution.py:439
  145.2 31.9 %collective-permute-start.24 = (f32[1024,256]{1,0:T(8,128)S(1)}, f32[1024,256]{1,0:T(8,128)S(1)}, u32[]{:S(2)}, u32[]{:S(2)}) collective-permute-start(f32[1024,256]{1,0:T(8,128)S(1)} %bitcast.70), channel_id=1, source_target_pairs={{0,8},{8,0},{1,9},{9,1},{2,10},{10,2},{3,11},{11,3},{4,12},{12,4},... | collective-permute-start | bytes 3145736 | tf_op jit(solution)/shard_map/ppermute | solution.py:570
  (11 other events, 59.6 us)

commit v7 on v5

--- a/solution.py
+++ b/solution.py
@@ -457,14 +457,25 @@
     return lax.optimization_barrier((value,) + others)[0]
 
 
-def gather(value, axis, *beside):
+def collected(value, travelled, axis, *beside):
     count, me = lax.axis_size(axis), lax.axis_index(axis)
     whole = jnp.zeros((count,) + value.shape, value.dtype)
     whole = after(lax.dynamic_update_index_in_dim(whole, value, me, 0), *beside)
-    for step in range(1, count):
-        part = ring(value, axis, step)
-        whole = lax.dynamic_update_index_in_dim(whole, part, (me + count - step) % count, 0)
-    return whole
+    for step, part in enumerate(travelled):
+        whole = lax.dynamic_update_index_in_dim(whole, part, (me + step + 1) % count, 0)
+    return whole.reshape(-1, N)
+
+
+def gather(value, axis, *beside):
+    steps = range(1, lax.axis_size(axis))
+    return collected(value, [ring(value, axis, -step) for step in steps], axis, *beside)
+
+
+def circular_gather(value, axis):
+    travelled = [ring(value, axis, -1)]
+    for _ in range(2, lax.axis_size(axis)):
+        travelled.append(ring(travelled[-1], axis, -1))
+    return collected(value, travelled, axis)
 
 
 def exchange(value, bits):
@@ -476,26 +487,6 @@
 def summed_over_z(value):
     value = (value + exchange(value, 1)) + (exchange(value, 2) + exchange(value, 3))
     return value + exchange(value, 4)
-
-
-def place_kernel(index, source, *refs):
-    target, semaphore = refs[-2:]
-    copy = pltpu.make_async_copy(source, target.at[index[0]], semaphore)
-    copy.start()
-    copy.wait()
-
-
-def placed(index, value, whole):
-    anywhere = pl.BlockSpec(memory_space=pl.ANY)
-    return pl.pallas_call(
-        place_kernel,
-        in_specs=[pl.BlockSpec(memory_space=pltpu.SMEM), pl.BlockSpec(memory_space=pltpu.VMEM)]
-        + [anywhere] * (0 if whole is None else 1),
-        out_specs=anywhere,
-        out_shape=jax.ShapeDtypeStruct((2,) + value.shape, value.dtype),
-        scratch_shapes=[pltpu.SemaphoreType.DMA],
-        input_output_aliases={} if whole is None else {2: 0},
-    )(index, value, *([] if whole is None else [whole]))
 
 
 def moved(value, even, odd):
@@ -523,8 +514,9 @@
     place = jnp.stack([yp, xp, odd, live]).astype(jnp.int32)
     flip, table, phases = staged(lax.axis_index("core").astype(jnp.int32).reshape(1), probe_modes)
     right = after(shifted(after(object_field, above), TILE, -1), flip)
-    mixed = jnp.where(col < xq, right, object_field)
-    mine = jnp.where(col < xp, right, object_field)
+    mine, mixed = [
+        [jnp.where(col < x, right[s], object_field[s]) for s in range(2)] for x in (xp, xq)
+    ]
     other = [moved(mixed[s], -1, 1) for s in range(2)]
 
     def split(grads, arrived):
@@ -534,7 +526,7 @@
         staying = jnp.where(col >= xp, kept, 0.0) + jnp.where(col >= xq, taken, 0.0)
         return staying, leaving
 
-    amplitude = moved(after(amplitudes, mixed), 0, 1)
+    amplitude = moved(after(amplitudes, *mixed), 0, 1)
     q1, obj = first(place, mine[0], other[0], flip, table)
     grads1, grads0, send, keep = second(
         place, mine[1], other[1], q1, amplitude, table, phases, flip, obj
@@ -545,19 +537,19 @@
     staying1, leaving1 = split(grads1, after(arrived1, *across))
     received1 = shifted(leaving1, TILE, 1)
     across[-1] = after(across[-1], leaving1)
-    partial = after(scatter_sum(across, "y"), received1)
-    total = summed_over_z(scatter_sum(pieces(partial, "x"), "x"))
-    grads0 = after(grads0, total)
-    arrived0 = moved(grads0, 1, -1)
-    total = gather(total, "x").reshape(-1, N)
+    across = pieces(after(scatter_sum(across, "y"), received1), "x")
+    arrived0 = moved(after(grads0, received1), 1, -1)
+    partial = scatter_sum(across, "x")
     staying0, leaving0 = split(grads0, arrived0)
+    total = summed_over_z(after(partial, leaving0))
     received0 = shifted(after(leaving0, total), TILE, 1)
-    total = after(gather(total, "y", leaving0).reshape(-1, N), received0)
-    core = lax.axis_index("core").astype(jnp.int32).reshape(1)
-    whole = placed(core, total, None)
-    probe_grad = placed(1 - core, lax.ppermute(total, "core", swap), whole)
+    total = circular_gather(total, "x")
+    object_grad = jnp.stack([staying0 + received0, staying1 + received1])
+    total = gather(total, "y", object_grad)
+    opposite = lax.ppermute(total, "core", swap)
+    half = lax.broadcasted_iota(jnp.int32, (2, 1, 1), 0)
+    probe_grad = jnp.where(half == lax.axis_index("core"), total, opposite)
     probe_grad = probe_grad.reshape(probe_modes.shape)
-    object_grad = jnp.stack([staying0 + received0, staying1 + received1])
     return (object_grad, probe_grad)
 
 

time: 167 us -> 164 us (0.982)
  Pallas kernels: 25.9 us -> 21.6 us
  starting transfers between devices: 73.3 us -> 70.1 us
  waiting for transfers between devices: 48.5 us -> 51.6 us
  other arithmetic: 6.64 us -> 8.93 us
    ppermute x12, waiting for transfers between devices: 22.3 us -> 14.5 us  [ring(): lax.ppermute(value, axis, [(i, (i + step) % count) for i in range(count)])]
    ppermute x1, starting transfers between devices: 1.49 us -> 8.6 us  [per_device(): opposite = lax.ppermute(total, 'core', swap)]
    ppermute x3, waiting for transfers between devices: 9.43 us -> 16.5 us  [shifted(): lax.ppermute(value, axes, [(source, source + steps) for source in range(f...]
    ppermute x5, starting transfers between devices: 25.5 us -> 19.5 us  [moved(): return lax.ppermute(value, POS + TILE, pairs)]
    ppermute x3, starting transfers between devices: 17.3 us -> 11.8 us  [shifted(): lax.ppermute(value, axes, [(source, source + steps) for source in range(f...]
    pallas_call x2 -> x0, Pallas kernels: 4.4 us -> none  [placed(): pl.pallas_call(place_kernel, in_specs=[pl.BlockSpec(memory_space=pltpu.SM...]
    select_n x1 -> x2, other arithmetic: 1.11 us -> 4.57 us  [the longest x1 2.82 us: per_device(): jnp.where(col < x, right[s], object_field[s])]
    unnamed x16 -> x18, local copies, waits for them, and re-layouts: 0.03 us -> 2.41 us
  transfers between devices with their start and end apart: 27 -> 27, of which waited for: 16 -> 18; matrix products, arithmetic and copies ran while one was open for 5% -> 4% of each run, Pallas kernels for 8% -> 7%
where the time goes in v7:
time: 164 us; the launch traced here: 163 us
  starting transfers between devices  70.1 us (43%)
  waiting for transfers between devices  51.6 us (31%)
  Pallas kernels  21.6 us (13%)
  other arithmetic  8.93 us (5%)
  between operations  5.96 us (4%)
  local copies, waits for them, and re-layouts  5.14 us (3%)
    ppermute x5, starting transfers between devices, moved(): return lax.ppermute(value, POS + TILE, pairs)  19.5 us
    ppermute x12, starting transfers between devices, ring(): lax.ppermute(value, axis, [(i, (i + step) % count) for i in range(count)])  17.9 us
    ppermute x3, waiting for transfers between devices, shifted(): lax.ppermute(value, axes, [(source, source + steps) for source in range(f...  16.5 us
    ppermute x12, waiting for transfers between devices, ring(): lax.ppermute(value, axis, [(i, (i + step) % count) for i in range(count)])  14.5 us
    pallas_call x2, Pallas kernels, call(): pl.pallas_call(kernel, in_specs=[pl.BlockSpec(memory_space=pltpu.SMEM)] +...  14.4 us
    ppermute x3, starting transfers between devices, shifted(): lax.ppermute(value, axes, [(source, source + steps) for source in range(f...  11.8 us
    ppermute x5, waiting for transfers between devices, moved(): return lax.ppermute(value, POS + TILE, pairs)  9.08 us
    ppermute x1, starting transfers between devices, per_device(): opposite = lax.ppermute(total, 'core', swap)  8.6 us
  transfers between devices with their start and end apart: 27, of which 18 were waited for; matrix products, arithmetic and copies ran while one was open for 4% of the time, Pallas kernels for 7%

profile of v7, /device:TPU:1, one launch (start us, length us, event | category | flops | bytes accessed | tf_op | source)
XLA Modules:
  0.0 163.3 jit_solution(17104331261815995573)
XLA Ops:
  0.6 4.5 %collective-permute-start = (s32[1,2]{1,0:T(1,128)}, s32[1,2]{1,0:T(1,128)S(1)}, u32[]{:S(2)}, u32[]{:S(2)}) collective-permute-start(s32[1,2]{1,0:T(1,128)} %param.9), channel_id=1, source_target_pairs={{0,8},{8,16},{16,24},{24,32},{32,40},{40,48},{48,56},{56,64},{64,7... | collective-permute-start | bytes 32 | tf_op jit(solution)/shard_map/ppermute | solution.py:510
  7.2 7.2 %shard_map.77 = (f32[8,256,256]{2,1,0:T(8,128)}, bf16[5,2,256,256]{3,2,1,0:T(8,128)(2,1)}, f32[2,256,256]{2,1,0:T(8,128)}) custom-call(s32[1]{0:T(128)} %bitcast.8.core, f32[8,256,256]{2,1,0:T(8,128)} %bitcast.77, bf16[5,2,256,256]{3,2,1,0:T(8,128)(2,1)} %constant.124.clone.table, f32[2,256,256]{2,1,0:T(8,128)} %constant.125.clone.phases), custom_call_target="tpu_custom_call" | custom-call | tf_op jit(solution)/shard_map/pallas_call | solution.py:395
  18.4 9.0 %collective-permute-done.1 = f32[2,2,256,256]{3,2,1,0:T(8,128)} collective-permute-done((f32[2,2,256,256]{3,2,1,0:T(8,128)}, f32[2,2,256,256]{3,2,1,0:T(8,128)}, u32[]{:S(2)}, u32[]{:S(2)}) %collective-permute-start.1) | collective-permute-done | bytes 1048608 | tf_op jit(solution)/shard_map/ppermute | solution.py:430
  27.4 2.8 %bitcast_select_fusion = (f32[2,256,256]{2,1,0:T(8,128)}, f32[2,256,256]{2,1,0:T(8,128)}, f32[2,256,256]{2,1,0:T(8,128)S(1)}, f32[2,256,256]{2,1,0:T(8,128)S(1)}) fusion(f32[2,2,256,256]{3,2,1,0:T(8,128)} %param.6, f32[2,2,256,256]{3,2,1,0:T(8,128)} %collective-permute-done.1, pred[256]{0:T(512)(128)(4,1)S(1)} %get-tuple-element.63, ...), kind=kLoop, calls=%fused_computation.2 | loop fusion | flops 524288 | bytes 4194816 | tf_op jit(solution)/shard_map/jit(_where)/select_n | solution.py:518
  30.2 8.5 %collective-permute-start.3 = (f32[2,256,256]{2,1,0:T(8,128)}, f32[2,256,256]{2,1,0:T(8,128)}, u32[]{:S(2)}, u32[]{:S(2)}) collective-permute-start(f32[2,256,256]{2,1,0:T(8,128)} %get-tuple-element.42), channel_id=1, source_target_pairs={{1,9},{3,11},{5,13},{7,15},{8,0},{9,17},{10,2},{11,19},{12,4},{13,... | collective-permute-start | bytes 1572872 | tf_op jit(solution)/shard_map/ppermute | solution.py:501
  42.5 6.3 %collective-permute-done.3.other = f32[2,256,256]{2,1,0:T(8,128)} collective-permute-done((f32[2,256,256]{2,1,0:T(8,128)}, f32[2,256,256]{2,1,0:T(8,128)}, u32[]{:S(2)}, u32[]{:S(2)}) %collective-permute-start.3) | collective-permute-done | bytes 524320 | tf_op jit(solution)/shard_map/ppermute | solution.py:501
  50.4 4.0 %shard_map.78 = (f32[4,2,256,256]{3,2,1,0:T(8,128)S(1)}, f32[2,256,256]{2,1,0:T(8,128)S(1)}) custom-call(s32[4]{0:T(128)S(1)} %pad_add_fusion.place, f32[2,256,256]{2,1,0:T(8,128)S(1)} %get-tuple-element.47.mine, f32[2,256,256]{2,1,0:T(8,128)} %collective-permute-done.3.other, f32[4,2,256,256]{3,2,1,0:T(8,128)S(1)} %bitcast.70, ...), custom_call_target="tpu_custom_call" | custom-call | flops 3221225472 | bytes 4194304 | tf_op jit(solution)/shard_map/pallas_call | solution.py:336
  54.5 10.3 %shard_map.79 = (f32[2,256,256]{2,1,0:T(8,128)S(1)}, f32[2,256,256]{2,1,0:T(8,128)S(1)}, f32[2,2,256,256]{3,2,1,0:T(8,128)}, f32[2,2,256,256]{3,2,1,0:T(8,128)S(1)}) custom-call(s32[4]{0:T(128)S(1)} %pad_add_fusion.place, f32[2,256,256]{2,1,0:T(8,128)S(1)} %get-tuple-element.46.mine, f32[2,256,256]{2,1,0:T(8,128)S(1)} %collective-permute-done.2.other, ...), custom_call_target="tpu_custom_call" | custom-call | flops 9663676416 | bytes 4194304 | tf_op jit(solution)/shard_map/pallas_call | solution.py:336
  64.9 6.0 %collective-permute-start.5 = (f32[2,256,256]{2,1,0:T(8,128)S(1)}, f32[2,256,256]{2,1,0:T(8,128)S(1)}, u32[]{:S(2)}, u32[]{:S(2)}) collective-permute-start(f32[2,256,256]{2,1,0:T(8,128)S(1)} %get-tuple-element.30), channel_id=1, source_target_pairs={{0,8},{1,249},{2,10},{3,251},{4,12},{5,253},{6,14},{7,255},{8,16},... | collective-permute-start | bytes 1572872 | tf_op jit(solution)/shard_map/ppermute | solution.py:501
  74.2 2.7 %collective-permute-done.5 = f32[2,256,256]{2,1,0:T(8,128)S(1)} collective-permute-done((f32[2,256,256]{2,1,0:T(8,128)S(1)}, f32[2,256,256]{2,1,0:T(8,128)S(1)}, u32[]{:S(2)}, u32[]{:S(2)}) %collective-permute-start.5) | collective-permute-done | bytes 524320 | tf_op jit(solution)/shard_map/ppermute | solution.py:501
  77.1 9.2 %collective-permute-start.7 = (f32[2,256,256]{2,1,0:T(8,128)S(1)}, f32[2,256,256]{2,1,0:T(8,128)S(1)}, u32[]{:S(2)}, u32[]{:S(2)}) collective-permute-start(f32[2,256,256]{2,1,0:T(8,128)S(1)} %select_add_fusion.1), channel_id=1, source_target_pairs={{0,1},{1,2},{2,3},{3,4},{4,5},{5,6},{6,7},{8,9},{9,10},{10,11},{11... | collective-permute-start | bytes 1572872 | tf_op jit(solution)/shard_map/ppermute | solution.py:430
  89.8 7.6 %collective-permute-done.7 = f32[2,256,256]{2,1,0:T(8,128)S(1)} collective-permute-done((f32[2,256,256]{2,1,0:T(8,128)S(1)}, f32[2,256,256]{2,1,0:T(8,128)S(1)}, u32[]{:S(2)}, u32[]{:S(2)}) %collective-permute-start.7) | collective-permute-done | bytes 524320 | tf_op jit(solution)/shard_map/ppermute | solution.py:430
  98.1 2.5 %collective-permute-start.8 = (f32[2,256,256]{2,1,0:T(8,128)S(1)}, f32[2,256,256]{2,1,0:T(8,128)S(1)}, u32[]{:S(2)}, u32[]{:S(2)}) collective-permute-start(f32[2,256,256]{2,1,0:T(8,128)S(1)} %get-tuple-element.34), channel_id=1, source_target_pairs={{0,8},{1,249},{2,10},{3,251},{4,12},{5,253},{6,14},{7,255},{8,16},... | collective-permute-start | bytes 1572872 | tf_op jit(solution)/shard_map/ppermute | solution.py:501
  112.4 2.0 %collective-permute-start.16 = (f32[64,256]{1,0:T(8,128)S(1)}, f32[64,256]{1,0:T(8,128)S(1)}, u32[]{:S(2)}, u32[]{:S(2)}) collective-permute-start(f32[64,256]{1,0:T(8,128)S(1)} %fusion.1), channel_id=1, source_target_pairs={{0,16},{1,17},{16,0},{17,1},{32,48},{33,49},{48,32},{49,33},{2,18}... | collective-permute-start | bytes 196616 | tf_op jit(solution)/shard_map/ppermute | solution.py:484
  116.5 3.1 %collective-permute-done.17 = f32[64,256]{1,0:T(8,128)S(1)} collective-permute-done((f32[64,256]{1,0:T(8,128)S(1)}, f32[64,256]{1,0:T(8,128)S(1)}, u32[]{:S(2)}, u32[]{:S(2)}) %collective-permute-start.17) | collective-permute-done | bytes 65568 | tf_op jit(solution)/shard_map/ppermute | solution.py:484
  119.6 3.7 %collective-permute-start.18 = (f32[64,256]{1,0:T(8,128)S(1)}, f32[64,256]{1,0:T(8,128)S(1)}, u32[]{:S(2)}, u32[]{:S(2)}) collective-permute-start(f32[64,256]{1,0:T(8,128)S(1)} %add_add_fusion.1), channel_id=1, source_target_pairs={{0,32},{1,33},{16,48},{17,49},{32,0},{33,1},{48,16},{49,17},{2,34}... | collective-permute-start | bytes 196616 | tf_op jit(solution)/shard_map/ppermute | solution.py:484
  123.3 3.5 %collective-permute-done.18 = f32[64,256]{1,0:T(8,128)S(1)} collective-permute-done((f32[64,256]{1,0:T(8,128)S(1)}, f32[64,256]{1,0:T(8,128)S(1)}, u32[]{:S(2)}, u32[]{:S(2)}) %collective-permute-start.18) | collective-permute-done | bytes 65568 | tf_op jit(solution)/shard_map/ppermute | solution.py:484
  130.3 2.1 %collective-permute-start.21 = (f32[64,256]{1,0:T(8,128)S(1)}, f32[64,256]{1,0:T(8,128)S(1)}, u32[]{:S(2)}, u32[]{:S(2)}) collective-permute-start(f32[64,256]{1,0:T(8,128)S(1)} %collective-permute-done.20), channel_id=1, source_target_pairs={{0,6},{2,0},{4,2},{6,4},{1,7},{3,1},{5,3},{7,5},{8,14},{10,8},{12,... | collective-permute-start | bytes 196616 | tf_op jit(solution)/shard_map/ppermute | solution.py:439
  133.7 3.0 %collective-permute-start.22 = (f32[64,256]{1,0:T(8,128)S(1)}, f32[64,256]{1,0:T(8,128)S(1)}, u32[]{:S(2)}, u32[]{:S(2)}) collective-permute-start(f32[64,256]{1,0:T(8,128)S(1)} %collective-permute-done.21), channel_id=1, source_target_pairs={{0,6},{2,0},{4,2},{6,4},{1,7},{3,1},{5,3},{7,5},{8,14},{10,8},{12,... | collective-permute-start | bytes 196616 | tf_op jit(solution)/shard_map/ppermute | solution.py:439
  138.0 3.0 %collective-permute-start.23 = (f32[256,256]{1,0:T(8,128)S(1)}, f32[256,256]{1,0:T(8,128)S(1)}, u32[]{:S(2)}, u32[]{:S(2)}) collective-permute-start(f32[256,256]{1,0:T(8,128)S(1)} %bitcast.80), channel_id=1, source_target_pairs={{0,192},{64,0},{128,64},{192,128},{1,193},{65,1},{129,65},{193,129... | collective-permute-start | bytes 786440 | tf_op jit(solution)/shard_map/ppermute | solution.py:439
  143.3 3.8 %collective-permute-done.23 = f32[256,256]{1,0:T(8,128)S(1)} collective-permute-done((f32[256,256]{1,0:T(8,128)S(1)}, f32[256,256]{1,0:T(8,128)S(1)}, u32[]{:S(2)}, u32[]{:S(2)}) %collective-permute-start.23) | collective-permute-done | bytes 262176 | tf_op jit(solution)/shard_map/ppermute | solution.py:439
  147.9 2.5 %collective-permute-done.25 = f32[256,256]{1,0:T(8,128)S(1)} collective-permute-done((f32[256,256]{1,0:T(8,128)S(1)}, f32[256,256]{1,0:T(8,128)S(1)}, u32[]{:S(2)}, u32[]{:S(2)}) %collective-permute-start.25) | collective-permute-done | bytes 262176 | tf_op jit(solution)/shard_map/ppermute | solution.py:439
  150.4 8.6 %collective-permute-start.26 = (f32[1024,256]{1,0:T(8,128)S(1)}, f32[1024,256]{1,0:T(8,128)S(1)}, u32[]{:S(2)}, u32[]{:S(2)}) collective-permute-start(f32[1024,256]{1,0:T(8,128)S(1)} %bitcast.75), channel_id=1, source_target_pairs={{0,8},{8,0},{1,9},{9,1},{2,10},{10,2},{3,11},{11,3},{4,12},{12,4},... | collective-permute-start | bytes 3145736 | tf_op jit(solution)/shard_map/ppermute | solution.py:549
  159.1 2.1 %collective-permute-done.26 = f32[1024,256]{1,0:T(8,128)S(1)} collective-permute-done((f32[1024,256]{1,0:T(8,128)S(1)}, f32[1024,256]{1,0:T(8,128)S(1)}, u32[]{:S(2)}, u32[]{:S(2)}) %collective-permute-start.26) | collective-permute-done | bytes 1048608 | tf_op jit(solution)/shard_map/ppermute | solution.py:549
  (84 shorter events, 39.4 us)
Async XLA Ops:
  0.6 5.3 %collective-permute-start = (s32[1,2]{1,0:T(1,128)}, s32[1,2]{1,0:T(1,128)S(1)}, u32[]{:S(2)}, u32[]{:S(2)}) collective-permute-start(s32[1,2]{1,0:T(1,128)} %param.9), channel_id=1, source_target_pairs={{0,8},{8,16},{16,24},{24,32},{32,40},{40,48},{48,56},{56,64},{64,7... | collective-permute-start | bytes 32 | tf_op jit(solution)/shard_map/ppermute | solution.py:510
  6.0 21.4 %collective-permute-start.1 = (f32[2,2,256,256]{3,2,1,0:T(8,128)}, f32[2,2,256,256]{3,2,1,0:T(8,128)}, u32[]{:S(2)}, u32[]{:S(2)}) collective-permute-start(f32[2,2,256,256]{3,2,1,0:T(8,128)} %param.6), channel_id=1, source_target_pairs={{1,0},{2,1},{3,2},{4,3},{5,4},{6,5},{7,6},{9,8},{10,9},{11,10},{12... | collective-permute-start | bytes 3145736 | tf_op jit(solution)/shard_map/ppermute | solution.py:430
  30.2 18.6 %collective-permute-start.3 = (f32[2,256,256]{2,1,0:T(8,128)}, f32[2,256,256]{2,1,0:T(8,128)}, u32[]{:S(2)}, u32[]{:S(2)}) collective-permute-start(f32[2,256,256]{2,1,0:T(8,128)} %get-tuple-element.42), channel_id=1, source_target_pairs={{1,9},{3,11},{5,13},{7,15},{8,0},{9,17},{10,2},{11,19},{12,4},{13,... | collective-permute-start | bytes 1572872 | tf_op jit(solution)/shard_map/ppermute | solution.py:501
  38.6 15.8 %collective-permute-start.2 = (f32[2,256,256]{2,1,0:T(8,128)}, f32[2,256,256]{2,1,0:T(8,128)S(1)}, u32[]{:S(2)}, u32[]{:S(2)}) collective-permute-start(f32[2,256,256]{2,1,0:T(8,128)} %get-tuple-element.43), channel_id=1, source_target_pairs={{1,9},{3,11},{5,13},{7,15},{8,0},{9,17},{10,2},{11,19},{12,4},{13,... | collective-permute-start | bytes 1572872 | tf_op jit(solution)/shard_map/ppermute | solution.py:501
  41.8 12.7 %collective-permute-start.4 = (f32[1,256,256]{2,1,0:T(8,128)S(1)}, f32[1,256,256]{2,1,0:T(8,128)S(1)}, u32[]{:S(2)}, u32[]{:S(2)}) collective-permute-start(f32[1,256,256]{2,1,0:T(8,128)S(1)} %copy-done.8), channel_id=1, source_target_pairs={{0,0},{1,9},{2,2},{3,11},{4,4},{5,13},{6,6},{7,15},{8,8},{9,17},{1... | collective-permute-start | bytes 786440 | tf_op jit(solution)/shard_map/ppermute | solution.py:501
  64.9 7.2 %collective-permute-start.6 = (f32[2,2,256,256]{3,2,1,0:T(8,128)}, f32[2,2,256,256]{3,2,1,0:T(8,128)}, u32[]{:S(2)}, u32[]{:S(2)}) collective-permute-start(f32[2,2,256,256]{3,2,1,0:T(8,128)} %get-tuple-element.32), channel_id=1, source_target_pairs={{0,8},{8,0},{1,9},{9,1},{2,10},{10,2},{3,11},{11,3},{4,12},{12,4},... | collective-permute-start | bytes 3145736 | tf_op jit(solution)/shard_map/ppermute | solution.py:536
  64.9 12.1 %collective-permute-start.5 = (f32[2,256,256]{2,1,0:T(8,128)S(1)}, f32[2,256,256]{2,1,0:T(8,128)S(1)}, u32[]{:S(2)}, u32[]{:S(2)}) collective-permute-start(f32[2,256,256]{2,1,0:T(8,128)S(1)} %get-tuple-element.30), channel_id=1, source_target_pairs={{0,8},{1,249},{2,10},{3,251},{4,12},{5,253},{6,14},{7,255},{8,16},... | collective-permute-start | bytes 1572872 | tf_op jit(solution)/shard_map/ppermute | solution.py:501
  77.1 20.2 %collective-permute-start.7 = (f32[2,256,256]{2,1,0:T(8,128)S(1)}, f32[2,256,256]{2,1,0:T(8,128)S(1)}, u32[]{:S(2)}, u32[]{:S(2)}) collective-permute-start(f32[2,256,256]{2,1,0:T(8,128)S(1)} %select_add_fusion.1), channel_id=1, source_target_pairs={{0,1},{1,2},{2,3},{3,4},{4,5},{5,6},{6,7},{8,9},{9,10},{10,11},{11... | collective-permute-start | bytes 1572872 | tf_op jit(solution)/shard_map/ppermute | solution.py:430
  86.3 14.3 %collective-permute-start.10 = (f32[256,256]{1,0:T(8,128)}, f32[256,256]{1,0:T(8,128)}, u32[]{:S(2)}, u32[]{:S(2)}) collective-permute-start(f32[256,256]{1,0:T(8,128)} %get-tuple-element.50), channel_id=1, source_target_pairs={{0,128},{64,192},{128,0},{192,64},{1,129},{65,193},{129,1},{193,65... | collective-permute-start | bytes 786440 | tf_op jit(solution)/shard_map/ppermute | solution.py:439
  88.3 12.4 %collective-permute-start.11 = (f32[256,256]{1,0:T(8,128)S(1)}, f32[256,256]{1,0:T(8,128)}, u32[]{:S(2)}, u32[]{:S(2)}) collective-permute-start(f32[256,256]{1,0:T(8,128)S(1)} %get-tuple-element.49), channel_id=1, source_target_pairs={{0,192},{64,0},{128,64},{192,128},{1,193},{65,1},{129,65},{193,129... | collective-permute-start | bytes 786440 | tf_op jit(solution)/shard_map/ppermute | solution.py:439
  89.1 12.8 %collective-permute-start.9 = (f32[256,256]{1,0:T(8,128)S(1)}, f32[256,256]{1,0:T(8,128)}, u32[]{:S(2)}, u32[]{:S(2)}) collective-permute-start(f32[256,256]{1,0:T(8,128)S(1)} %get-tuple-element.51), channel_id=1, source_target_pairs={{0,64},{64,128},{128,192},{192,0},{1,65},{65,129},{129,193},{193,1... | collective-permute-start | bytes 786440 | tf_op jit(solution)/shard_map/ppermute | solution.py:439
  98.1 12.1 %collective-permute-start.8 = (f32[2,256,256]{2,1,0:T(8,128)S(1)}, f32[2,256,256]{2,1,0:T(8,128)S(1)}, u32[]{:S(2)}, u32[]{:S(2)}) collective-permute-start(f32[2,256,256]{2,1,0:T(8,128)S(1)} %get-tuple-element.34), channel_id=1, source_target_pairs={{0,8},{1,249},{2,10},{3,251},{4,12},{5,253},{6,14},{7,255},{8,16},... | collective-permute-start | bytes 1572872 | tf_op jit(solution)/shard_map/ppermute | solution.py:501
  103.1 4.9 %collective-permute-start.12 = (f32[64,256]{1,0:T(8,128)S(1)}, f32[64,256]{1,0:T(8,128)S(1)}, u32[]{:S(2)}, u32[]{:S(2)}) collective-permute-start(f32[64,256]{1,0:T(8,128)S(1)} %get-tuple-element.52), channel_id=1, source_target_pairs={{0,2},{2,4},{4,6},{6,0},{1,3},{3,5},{5,7},{7,1},{8,10},{10,12},{12... | collective-permute-start | bytes 196616 | tf_op jit(solution)/shard_map/ppermute | solution.py:439
  104.3 4.9 %collective-permute-start.13 = (f32[64,256]{1,0:T(8,128)S(1)}, f32[64,256]{1,0:T(8,128)S(1)}, u32[]{:S(2)}, u32[]{:S(2)}) collective-permute-start(f32[64,256]{1,0:T(8,128)S(1)} %get-tuple-element.54), channel_id=1, source_target_pairs={{0,4},{2,6},{4,0},{6,2},{1,5},{3,7},{5,1},{7,3},{8,12},{10,14},{12... | collective-permute-start | bytes 196616 | tf_op jit(solution)/shard_map/ppermute | solution.py:439
  110.4 4.2 %collective-permute-start.15 = (f32[64,256]{1,0:T(8,128)S(1)}, f32[64,256]{1,0:T(8,128)S(1)}, u32[]{:S(2)}, u32[]{:S(2)}) collective-permute-start(f32[64,256]{1,0:T(8,128)S(1)} %fusion.1), channel_id=1, source_target_pairs={{0,1},{1,0},{16,17},{17,16},{32,33},{33,32},{48,49},{49,48},{2,3},... | collective-permute-start | bytes 196616 | tf_op jit(solution)/shard_map/ppermute | solution.py:484
  112.4 4.2 %collective-permute-start.16 = (f32[64,256]{1,0:T(8,128)S(1)}, f32[64,256]{1,0:T(8,128)S(1)}, u32[]{:S(2)}, u32[]{:S(2)}) collective-permute-start(f32[64,256]{1,0:T(8,128)S(1)} %fusion.1), channel_id=1, source_target_pairs={{0,16},{1,17},{16,0},{17,1},{32,48},{33,49},{48,32},{49,33},{2,18}... | collective-permute-start | bytes 196616 | tf_op jit(solution)/shard_map/ppermute | solution.py:484
  114.4 5.2 %collective-permute-start.17 = (f32[64,256]{1,0:T(8,128)S(1)}, f32[64,256]{1,0:T(8,128)S(1)}, u32[]{:S(2)}, u32[]{:S(2)}) collective-permute-start(f32[64,256]{1,0:T(8,128)S(1)} %fusion.1), channel_id=1, source_target_pairs={{0,17},{1,16},{16,1},{17,0},{32,49},{33,48},{48,33},{49,32},{2,19}... | collective-permute-start | bytes 196616 | tf_op jit(solution)/shard_map/ppermute | solution.py:484
  119.6 7.1 %collective-permute-start.18 = (f32[64,256]{1,0:T(8,128)S(1)}, f32[64,256]{1,0:T(8,128)S(1)}, u32[]{:S(2)}, u32[]{:S(2)}) collective-permute-start(f32[64,256]{1,0:T(8,128)S(1)} %add_add_fusion.1), channel_id=1, source_target_pairs={{0,32},{1,33},{16,48},{17,49},{32,0},{33,1},{48,16},{49,17},{2,34}... | collective-permute-start | bytes 196616 | tf_op jit(solution)/shard_map/ppermute | solution.py:484
  127.5 14.4 %collective-permute-start.19 = (f32[2,256,256]{2,1,0:T(8,128)S(1)}, f32[2,256,256]{2,1,0:T(8,128)S(1)}, u32[]{:S(2)}, u32[]{:S(2)}) collective-permute-start(f32[2,256,256]{2,1,0:T(8,128)S(1)} %select_add_fusion), channel_id=1, source_target_pairs={{0,1},{1,2},{2,3},{3,4},{4,5},{5,6},{6,7},{8,9},{9,10},{10,11},{11... | collective-permute-start | bytes 1572872 | tf_op jit(solution)/shard_map/ppermute | solution.py:430
  133.7 4.3 %collective-permute-start.22 = (f32[64,256]{1,0:T(8,128)S(1)}, f32[64,256]{1,0:T(8,128)S(1)}, u32[]{:S(2)}, u32[]{:S(2)}) collective-permute-start(f32[64,256]{1,0:T(8,128)S(1)} %collective-permute-done.21), channel_id=1, source_target_pairs={{0,6},{2,0},{4,2},{6,4},{1,7},{3,1},{5,3},{7,5},{8,14},{10,8},{12,... | collective-permute-start | bytes 196616 | tf_op jit(solution)/shard_map/ppermute | solution.py:439
  138.0 9.1 %collective-permute-start.23 = (f32[256,256]{1,0:T(8,128)S(1)}, f32[256,256]{1,0:T(8,128)S(1)}, u32[]{:S(2)}, u32[]{:S(2)}) collective-permute-start(f32[256,256]{1,0:T(8,128)S(1)} %bitcast.80), channel_id=1, source_target_pairs={{0,192},{64,0},{128,64},{192,128},{1,193},{65,1},{129,65},{193,129... | collective-permute-start | bytes 786440 | tf_op jit(solution)/shard_map/ppermute | solution.py:439
  141.0 6.8 %collective-permute-start.24 = (f32[256,256]{1,0:T(8,128)S(1)}, f32[256,256]{1,0:T(8,128)S(1)}, u32[]{:S(2)}, u32[]{:S(2)}) collective-permute-start(f32[256,256]{1,0:T(8,128)S(1)} %bitcast.81), channel_id=1, source_target_pairs={{0,128},{64,192},{128,0},{192,64},{1,129},{65,193},{129,1},{193,65... | collective-permute-start | bytes 786440 | tf_op jit(solution)/shard_map/ppermute | solution.py:439
  141.1 9.2 %collective-permute-start.25 = (f32[256,256]{1,0:T(8,128)S(1)}, f32[256,256]{1,0:T(8,128)S(1)}, u32[]{:S(2)}, u32[]{:S(2)}) collective-permute-start(f32[256,256]{1,0:T(8,128)S(1)} %bitcast.82), channel_id=1, source_target_pairs={{0,64},{64,128},{128,192},{192,0},{1,65},{65,129},{129,193},{193,1... | collective-permute-start | bytes 786440 | tf_op jit(solution)/shard_map/ppermute | solution.py:439
  150.4 10.9 %collective-permute-start.26 = (f32[1024,256]{1,0:T(8,128)S(1)}, f32[1024,256]{1,0:T(8,128)S(1)}, u32[]{:S(2)}, u32[]{:S(2)}) collective-permute-start(f32[1024,256]{1,0:T(8,128)S(1)} %bitcast.75), channel_id=1, source_target_pairs={{0,8},{8,0},{1,9},{9,1},{2,10},{10,2},{3,11},{11,3},{4,12},{12,4},... | collective-permute-start | bytes 3145736 | tf_op jit(solution)/shard_map/ppermute | solution.py:549
  (12 other events, 107.1 us)

commit v8 on v7

--- a/solution.py
+++ b/solution.py
@@ -442,7 +442,7 @@
 def pieces(value, axis):
     count, me = lax.axis_size(axis), lax.axis_index(axis)
     value = value.reshape(count, -1, N)
-    return [piece(value, (me + step) % count) for step in range(1, count)] + [piece(value, me)]
+    return [piece(value, (me + step) & (count - 1)) for step in range(1, count)] + [piece(value, me)]
 
 
 def scatter_sum(parts, axis):
@@ -457,12 +457,19 @@
     return lax.optimization_barrier((value,) + others)[0]
 
 
+def circular_sum(parts, axis, *beside):
+    total = ring(parts[0], axis, -1)
+    for step, part in enumerate(parts[1:-1]):
+        total = ring(total + (after(part, *beside) if step else part), axis, -1)
+    return total + parts[-1]
+
+
 def collected(value, travelled, axis, *beside):
     count, me = lax.axis_size(axis), lax.axis_index(axis)
     whole = jnp.zeros((count,) + value.shape, value.dtype)
     whole = after(lax.dynamic_update_index_in_dim(whole, value, me, 0), *beside)
     for step, part in enumerate(travelled):
-        whole = lax.dynamic_update_index_in_dim(whole, part, (me + step + 1) % count, 0)
+        whole = lax.dynamic_update_index_in_dim(whole, part, (me + step + 1) & (count - 1), 0)
     return whole.reshape(-1, N)
 
 
@@ -537,9 +544,9 @@
     staying1, leaving1 = split(grads1, after(arrived1, *across))
     received1 = shifted(leaving1, TILE, 1)
     across[-1] = after(across[-1], leaving1)
-    across = pieces(after(scatter_sum(across, "y"), received1), "x")
-    arrived0 = moved(after(grads0, received1), 1, -1)
-    partial = scatter_sum(across, "x")
+    across = pieces(scatter_sum(across, "y"), "x")
+    arrived0 = moved(after(grads0, leaving1), 1, -1)
+    partial = circular_sum(across, "x", received1)
     staying0, leaving0 = split(grads0, arrived0)
     total = summed_over_z(after(partial, leaving0))
     received0 = shifted(after(leaving0, total), TILE, 1)

time: 164 us -> 165 us (level)
  starting transfers between devices: 70.1 us -> 82.9 us
  waiting for transfers between devices: 51.6 us -> 40.8 us
    ppermute x12, starting transfers between devices: 17.9 us -> 27.4 us  [ring(): lax.ppermute(value, axis, [(i, (i + step) % count) for i in range(count)])]
    ppermute x3, waiting for transfers between devices: 16.5 us -> 8.97 us  [shifted(): lax.ppermute(value, axes, [(source, source + steps) for source in range(f...]
    ppermute x1, starting transfers between devices: 8.6 us -> 13.3 us  [per_device(): opposite = lax.ppermute(total, 'core', swap)]
    ppermute x5, waiting for transfers between devices: 9.08 us -> 6.18 us  [moved(): return lax.ppermute(value, POS + TILE, pairs)]
  transfers between devices with their start and end apart: 27 -> 27, of which waited for: 18 -> 16; matrix products, arithmetic and copies ran while one was open for 4% -> 4% of each run, Pallas kernels for 7% -> 7%
where the time goes in v8:
time: 165 us; the launch traced here: 164 us
  starting transfers between devices  82.9 us (50%)
  waiting for transfers between devices  40.8 us (25%)
  Pallas kernels  21.6 us (13%)
  other arithmetic  8.87 us (5%)
  between operations  6.26 us (4%)
  local copies, waits for them, and re-layouts  3.62 us (2%)
    ppermute x12, starting transfers between devices, ring(): lax.ppermute(value, axis, [(i, (i + step) % count) for i in range(count)])  27.4 us
    ppermute x5, starting transfers between devices, moved(): return lax.ppermute(value, POS + TILE, pairs)  19.4 us
    ppermute x12, waiting for transfers between devices, ring(): lax.ppermute(value, axis, [(i, (i + step) % count) for i in range(count)])  14.4 us
    pallas_call x2, Pallas kernels, call(): pl.pallas_call(kernel, in_specs=[pl.BlockSpec(memory_space=pltpu.SMEM)] +...  14.4 us
    ppermute x1, starting transfers between devices, per_device(): opposite = lax.ppermute(total, 'core', swap)  13.3 us
    ppermute x3, starting transfers between devices, shifted(): lax.ppermute(value, axes, [(source, source + steps) for source in range(f...  12 us
    ppermute x3, waiting for transfers between devices, shifted(): lax.ppermute(value, axes, [(source, source + steps) for source in range(f...  8.97 us
    ppermute x4, waiting for transfers between devices, exchange(): return lax.ppermute(value, axes, [(i, i ^ bits) for i in range(count)])  8.27 us
  transfers between devices with their start and end apart: 27, of which 16 were waited for; matrix products, arithmetic and copies ran while one was open for 4% of the time, Pallas kernels for 7%

profile of v8, /device:TPU:1, one launch (start us, length us, event | category | flops | bytes accessed | tf_op | source)
XLA Modules:
  0.0 164.0 jit_solution(13393034950707849548)
XLA Ops:
  0.6 4.5 %collective-permute-start = (s32[1,2]{1,0:T(1,128)}, s32[1,2]{1,0:T(1,128)S(1)}, u32[]{:S(2)}, u32[]{:S(2)}) collective-permute-start(s32[1,2]{1,0:T(1,128)} %param.9), channel_id=1, source_target_pairs={{0,8},{8,16},{16,24},{24,32},{32,40},{40,48},{48,56},{56,64},{64,7... | collective-permute-start | bytes 32 | tf_op jit(solution)/shard_map/ppermute | solution.py:517
  7.2 7.2 %shard_map.77 = (f32[8,256,256]{2,1,0:T(8,128)}, bf16[5,2,256,256]{3,2,1,0:T(8,128)(2,1)}, f32[2,256,256]{2,1,0:T(8,128)}) custom-call(s32[1]{0:T(128)} %bitcast.8.core, f32[8,256,256]{2,1,0:T(8,128)} %bitcast.73, bf16[5,2,256,256]{3,2,1,0:T(8,128)(2,1)} %constant.82.clone.table, f32[2,256,256]{2,1,0:T(8,128)} %constant.83.clone.phases), custom_call_target="tpu_custom_call" | custom-call | tf_op jit(solution)/shard_map/pallas_call | solution.py:395
  18.4 9.0 %collective-permute-done.1 = f32[2,2,256,256]{3,2,1,0:T(8,128)} collective-permute-done((f32[2,2,256,256]{3,2,1,0:T(8,128)}, f32[2,2,256,256]{3,2,1,0:T(8,128)}, u32[]{:S(2)}, u32[]{:S(2)}) %collective-permute-start.1) | collective-permute-done | bytes 1048608 | tf_op jit(solution)/shard_map/ppermute | solution.py:430
  27.4 2.8 %bitcast_select_fusion = (f32[2,256,256]{2,1,0:T(8,128)}, f32[2,256,256]{2,1,0:T(8,128)}, f32[2,256,256]{2,1,0:T(8,128)S(1)}, f32[2,256,256]{2,1,0:T(8,128)S(1)}) fusion(f32[2,2,256,256]{3,2,1,0:T(8,128)} %param.6, f32[2,2,256,256]{3,2,1,0:T(8,128)} %collective-permute-done.1, pred[256]{0:T(512)(128)(4,1)S(1)} %get-tuple-element.62, ...), kind=kLoop, calls=%fused_computation.2 | loop fusion | flops 524288 | bytes 4194816 | tf_op jit(solution)/shard_map/jit(_where)/select_n | solution.py:525
  30.2 8.5 %collective-permute-start.3 = (f32[2,256,256]{2,1,0:T(8,128)}, f32[2,256,256]{2,1,0:T(8,128)}, u32[]{:S(2)}, u32[]{:S(2)}) collective-permute-start(f32[2,256,256]{2,1,0:T(8,128)} %get-tuple-element.42), channel_id=1, source_target_pairs={{1,9},{3,11},{5,13},{7,15},{8,0},{9,17},{10,2},{11,19},{12,4},{13,... | collective-permute-start | bytes 1572872 | tf_op jit(solution)/shard_map/ppermute | solution.py:508
  42.7 6.2 %collective-permute-done.3.other = f32[2,256,256]{2,1,0:T(8,128)} collective-permute-done((f32[2,256,256]{2,1,0:T(8,128)}, f32[2,256,256]{2,1,0:T(8,128)}, u32[]{:S(2)}, u32[]{:S(2)}) %collective-permute-start.3) | collective-permute-done | bytes 524320 | tf_op jit(solution)/shard_map/ppermute | solution.py:508
  50.4 4.0 %shard_map.78 = (f32[4,2,256,256]{3,2,1,0:T(8,128)S(1)}, f32[2,256,256]{2,1,0:T(8,128)S(1)}) custom-call(s32[4]{0:T(128)S(1)} %pad_add_fusion.place, f32[2,256,256]{2,1,0:T(8,128)S(1)} %get-tuple-element.47.mine, f32[2,256,256]{2,1,0:T(8,128)} %collective-permute-done.3.other, f32[4,2,256,256]{3,2,1,0:T(8,128)S(1)} %bitcast.66, ...), custom_call_target="tpu_custom_call" | custom-call | flops 3221225472 | bytes 4194304 | tf_op jit(solution)/shard_map/pallas_call | solution.py:336
  54.5 10.4 %shard_map.79 = (f32[2,256,256]{2,1,0:T(8,128)S(1)}, f32[2,256,256]{2,1,0:T(8,128)S(1)}, f32[2,2,256,256]{3,2,1,0:T(8,128)}, f32[2,2,256,256]{3,2,1,0:T(8,128)S(1)}) custom-call(s32[4]{0:T(128)S(1)} %pad_add_fusion.place, f32[2,256,256]{2,1,0:T(8,128)S(1)} %get-tuple-element.46.mine, f32[2,256,256]{2,1,0:T(8,128)S(1)} %collective-permute-done.2.other, ...), custom_call_target="tpu_custom_call" | custom-call | flops 9663676416 | bytes 4194304 | tf_op jit(solution)/shard_map/pallas_call | solution.py:336
  64.9 6.0 %collective-permute-start.5 = (f32[2,256,256]{2,1,0:T(8,128)S(1)}, f32[2,256,256]{2,1,0:T(8,128)S(1)}, u32[]{:S(2)}, u32[]{:S(2)}) collective-permute-start(f32[2,256,256]{2,1,0:T(8,128)S(1)} %get-tuple-element.30), channel_id=1, source_target_pairs={{0,8},{1,249},{2,10},{3,251},{4,12},{5,253},{6,14},{7,255},{8,16},... | collective-permute-start | bytes 1572872 | tf_op jit(solution)/shard_map/ppermute | solution.py:508
  73.7 3.0 %collective-permute-start.10 = (f32[256,256]{1,0:T(8,128)S(1)}, f32[256,256]{1,0:T(8,128)S(1)}, u32[]{:S(2)}, u32[]{:S(2)}) collective-permute-start(f32[256,256]{1,0:T(8,128)S(1)} %get-tuple-element.49), channel_id=1, source_target_pairs={{0,192},{64,0},{128,64},{192,128},{1,193},{65,1},{129,65},{193,129... | collective-permute-start | bytes 786440 | tf_op jit(solution)/shard_map/ppermute | solution.py:439
  78.5 8.6 %collective-permute-start.13 = (f32[2,256,256]{2,1,0:T(8,128)S(1)}, f32[2,256,256]{2,1,0:T(8,128)}, u32[]{:S(2)}, u32[]{:S(2)}) collective-permute-start(f32[2,256,256]{2,1,0:T(8,128)S(1)} %select_add_fusion.1), channel_id=1, source_target_pairs={{0,1},{1,2},{2,3},{3,4},{4,5},{5,6},{6,7},{8,9},{9,10},{10,11},{11... | collective-permute-start | bytes 1572872 | tf_op jit(solution)/shard_map/ppermute | solution.py:430
  89.5 2.5 %collective-permute-done.9 = f32[256,256]{1,0:T(8,128)S(1)} collective-permute-done((f32[256,256]{1,0:T(8,128)S(1)}, f32[256,256]{1,0:T(8,128)S(1)}, u32[]{:S(2)}, u32[]{:S(2)}) %collective-permute-start.9) | collective-permute-done | bytes 262176 | tf_op jit(solution)/shard_map/ppermute | solution.py:439
  92.2 2.6 %collective-permute-start.11 = (f32[64,256]{1,0:T(8,128)S(1)}, f32[64,256]{1,0:T(8,128)S(1)}, u32[]{:S(2)}, u32[]{:S(2)}) collective-permute-start(f32[64,256]{1,0:T(8,128)S(1)} %get-tuple-element.53), channel_id=1, source_target_pairs={{0,6},{2,0},{4,2},{6,4},{1,7},{3,1},{5,3},{7,5},{8,14},{10,8},{12,... | collective-permute-start | bytes 196616 | tf_op jit(solution)/shard_map/ppermute | solution.py:439
  96.1 3.3 %collective-permute-start.12 = (f32[64,256]{1,0:T(8,128)S(1)}, f32[64,256]{1,0:T(8,128)S(1)}, u32[]{:S(2)}, u32[]{:S(2)}) collective-permute-start(f32[64,256]{1,0:T(8,128)S(1)} %bitcast_add_fusion.1), channel_id=1, source_target_pairs={{0,6},{2,0},{4,2},{6,4},{1,7},{3,1},{5,3},{7,5},{8,14},{10,8},{12,... | collective-permute-start | bytes 196616 | tf_op jit(solution)/shard_map/ppermute | solution.py:439
  100.7 3.1 %collective-permute-start.14 = (f32[64,256]{1,0:T(8,128)S(1)}, f32[64,256]{1,0:T(8,128)S(1)}, u32[]{:S(2)}, u32[]{:S(2)}) collective-permute-start(f32[64,256]{1,0:T(8,128)S(1)} %add.152), channel_id=1, source_target_pairs={{0,6},{2,0},{4,2},{6,4},{1,7},{3,1},{5,3},{7,5},{8,14},{10,8},{12,... | collective-permute-start | bytes 196616 | tf_op jit(solution)/shard_map/ppermute | solution.py:439
  109.3 2.9 %collective-permute-done.17 = f32[64,256]{1,0:T(8,128)S(1)} collective-permute-done((f32[64,256]{1,0:T(8,128)S(1)}, f32[64,256]{1,0:T(8,128)S(1)}, u32[]{:S(2)}, u32[]{:S(2)}) %collective-permute-start.17) | collective-permute-done | bytes 65568 | tf_op jit(solution)/shard_map/ppermute | solution.py:491
  112.3 2.7 %collective-permute-start.18 = (f32[64,256]{1,0:T(8,128)S(1)}, f32[64,256]{1,0:T(8,128)S(1)}, u32[]{:S(2)}, u32[]{:S(2)}) collective-permute-start(f32[64,256]{1,0:T(8,128)S(1)} %add_add_fusion.1), channel_id=1, source_target_pairs={{0,32},{1,33},{16,48},{17,49},{32,0},{33,1},{48,16},{49,17},{2,34}... | collective-permute-start | bytes 196616 | tf_op jit(solution)/shard_map/ppermute | solution.py:491
  115.0 4.8 %collective-permute-done.18 = f32[64,256]{1,0:T(8,128)S(1)} collective-permute-done((f32[64,256]{1,0:T(8,128)S(1)}, f32[64,256]{1,0:T(8,128)S(1)}, u32[]{:S(2)}, u32[]{:S(2)}) %collective-permute-start.18) | collective-permute-done | bytes 65568 | tf_op jit(solution)/shard_map/ppermute | solution.py:491
  119.8 2.6 %collective-permute-start.20 = (f32[64,256]{1,0:T(8,128)S(1)}, f32[64,256]{1,0:T(8,128)S(1)}, u32[]{:S(2)}, u32[]{:S(2)}) collective-permute-start(f32[64,256]{1,0:T(8,128)S(1)} %get-tuple-element.41), channel_id=1, source_target_pairs={{0,6},{2,0},{4,2},{6,4},{1,7},{3,1},{5,3},{7,5},{8,14},{10,8},{12,... | collective-permute-start | bytes 196616 | tf_op jit(solution)/shard_map/ppermute | solution.py:439
  124.5 2.5 %collective-permute-start.21 = (f32[64,256]{1,0:T(8,128)S(1)}, f32[64,256]{1,0:T(8,128)S(1)}, u32[]{:S(2)}, u32[]{:S(2)}) collective-permute-start(f32[64,256]{1,0:T(8,128)S(1)} %collective-permute-done.20), channel_id=1, source_target_pairs={{0,6},{2,0},{4,2},{6,4},{1,7},{3,1},{5,3},{7,5},{8,14},{10,8},{12,... | collective-permute-start | bytes 196616 | tf_op jit(solution)/shard_map/ppermute | solution.py:439
  128.3 3.0 %collective-permute-start.22 = (f32[64,256]{1,0:T(8,128)S(1)}, f32[64,256]{1,0:T(8,128)S(1)}, u32[]{:S(2)}, u32[]{:S(2)}) collective-permute-start(f32[64,256]{1,0:T(8,128)S(1)} %collective-permute-done.21), channel_id=1, source_target_pairs={{0,6},{2,0},{4,2},{6,4},{1,7},{3,1},{5,3},{7,5},{8,14},{10,8},{12,... | collective-permute-start | bytes 196616 | tf_op jit(solution)/shard_map/ppermute | solution.py:439
  132.6 4.3 %collective-permute-start.23 = (f32[256,256]{1,0:T(8,128)S(1)}, f32[256,256]{1,0:T(8,128)S(1)}, u32[]{:S(2)}, u32[]{:S(2)}) collective-permute-start(f32[256,256]{1,0:T(8,128)S(1)} %bitcast.77), channel_id=1, source_target_pairs={{0,192},{64,0},{128,64},{192,128},{1,193},{65,1},{129,65},{193,129... | collective-permute-start | bytes 786440 | tf_op jit(solution)/shard_map/ppermute | solution.py:439
  143.7 2.7 %collective-permute-done.25 = f32[256,256]{1,0:T(8,128)S(1)} collective-permute-done((f32[256,256]{1,0:T(8,128)S(1)}, f32[256,256]{1,0:T(8,128)S(1)}, u32[]{:S(2)}, u32[]{:S(2)}) %collective-permute-start.25) | collective-permute-done | bytes 262176 | tf_op jit(solution)/shard_map/ppermute | solution.py:439
  146.4 13.3 %collective-permute-start.26 = (f32[1024,256]{1,0:T(8,128)S(1)}, f32[1024,256]{1,0:T(8,128)S(1)}, u32[]{:S(2)}, u32[]{:S(2)}) collective-permute-start(f32[1024,256]{1,0:T(8,128)S(1)} %bitcast.71), channel_id=1, source_target_pairs={{0,8},{8,0},{1,9},{9,1},{2,10},{10,2},{3,11},{11,3},{4,12},{12,4},... | collective-permute-start | bytes 3145736 | tf_op jit(solution)/shard_map/ppermute | solution.py:556
  (82 shorter events, 37.7 us)
Async XLA Ops:
  0.6 5.3 %collective-permute-start = (s32[1,2]{1,0:T(1,128)}, s32[1,2]{1,0:T(1,128)S(1)}, u32[]{:S(2)}, u32[]{:S(2)}) collective-permute-start(s32[1,2]{1,0:T(1,128)} %param.9), channel_id=1, source_target_pairs={{0,8},{8,16},{16,24},{24,32},{32,40},{40,48},{48,56},{56,64},{64,7... | collective-permute-start | bytes 32 | tf_op jit(solution)/shard_map/ppermute | solution.py:517
  6.0 21.4 %collective-permute-start.1 = (f32[2,2,256,256]{3,2,1,0:T(8,128)}, f32[2,2,256,256]{3,2,1,0:T(8,128)}, u32[]{:S(2)}, u32[]{:S(2)}) collective-permute-start(f32[2,2,256,256]{3,2,1,0:T(8,128)} %param.6), channel_id=1, source_target_pairs={{1,0},{2,1},{3,2},{4,3},{5,4},{6,5},{7,6},{9,8},{10,9},{11,10},{12... | collective-permute-start | bytes 3145736 | tf_op jit(solution)/shard_map/ppermute | solution.py:430
  30.2 18.6 %collective-permute-start.3 = (f32[2,256,256]{2,1,0:T(8,128)}, f32[2,256,256]{2,1,0:T(8,128)}, u32[]{:S(2)}, u32[]{:S(2)}) collective-permute-start(f32[2,256,256]{2,1,0:T(8,128)} %get-tuple-element.42), channel_id=1, source_target_pairs={{1,9},{3,11},{5,13},{7,15},{8,0},{9,17},{10,2},{11,19},{12,4},{13,... | collective-permute-start | bytes 1572872 | tf_op jit(solution)/shard_map/ppermute | solution.py:508
  38.7 15.8 %collective-permute-start.2 = (f32[2,256,256]{2,1,0:T(8,128)}, f32[2,256,256]{2,1,0:T(8,128)S(1)}, u32[]{:S(2)}, u32[]{:S(2)}) collective-permute-start(f32[2,256,256]{2,1,0:T(8,128)} %get-tuple-element.43), channel_id=1, source_target_pairs={{1,9},{3,11},{5,13},{7,15},{8,0},{9,17},{10,2},{11,19},{12,4},{13,... | collective-permute-start | bytes 1572872 | tf_op jit(solution)/shard_map/ppermute | solution.py:508
  42.0 12.5 %collective-permute-start.4 = (f32[1,256,256]{2,1,0:T(8,128)S(1)}, f32[1,256,256]{2,1,0:T(8,128)S(1)}, u32[]{:S(2)}, u32[]{:S(2)}) collective-permute-start(f32[1,256,256]{2,1,0:T(8,128)S(1)} %copy-done.6), channel_id=1, source_target_pairs={{0,0},{1,9},{2,2},{3,11},{4,4},{5,13},{6,6},{7,15},{8,8},{9,17},{1... | collective-permute-start | bytes 786440 | tf_op jit(solution)/shard_map/ppermute | solution.py:508
  64.9 7.3 %collective-permute-start.6 = (f32[2,2,256,256]{3,2,1,0:T(8,128)}, f32[2,2,256,256]{3,2,1,0:T(8,128)}, u32[]{:S(2)}, u32[]{:S(2)}) collective-permute-start(f32[2,2,256,256]{3,2,1,0:T(8,128)} %get-tuple-element.32), channel_id=1, source_target_pairs={{0,8},{8,0},{1,9},{9,1},{2,10},{10,2},{3,11},{11,3},{4,12},{12,4},... | collective-permute-start | bytes 3145736 | tf_op jit(solution)/shard_map/ppermute | solution.py:543
  64.9 13.4 %collective-permute-start.5 = (f32[2,256,256]{2,1,0:T(8,128)S(1)}, f32[2,256,256]{2,1,0:T(8,128)S(1)}, u32[]{:S(2)}, u32[]{:S(2)}) collective-permute-start(f32[2,256,256]{2,1,0:T(8,128)S(1)} %get-tuple-element.30), channel_id=1, source_target_pairs={{0,8},{1,249},{2,10},{3,251},{4,12},{5,253},{6,14},{7,255},{8,16},... | collective-permute-start | bytes 1572872 | tf_op jit(solution)/shard_map/ppermute | solution.py:508
  73.7 15.9 %collective-permute-start.10 = (f32[256,256]{1,0:T(8,128)S(1)}, f32[256,256]{1,0:T(8,128)S(1)}, u32[]{:S(2)}, u32[]{:S(2)}) collective-permute-start(f32[256,256]{1,0:T(8,128)S(1)} %get-tuple-element.49), channel_id=1, source_target_pairs={{0,192},{64,0},{128,64},{192,128},{1,193},{65,1},{129,65},{193,129... | collective-permute-start | bytes 786440 | tf_op jit(solution)/shard_map/ppermute | solution.py:439
  76.6 12.9 %collective-permute-start.8 = (f32[256,256]{1,0:T(8,128)S(1)}, f32[256,256]{1,0:T(8,128)S(1)}, u32[]{:S(2)}, u32[]{:S(2)}) collective-permute-start(f32[256,256]{1,0:T(8,128)S(1)} %get-tuple-element.51), channel_id=1, source_target_pairs={{0,64},{64,128},{128,192},{192,0},{1,65},{65,129},{129,193},{193,1... | collective-permute-start | bytes 786440 | tf_op jit(solution)/shard_map/ppermute | solution.py:439
  76.7 15.4 %collective-permute-start.9 = (f32[256,256]{1,0:T(8,128)S(1)}, f32[256,256]{1,0:T(8,128)S(1)}, u32[]{:S(2)}, u32[]{:S(2)}) collective-permute-start(f32[256,256]{1,0:T(8,128)S(1)} %get-tuple-element.50), channel_id=1, source_target_pairs={{0,128},{64,192},{128,0},{192,64},{1,129},{65,193},{129,1},{193,65... | collective-permute-start | bytes 786440 | tf_op jit(solution)/shard_map/ppermute | solution.py:439
  78.5 20.9 %collective-permute-start.13 = (f32[2,256,256]{2,1,0:T(8,128)S(1)}, f32[2,256,256]{2,1,0:T(8,128)}, u32[]{:S(2)}, u32[]{:S(2)}) collective-permute-start(f32[2,256,256]{2,1,0:T(8,128)S(1)} %select_add_fusion.1), channel_id=1, source_target_pairs={{0,1},{1,2},{2,3},{3,4},{4,5},{5,6},{6,7},{8,9},{9,10},{10,11},{11... | collective-permute-start | bytes 1572872 | tf_op jit(solution)/shard_map/ppermute | solution.py:430
  87.1 16.7 %collective-permute-start.7 = (f32[2,256,256]{2,1,0:T(8,128)S(1)}, f32[2,256,256]{2,1,0:T(8,128)S(1)}, u32[]{:S(2)}, u32[]{:S(2)}) collective-permute-start(f32[2,256,256]{2,1,0:T(8,128)S(1)} %get-tuple-element.34), channel_id=1, source_target_pairs={{0,8},{1,249},{2,10},{3,251},{4,12},{5,253},{6,14},{7,255},{8,16},... | collective-permute-start | bytes 1572872 | tf_op jit(solution)/shard_map/ppermute | solution.py:508
  96.1 4.6 %collective-permute-start.12 = (f32[64,256]{1,0:T(8,128)S(1)}, f32[64,256]{1,0:T(8,128)S(1)}, u32[]{:S(2)}, u32[]{:S(2)}) collective-permute-start(f32[64,256]{1,0:T(8,128)S(1)} %bitcast_add_fusion.1), channel_id=1, source_target_pairs={{0,6},{2,0},{4,2},{6,4},{1,7},{3,1},{5,3},{7,5},{8,14},{10,8},{12,... | collective-permute-start | bytes 196616 | tf_op jit(solution)/shard_map/ppermute | solution.py:439
  100.7 4.4 %collective-permute-start.14 = (f32[64,256]{1,0:T(8,128)S(1)}, f32[64,256]{1,0:T(8,128)S(1)}, u32[]{:S(2)}, u32[]{:S(2)}) collective-permute-start(f32[64,256]{1,0:T(8,128)S(1)} %add.152), channel_id=1, source_target_pairs={{0,6},{2,0},{4,2},{6,4},{1,7},{3,1},{5,3},{7,5},{8,14},{10,8},{12,... | collective-permute-start | bytes 196616 | tf_op jit(solution)/shard_map/ppermute | solution.py:439
  105.2 4.1 %collective-permute-start.16 = (f32[64,256]{1,0:T(8,128)S(1)}, f32[64,256]{1,0:T(8,128)S(1)}, u32[]{:S(2)}, u32[]{:S(2)}) collective-permute-start(f32[64,256]{1,0:T(8,128)S(1)} %bitcast_add_fusion), channel_id=1, source_target_pairs={{0,16},{1,17},{16,0},{17,1},{32,48},{33,49},{48,32},{49,33},{2,18}... | collective-permute-start | bytes 196616 | tf_op jit(solution)/shard_map/ppermute | solution.py:491
  106.8 5.5 %collective-permute-start.17 = (f32[64,256]{1,0:T(8,128)S(1)}, f32[64,256]{1,0:T(8,128)S(1)}, u32[]{:S(2)}, u32[]{:S(2)}) collective-permute-start(f32[64,256]{1,0:T(8,128)S(1)} %bitcast_add_fusion), channel_id=1, source_target_pairs={{0,17},{1,16},{16,1},{17,0},{32,49},{33,48},{48,33},{49,32},{2,19}... | collective-permute-start | bytes 196616 | tf_op jit(solution)/shard_map/ppermute | solution.py:491
  112.3 7.4 %collective-permute-start.18 = (f32[64,256]{1,0:T(8,128)S(1)}, f32[64,256]{1,0:T(8,128)S(1)}, u32[]{:S(2)}, u32[]{:S(2)}) collective-permute-start(f32[64,256]{1,0:T(8,128)S(1)} %add_add_fusion.1), channel_id=1, source_target_pairs={{0,32},{1,33},{16,48},{17,49},{32,0},{33,1},{48,16},{49,17},{2,34}... | collective-permute-start | bytes 196616 | tf_op jit(solution)/shard_map/ppermute | solution.py:491
  119.8 4.7 %collective-permute-start.20 = (f32[64,256]{1,0:T(8,128)S(1)}, f32[64,256]{1,0:T(8,128)S(1)}, u32[]{:S(2)}, u32[]{:S(2)}) collective-permute-start(f32[64,256]{1,0:T(8,128)S(1)} %get-tuple-element.41), channel_id=1, source_target_pairs={{0,6},{2,0},{4,2},{6,4},{1,7},{3,1},{5,3},{7,5},{8,14},{10,8},{12,... | collective-permute-start | bytes 196616 | tf_op jit(solution)/shard_map/ppermute | solution.py:439
  122.3 16.2 %collective-permute-start.19 = (f32[2,256,256]{2,1,0:T(8,128)S(1)}, f32[2,256,256]{2,1,0:T(8,128)S(1)}, u32[]{:S(2)}, u32[]{:S(2)}) collective-permute-start(f32[2,256,256]{2,1,0:T(8,128)S(1)} %select_add_fusion), channel_id=1, source_target_pairs={{0,1},{1,2},{2,3},{3,4},{4,5},{5,6},{6,7},{8,9},{9,10},{10,11},{11... | collective-permute-start | bytes 1572872 | tf_op jit(solution)/shard_map/ppermute | solution.py:430
  128.3 4.3 %collective-permute-start.22 = (f32[64,256]{1,0:T(8,128)S(1)}, f32[64,256]{1,0:T(8,128)S(1)}, u32[]{:S(2)}, u32[]{:S(2)}) collective-permute-start(f32[64,256]{1,0:T(8,128)S(1)} %collective-permute-done.21), channel_id=1, source_target_pairs={{0,6},{2,0},{4,2},{6,4},{1,7},{3,1},{5,3},{7,5},{8,14},{10,8},{12,... | collective-permute-start | bytes 196616 | tf_op jit(solution)/shard_map/ppermute | solution.py:439
  132.6 10.4 %collective-permute-start.23 = (f32[256,256]{1,0:T(8,128)S(1)}, f32[256,256]{1,0:T(8,128)S(1)}, u32[]{:S(2)}, u32[]{:S(2)}) collective-permute-start(f32[256,256]{1,0:T(8,128)S(1)} %bitcast.77), channel_id=1, source_target_pairs={{0,192},{64,0},{128,64},{192,128},{1,193},{65,1},{129,65},{193,129... | collective-permute-start | bytes 786440 | tf_op jit(solution)/shard_map/ppermute | solution.py:439
  136.9 6.8 %collective-permute-start.24 = (f32[256,256]{1,0:T(8,128)S(1)}, f32[256,256]{1,0:T(8,128)S(1)}, u32[]{:S(2)}, u32[]{:S(2)}) collective-permute-start(f32[256,256]{1,0:T(8,128)S(1)} %bitcast.78), channel_id=1, source_target_pairs={{0,128},{64,192},{128,0},{192,64},{1,129},{65,193},{129,1},{193,65... | collective-permute-start | bytes 786440 | tf_op jit(solution)/shard_map/ppermute | solution.py:439
  138.4 8.0 %collective-permute-start.25 = (f32[256,256]{1,0:T(8,128)S(1)}, f32[256,256]{1,0:T(8,128)S(1)}, u32[]{:S(2)}, u32[]{:S(2)}) collective-permute-start(f32[256,256]{1,0:T(8,128)S(1)} %bitcast.79), channel_id=1, source_target_pairs={{0,64},{64,128},{128,192},{192,0},{1,65},{65,129},{129,193},{193,1... | collective-permute-start | bytes 786440 | tf_op jit(solution)/shard_map/ppermute | solution.py:439
  146.4 15.5 %collective-permute-start.26 = (f32[1024,256]{1,0:T(8,128)S(1)}, f32[1024,256]{1,0:T(8,128)S(1)}, u32[]{:S(2)}, u32[]{:S(2)}) collective-permute-start(f32[1024,256]{1,0:T(8,128)S(1)} %bitcast.71), channel_id=1, source_target_pairs={{0,8},{8,0},{1,9},{9,1},{2,10},{10,2},{3,11},{11,3},{4,12},{12,4},... | collective-permute-start | bytes 3145736 | tf_op jit(solution)/shard_map/ppermute | solution.py:556
  (10 other events, 75.0 us)

commit v9 on v8

--- a/solution.py
+++ b/solution.py
@@ -360,7 +360,7 @@
         [(probes.shape, F32), ((2, N, N), F32)],
         [operand(modes)] + products_scratch(modes),
         3 << 30,
-        20,
+        14,
     )
 
 
@@ -373,7 +373,7 @@
         [field_shape, field_shape, terms_shape, terms_shape],
         [field_shape, ((N, N), F32), operand(modes)] + products_scratch(modes),
         9 << 30,
-        26,
+        22,
     )
 
 
@@ -478,13 +478,6 @@
     return collected(value, [ring(value, axis, -step) for step in steps], axis, *beside)
 
 
-def circular_gather(value, axis):
-    travelled = [ring(value, axis, -1)]
-    for _ in range(2, lax.axis_size(axis)):
-        travelled.append(ring(travelled[-1], axis, -1))
-    return collected(value, travelled, axis)
-
-
 def exchange(value, bits):
     axes = ("zh", "zl")
     count = math.prod(lax.axis_size(axis) for axis in axes)
@@ -549,10 +542,10 @@
     partial = circular_sum(across, "x", received1)
     staying0, leaving0 = split(grads0, arrived0)
     total = summed_over_z(after(partial, leaving0))
+    total = gather(total, "x")
     received0 = shifted(after(leaving0, total), TILE, 1)
-    total = circular_gather(total, "x")
+    total = after(gather(total, "y"), received0)
     object_grad = jnp.stack([staying0 + received0, staying1 + received1])
-    total = gather(total, "y", object_grad)
     opposite = lax.ppermute(total, "core", swap)
     half = lax.broadcasted_iota(jnp.int32, (2, 1, 1), 0)
     probe_grad = jnp.where(half == lax.axis_index("core"), total, opposite)

time: 165 us -> 164 us (level)
  the two profiles are of different devices: /device:TPU:1 before, /device:TPU:141 now
where the time goes in v9:
time: 164 us; the launch traced here: 163 us
  starting transfers between devices  73.5 us (45%)
  waiting for transfers between devices  48.4 us (30%)
  Pallas kernels  21.2 us (13%)
  other arithmetic  9.01 us (5%)
  between operations  6.31 us (4%)
  local copies, waits for them, and re-layouts  4.85 us (3%)
    ppermute x3, waiting for transfers between devices, shifted(): lax.ppermute(value, axes, [(source, source + steps) for source in range(f...  17.6 us
    ppermute x1, starting transfers between devices, per_device(): opposite = lax.ppermute(total, 'core', swap)  17.6 us
    ppermute x5, starting transfers between devices, moved(): return lax.ppermute(value, POS + TILE, pairs)  16.7 us
    ppermute x3, starting transfers between devices, shifted(): lax.ppermute(value, axes, [(source, source + steps) for source in range(f...  14.9 us
    pallas_call x2, Pallas kernels, call(): pl.pallas_call(kernel, in_specs=[pl.BlockSpec(memory_space=pltpu.SMEM)] +...  14 us
    ppermute x12, starting transfers between devices, ring(): lax.ppermute(value, axis, [(i, (i + step) % count) for i in range(count)])  13.3 us
    ppermute x4, waiting for transfers between devices, exchange(): return lax.ppermute(value, axes, [(i, i ^ bits) for i in range(count)])  12 us
    ppermute x12, waiting for transfers between devices, ring(): lax.ppermute(value, axis, [(i, (i + step) % count) for i in range(count)])  11.4 us
  transfers between devices with their start and end apart: 27, of which 15 were waited for; matrix products, arithmetic and copies ran while one was open for 4% of the time, Pallas kernels for 7%

profile of v9, /device:TPU:141, one launch (start us, length us, event | category | flops | bytes accessed | tf_op | source)
XLA Modules:
  0.0 163.3 jit_solution(755796390238199673)
XLA Ops:
  3.3 2.6 %collective-permute-start.1 = (f32[2,2,256,256]{3,2,1,0:T(8,128)}, f32[2,2,256,256]{3,2,1,0:T(8,128)}, u32[]{:S(2)}, u32[]{:S(2)}) collective-permute-start(f32[2,2,256,256]{3,2,1,0:T(8,128)} %param.6), channel_id=1, source_target_pairs={{1,0},{2,1},{3,2},{4,3},{5,4},{6,5},{7,6},{9,8},{10,9},{11,10},{12... | collective-permute-start | bytes 3145736 | tf_op jit(solution)/shard_map/ppermute | solution.py:430
  6.0 7.2 %shard_map.77 = (f32[8,256,256]{2,1,0:T(8,128)}, bf16[5,2,256,256]{3,2,1,0:T(8,128)(2,1)}, f32[2,256,256]{2,1,0:T(8,128)}) custom-call(s32[1]{0:T(128)} %bitcast.8.core, f32[8,256,256]{2,1,0:T(8,128)} %bitcast.73, bf16[5,2,256,256]{3,2,1,0:T(8,128)(2,1)} %constant.82.clone.table, f32[2,256,256]{2,1,0:T(8,128)} %constant.83.clone.phases), custom_call_target="tpu_custom_call" | custom-call | tf_op jit(solution)/shard_map/pallas_call | solution.py:395
  17.1 9.8 %collective-permute-done.1 = f32[2,2,256,256]{3,2,1,0:T(8,128)} collective-permute-done((f32[2,2,256,256]{3,2,1,0:T(8,128)}, f32[2,2,256,256]{3,2,1,0:T(8,128)}, u32[]{:S(2)}, u32[]{:S(2)}) %collective-permute-start.1) | collective-permute-done | bytes 1048608 | tf_op jit(solution)/shard_map/ppermute | solution.py:430
  26.9 2.8 %bitcast_select_fusion = (f32[2,256,256]{2,1,0:T(8,128)}, f32[2,256,256]{2,1,0:T(8,128)}, f32[2,256,256]{2,1,0:T(8,128)S(1)}, f32[2,256,256]{2,1,0:T(8,128)S(1)}) fusion(f32[2,2,256,256]{3,2,1,0:T(8,128)} %param.6, f32[2,2,256,256]{3,2,1,0:T(8,128)} %collective-permute-done.1, pred[256]{0:T(512)(128)(4,1)S(1)} %get-tuple-element.62, ...), kind=kLoop, calls=%fused_computation.2 | loop fusion | flops 524288 | bytes 4194816 | tf_op jit(solution)/shard_map/jit(_where)/select_n | solution.py:518
  29.7 6.1 %collective-permute-start.3 = (f32[2,256,256]{2,1,0:T(8,128)}, f32[2,256,256]{2,1,0:T(8,128)}, u32[]{:S(2)}, u32[]{:S(2)}) collective-permute-start(f32[2,256,256]{2,1,0:T(8,128)} %get-tuple-element.42), channel_id=1, source_target_pairs={{1,9},{3,11},{5,13},{7,15},{8,0},{9,17},{10,2},{11,19},{12,4},{13,... | collective-permute-start | bytes 1572872 | tf_op jit(solution)/shard_map/ppermute | solution.py:501
  35.8 3.5 %collective-permute-start.2 = (f32[2,256,256]{2,1,0:T(8,128)}, f32[2,256,256]{2,1,0:T(8,128)S(1)}, u32[]{:S(2)}, u32[]{:S(2)}) collective-permute-start(f32[2,256,256]{2,1,0:T(8,128)} %get-tuple-element.43), channel_id=1, source_target_pairs={{1,9},{3,11},{5,13},{7,15},{8,0},{9,17},{10,2},{11,19},{12,4},{13,... | collective-permute-start | bytes 1572872 | tf_op jit(solution)/shard_map/ppermute | solution.py:501
  44.5 4.0 %shard_map.78 = (f32[4,2,256,256]{3,2,1,0:T(8,128)S(1)}, f32[2,256,256]{2,1,0:T(8,128)S(1)}) custom-call(s32[4]{0:T(128)S(1)} %pad_add_fusion.place, f32[2,256,256]{2,1,0:T(8,128)S(1)} %get-tuple-element.47.mine, f32[2,256,256]{2,1,0:T(8,128)} %collective-permute-done.3.other, f32[4,2,256,256]{3,2,1,0:T(8,128)S(1)} %bitcast.66, ...), custom_call_target="tpu_custom_call" | custom-call | flops 3221225472 | bytes 4194304 | tf_op jit(solution)/shard_map/pallas_call | solution.py:336
  48.6 9.9 %shard_map.79 = (f32[2,256,256]{2,1,0:T(8,128)S(1)}, f32[2,256,256]{2,1,0:T(8,128)S(1)}, f32[2,2,256,256]{3,2,1,0:T(8,128)}, f32[2,2,256,256]{3,2,1,0:T(8,128)S(1)}) custom-call(s32[4]{0:T(128)S(1)} %pad_add_fusion.place, f32[2,256,256]{2,1,0:T(8,128)S(1)} %get-tuple-element.46.mine, f32[2,256,256]{2,1,0:T(8,128)S(1)} %collective-permute-done.2.other, ...), custom_call_target="tpu_custom_call" | custom-call | flops 9663676416 | bytes 4194304 | tf_op jit(solution)/shard_map/pallas_call | solution.py:336
  60.1 2.5 %collective-permute-start.5 = (f32[2,256,256]{2,1,0:T(8,128)S(1)}, f32[2,256,256]{2,1,0:T(8,128)S(1)}, u32[]{:S(2)}, u32[]{:S(2)}) collective-permute-start(f32[2,256,256]{2,1,0:T(8,128)S(1)} %get-tuple-element.30), channel_id=1, source_target_pairs={{0,8},{1,249},{2,10},{3,251},{4,12},{5,253},{6,14},{7,255},{8,16},... | collective-permute-start | bytes 1572872 | tf_op jit(solution)/shard_map/ppermute | solution.py:501
  67.1 2.6 %collective-permute-start.9 = (f32[256,256]{1,0:T(8,128)S(1)}, f32[256,256]{1,0:T(8,128)S(1)}, u32[]{:S(2)}, u32[]{:S(2)}) collective-permute-start(f32[256,256]{1,0:T(8,128)S(1)} %get-tuple-element.50), channel_id=1, source_target_pairs={{0,128},{64,192},{128,0},{192,64},{1,129},{65,193},{129,1},{193,65... | collective-permute-start | bytes 786440 | tf_op jit(solution)/shard_map/ppermute | solution.py:439
  69.9 10.3 %collective-permute-start.13 = (f32[2,256,256]{2,1,0:T(8,128)S(1)}, f32[2,256,256]{2,1,0:T(8,128)}, u32[]{:S(2)}, u32[]{:S(2)}) collective-permute-start(f32[2,256,256]{2,1,0:T(8,128)S(1)} %select_add_fusion.1), channel_id=1, source_target_pairs={{0,1},{1,2},{2,3},{3,4},{4,5},{5,6},{6,7},{8,9},{9,10},{10,11},{11... | collective-permute-start | bytes 1572872 | tf_op jit(solution)/shard_map/ppermute | solution.py:430
  80.2 4.0 %collective-permute-start.7 = (f32[2,256,256]{2,1,0:T(8,128)S(1)}, f32[2,256,256]{2,1,0:T(8,128)S(1)}, u32[]{:S(2)}, u32[]{:S(2)}) collective-permute-start(f32[2,256,256]{2,1,0:T(8,128)S(1)} %get-tuple-element.34), channel_id=1, source_target_pairs={{0,8},{1,249},{2,10},{3,251},{4,12},{5,253},{6,14},{7,255},{8,16},... | collective-permute-start | bytes 1572872 | tf_op jit(solution)/shard_map/ppermute | solution.py:501
  84.7 3.4 %collective-permute-done.11 = f32[64,256]{1,0:T(8,128)S(1)} collective-permute-done((f32[64,256]{1,0:T(8,128)S(1)}, f32[64,256]{1,0:T(8,128)S(1)}, u32[]{:S(2)}, u32[]{:S(2)}) %collective-permute-start.11) | collective-permute-done | bytes 65568 | tf_op jit(solution)/shard_map/ppermute | solution.py:439
  88.4 3.6 %collective-permute-done.13 = f32[2,256,256]{2,1,0:T(8,128)} collective-permute-done((f32[2,256,256]{2,1,0:T(8,128)S(1)}, f32[2,256,256]{2,1,0:T(8,128)}, u32[]{:S(2)}, u32[]{:S(2)}) %collective-permute-start.13) | collective-permute-done | bytes 524320 | tf_op jit(solution)/shard_map/ppermute | solution.py:430
  92.5 5.1 %collective-permute-done.7 = f32[2,256,256]{2,1,0:T(8,128)S(1)} collective-permute-done((f32[2,256,256]{2,1,0:T(8,128)S(1)}, f32[2,256,256]{2,1,0:T(8,128)S(1)}, u32[]{:S(2)}, u32[]{:S(2)}) %collective-permute-start.7) | collective-permute-done | bytes 524320 | tf_op jit(solution)/shard_map/ppermute | solution.py:501
  99.3 6.1 %collective-permute-start.16 = (f32[64,256]{1,0:T(8,128)S(1)}, f32[64,256]{1,0:T(8,128)S(1)}, u32[]{:S(2)}, u32[]{:S(2)}) collective-permute-start(f32[64,256]{1,0:T(8,128)S(1)} %bitcast_add_fusion), channel_id=1, source_target_pairs={{0,16},{1,17},{16,0},{17,1},{32,48},{33,49},{48,32},{49,33},{2,18}... | collective-permute-start | bytes 196616 | tf_op jit(solution)/shard_map/ppermute | solution.py:484
  105.4 2.3 %collective-permute-done.16 = f32[64,256]{1,0:T(8,128)S(1)} collective-permute-done((f32[64,256]{1,0:T(8,128)S(1)}, f32[64,256]{1,0:T(8,128)S(1)}, u32[]{:S(2)}, u32[]{:S(2)}) %collective-permute-start.16) | collective-permute-done | bytes 65568 | tf_op jit(solution)/shard_map/ppermute | solution.py:484
  107.8 2.6 %collective-permute-done.17 = f32[64,256]{1,0:T(8,128)S(1)} collective-permute-done((f32[64,256]{1,0:T(8,128)S(1)}, f32[64,256]{1,0:T(8,128)S(1)}, u32[]{:S(2)}, u32[]{:S(2)}) %collective-permute-start.17) | collective-permute-done | bytes 65568 | tf_op jit(solution)/shard_map/ppermute | solution.py:484
  110.5 7.0 %collective-permute-done.18 = f32[64,256]{1,0:T(8,128)S(1)} collective-permute-done((f32[64,256]{1,0:T(8,128)S(1)}, f32[64,256]{1,0:T(8,128)S(1)}, u32[]{:S(2)}, u32[]{:S(2)}) %collective-permute-start.18) | collective-permute-done | bytes 65568 | tf_op jit(solution)/shard_map/ppermute | solution.py:484
  117.6 4.5 %collective-permute-start.20 = (f32[64,256]{1,0:T(8,128)S(1)}, f32[64,256]{1,0:T(8,128)S(1)}, u32[]{:S(2)}, u32[]{:S(2)}) collective-permute-start(f32[64,256]{1,0:T(8,128)S(1)} %get-tuple-element.41), channel_id=1, source_target_pairs={{0,4},{2,6},{4,0},{6,2},{1,5},{3,7},{5,1},{7,3},{8,12},{10,14},{12... | collective-permute-start | bytes 196616 | tf_op jit(solution)/shard_map/ppermute | solution.py:439
  130.6 2.7 %collective-permute-done.23 = f32[256,256]{1,0:T(8,128)S(1)} collective-permute-done((f32[256,256]{1,0:T(8,128)S(1)}, f32[256,256]{1,0:T(8,128)S(1)}, u32[]{:S(2)}, u32[]{:S(2)}) %collective-permute-start.23) | collective-permute-done | bytes 262176 | tf_op jit(solution)/shard_map/ppermute | solution.py:439
  133.4 2.1 %collective-permute-done.25 = f32[256,256]{1,0:T(8,128)S(1)} collective-permute-done((f32[256,256]{1,0:T(8,128)S(1)}, f32[256,256]{1,0:T(8,128)S(1)}, u32[]{:S(2)}, u32[]{:S(2)}) %collective-permute-start.25) | collective-permute-done | bytes 262176 | tf_op jit(solution)/shard_map/ppermute | solution.py:439
  135.5 4.3 %collective-permute-done.22 = f32[2,256,256]{2,1,0:T(8,128)} collective-permute-done((f32[2,256,256]{2,1,0:T(8,128)S(1)}, f32[2,256,256]{2,1,0:T(8,128)}, u32[]{:S(2)}, u32[]{:S(2)}) %collective-permute-start.22) | collective-permute-done | bytes 524320 | tf_op jit(solution)/shard_map/ppermute | solution.py:430
  139.7 17.6 %collective-permute-start.26 = (f32[1024,256]{1,0:T(8,128)S(1)}, f32[1024,256]{1,0:T(8,128)}, u32[]{:S(2)}, u32[]{:S(2)}) collective-permute-start(f32[1024,256]{1,0:T(8,128)S(1)} %bitcast.71), channel_id=1, source_target_pairs={{0,8},{8,0},{1,9},{9,1},{2,10},{10,2},{3,11},{11,3},{4,12},{12,4},... | collective-permute-start | bytes 3145736 | tf_op jit(solution)/shard_map/ppermute | solution.py:549
  (82 shorter events, 30.5 us)
Async XLA Ops:
  3.3 23.6 %collective-permute-start.1 = (f32[2,2,256,256]{3,2,1,0:T(8,128)}, f32[2,2,256,256]{3,2,1,0:T(8,128)}, u32[]{:S(2)}, u32[]{:S(2)}) collective-permute-start(f32[2,2,256,256]{3,2,1,0:T(8,128)} %param.6), channel_id=1, source_target_pairs={{1,0},{2,1},{3,2},{4,3},{5,4},{6,5},{7,6},{9,8},{10,9},{11,10},{12... | collective-permute-start | bytes 3145736 | tf_op jit(solution)/shard_map/ppermute | solution.py:430
  29.7 13.2 %collective-permute-start.3 = (f32[2,256,256]{2,1,0:T(8,128)}, f32[2,256,256]{2,1,0:T(8,128)}, u32[]{:S(2)}, u32[]{:S(2)}) collective-permute-start(f32[2,256,256]{2,1,0:T(8,128)} %get-tuple-element.42), channel_id=1, source_target_pairs={{1,9},{3,11},{5,13},{7,15},{8,0},{9,17},{10,2},{11,19},{12,4},{13,... | collective-permute-start | bytes 1572872 | tf_op jit(solution)/shard_map/ppermute | solution.py:501
  35.8 12.7 %collective-permute-start.2 = (f32[2,256,256]{2,1,0:T(8,128)}, f32[2,256,256]{2,1,0:T(8,128)S(1)}, u32[]{:S(2)}, u32[]{:S(2)}) collective-permute-start(f32[2,256,256]{2,1,0:T(8,128)} %get-tuple-element.43), channel_id=1, source_target_pairs={{1,9},{3,11},{5,13},{7,15},{8,0},{9,17},{10,2},{11,19},{12,4},{13,... | collective-permute-start | bytes 1572872 | tf_op jit(solution)/shard_map/ppermute | solution.py:501
  40.8 7.8 %collective-permute-start.4 = (f32[1,256,256]{2,1,0:T(8,128)S(1)}, f32[1,256,256]{2,1,0:T(8,128)S(1)}, u32[]{:S(2)}, u32[]{:S(2)}) collective-permute-start(f32[1,256,256]{2,1,0:T(8,128)S(1)} %copy-done.6), channel_id=1, source_target_pairs={{0,0},{1,9},{2,2},{3,11},{4,4},{5,13},{6,6},{7,15},{8,8},{9,17},{1... | collective-permute-start | bytes 786440 | tf_op jit(solution)/shard_map/ppermute | solution.py:501
  58.5 5.4 %collective-permute-start.6 = (f32[2,2,256,256]{3,2,1,0:T(8,128)}, f32[2,2,256,256]{3,2,1,0:T(8,128)}, u32[]{:S(2)}, u32[]{:S(2)}) collective-permute-start(f32[2,2,256,256]{3,2,1,0:T(8,128)} %get-tuple-element.32), channel_id=1, source_target_pairs={{0,8},{8,0},{1,9},{9,1},{2,10},{10,2},{3,11},{11,3},{4,12},{12,4},... | collective-permute-start | bytes 3145736 | tf_op jit(solution)/shard_map/ppermute | solution.py:536
  60.1 9.7 %collective-permute-start.5 = (f32[2,256,256]{2,1,0:T(8,128)S(1)}, f32[2,256,256]{2,1,0:T(8,128)S(1)}, u32[]{:S(2)}, u32[]{:S(2)}) collective-permute-start(f32[2,256,256]{2,1,0:T(8,128)S(1)} %get-tuple-element.30), channel_id=1, source_target_pairs={{0,8},{1,249},{2,10},{3,251},{4,12},{5,253},{6,14},{7,255},{8,16},... | collective-permute-start | bytes 1572872 | tf_op jit(solution)/shard_map/ppermute | solution.py:501
  65.4 18.8 %collective-permute-start.10 = (f32[256,256]{1,0:T(8,128)S(1)}, f32[256,256]{1,0:T(8,128)S(1)}, u32[]{:S(2)}, u32[]{:S(2)}) collective-permute-start(f32[256,256]{1,0:T(8,128)S(1)} %get-tuple-element.49), channel_id=1, source_target_pairs={{0,192},{64,0},{128,64},{192,128},{1,193},{65,1},{129,65},{193,129... | collective-permute-start | bytes 786440 | tf_op jit(solution)/shard_map/ppermute | solution.py:439
  65.8 18.4 %collective-permute-start.8 = (f32[256,256]{1,0:T(8,128)S(1)}, f32[256,256]{1,0:T(8,128)S(1)}, u32[]{:S(2)}, u32[]{:S(2)}) collective-permute-start(f32[256,256]{1,0:T(8,128)S(1)} %get-tuple-element.51), channel_id=1, source_target_pairs={{0,64},{64,128},{128,192},{192,0},{1,65},{65,129},{129,193},{193,1... | collective-permute-start | bytes 786440 | tf_op jit(solution)/shard_map/ppermute | solution.py:439
  67.1 17.1 %collective-permute-start.9 = (f32[256,256]{1,0:T(8,128)S(1)}, f32[256,256]{1,0:T(8,128)S(1)}, u32[]{:S(2)}, u32[]{:S(2)}) collective-permute-start(f32[256,256]{1,0:T(8,128)S(1)} %get-tuple-element.50), channel_id=1, source_target_pairs={{0,128},{64,192},{128,0},{192,64},{1,129},{65,193},{129,1},{193,65... | collective-permute-start | bytes 786440 | tf_op jit(solution)/shard_map/ppermute | solution.py:439
  69.9 22.0 %collective-permute-start.13 = (f32[2,256,256]{2,1,0:T(8,128)S(1)}, f32[2,256,256]{2,1,0:T(8,128)}, u32[]{:S(2)}, u32[]{:S(2)}) collective-permute-start(f32[2,256,256]{2,1,0:T(8,128)S(1)} %select_add_fusion.1), channel_id=1, source_target_pairs={{0,1},{1,2},{2,3},{3,4},{4,5},{5,6},{6,7},{8,9},{9,10},{10,11},{11... | collective-permute-start | bytes 1572872 | tf_op jit(solution)/shard_map/ppermute | solution.py:430
  80.2 17.3 %collective-permute-start.7 = (f32[2,256,256]{2,1,0:T(8,128)S(1)}, f32[2,256,256]{2,1,0:T(8,128)S(1)}, u32[]{:S(2)}, u32[]{:S(2)}) collective-permute-start(f32[2,256,256]{2,1,0:T(8,128)S(1)} %get-tuple-element.34), channel_id=1, source_target_pairs={{0,8},{1,249},{2,10},{3,251},{4,12},{5,253},{6,14},{7,255},{8,16},... | collective-permute-start | bytes 1572872 | tf_op jit(solution)/shard_map/ppermute | solution.py:501
  88.0 4.1 %collective-permute-start.12 = (f32[64,256]{1,0:T(8,128)S(1)}, f32[64,256]{1,0:T(8,128)S(1)}, u32[]{:S(2)}, u32[]{:S(2)}) collective-permute-start(f32[64,256]{1,0:T(8,128)S(1)} %bitcast_add_fusion.1), channel_id=1, source_target_pairs={{0,6},{2,0},{4,2},{6,4},{1,7},{3,1},{5,3},{7,5},{8,14},{10,8},{12,... | collective-permute-start | bytes 196616 | tf_op jit(solution)/shard_map/ppermute | solution.py:439
  92.2 5.6 %collective-permute-start.14 = (f32[64,256]{1,0:T(8,128)S(1)}, f32[64,256]{1,0:T(8,128)S(1)}, u32[]{:S(2)}, u32[]{:S(2)}) collective-permute-start(f32[64,256]{1,0:T(8,128)S(1)} %add.152), channel_id=1, source_target_pairs={{0,6},{2,0},{4,2},{6,4},{1,7},{3,1},{5,3},{7,5},{8,14},{10,8},{12,... | collective-permute-start | bytes 196616 | tf_op jit(solution)/shard_map/ppermute | solution.py:439
  97.8 7.6 %collective-permute-start.15 = (f32[64,256]{1,0:T(8,128)S(1)}, f32[64,256]{1,0:T(8,128)S(1)}, u32[]{:S(2)}, u32[]{:S(2)}) collective-permute-start(f32[64,256]{1,0:T(8,128)S(1)} %bitcast_add_fusion), channel_id=1, source_target_pairs={{0,1},{1,0},{16,17},{17,16},{32,33},{33,32},{48,49},{49,48},{2,3},... | collective-permute-start | bytes 196616 | tf_op jit(solution)/shard_map/ppermute | solution.py:484
  99.3 8.4 %collective-permute-start.16 = (f32[64,256]{1,0:T(8,128)S(1)}, f32[64,256]{1,0:T(8,128)S(1)}, u32[]{:S(2)}, u32[]{:S(2)}) collective-permute-start(f32[64,256]{1,0:T(8,128)S(1)} %bitcast_add_fusion), channel_id=1, source_target_pairs={{0,16},{1,17},{16,0},{17,1},{32,48},{33,49},{48,32},{49,33},{2,18}... | collective-permute-start | bytes 196616 | tf_op jit(solution)/shard_map/ppermute | solution.py:484
  105.4 4.9 %collective-permute-start.17 = (f32[64,256]{1,0:T(8,128)S(1)}, f32[64,256]{1,0:T(8,128)S(1)}, u32[]{:S(2)}, u32[]{:S(2)}) collective-permute-start(f32[64,256]{1,0:T(8,128)S(1)} %bitcast_add_fusion), channel_id=1, source_target_pairs={{0,17},{1,16},{16,1},{17,0},{32,49},{33,48},{48,33},{49,32},{2,19}... | collective-permute-start | bytes 196616 | tf_op jit(solution)/shard_map/ppermute | solution.py:484
  110.4 7.1 %collective-permute-start.18 = (f32[64,256]{1,0:T(8,128)S(1)}, f32[64,256]{1,0:T(8,128)S(1)}, u32[]{:S(2)}, u32[]{:S(2)}) collective-permute-start(f32[64,256]{1,0:T(8,128)S(1)} %add_add_fusion.1), channel_id=1, source_target_pairs={{0,32},{1,33},{16,48},{17,49},{32,0},{33,1},{48,16},{49,17},{2,34}... | collective-permute-start | bytes 196616 | tf_op jit(solution)/shard_map/ppermute | solution.py:484
  117.5 4.6 %collective-permute-start.19 = (f32[64,256]{1,0:T(8,128)S(1)}, f32[64,256]{1,0:T(8,128)S(1)}, u32[]{:S(2)}, u32[]{:S(2)}) collective-permute-start(f32[64,256]{1,0:T(8,128)S(1)} %get-tuple-element.41), channel_id=1, source_target_pairs={{0,6},{2,0},{4,2},{6,4},{1,7},{3,1},{5,3},{7,5},{8,14},{10,8},{12,... | collective-permute-start | bytes 196616 | tf_op jit(solution)/shard_map/ppermute | solution.py:439
  117.6 6.4 %collective-permute-start.20 = (f32[64,256]{1,0:T(8,128)S(1)}, f32[64,256]{1,0:T(8,128)S(1)}, u32[]{:S(2)}, u32[]{:S(2)}) collective-permute-start(f32[64,256]{1,0:T(8,128)S(1)} %get-tuple-element.41), channel_id=1, source_target_pairs={{0,4},{2,6},{4,0},{6,2},{1,5},{3,7},{5,1},{7,3},{8,12},{10,14},{12... | collective-permute-start | bytes 196616 | tf_op jit(solution)/shard_map/ppermute | solution.py:439
  125.2 8.1 %collective-permute-start.23 = (f32[256,256]{1,0:T(8,128)S(1)}, f32[256,256]{1,0:T(8,128)S(1)}, u32[]{:S(2)}, u32[]{:S(2)}) collective-permute-start(f32[256,256]{1,0:T(8,128)S(1)} %bitcast.77), channel_id=1, source_target_pairs={{0,192},{64,0},{128,64},{192,128},{1,193},{65,1},{129,65},{193,129... | collective-permute-start | bytes 786440 | tf_op jit(solution)/shard_map/ppermute | solution.py:439
  125.3 8.0 %collective-permute-start.24 = (f32[256,256]{1,0:T(8,128)S(1)}, f32[256,256]{1,0:T(8,128)S(1)}, u32[]{:S(2)}, u32[]{:S(2)}) collective-permute-start(f32[256,256]{1,0:T(8,128)S(1)} %bitcast.78), channel_id=1, source_target_pairs={{0,128},{64,192},{128,0},{192,64},{1,129},{65,193},{129,1},{193,65... | collective-permute-start | bytes 786440 | tf_op jit(solution)/shard_map/ppermute | solution.py:439
  126.6 8.8 %collective-permute-start.25 = (f32[256,256]{1,0:T(8,128)S(1)}, f32[256,256]{1,0:T(8,128)S(1)}, u32[]{:S(2)}, u32[]{:S(2)}) collective-permute-start(f32[256,256]{1,0:T(8,128)S(1)} %bitcast.79), channel_id=1, source_target_pairs={{0,64},{64,128},{128,192},{192,0},{1,65},{65,129},{129,193},{193,1... | collective-permute-start | bytes 786440 | tf_op jit(solution)/shard_map/ppermute | solution.py:439
  128.7 11.0 %collective-permute-start.22 = (f32[2,256,256]{2,1,0:T(8,128)S(1)}, f32[2,256,256]{2,1,0:T(8,128)}, u32[]{:S(2)}, u32[]{:S(2)}) collective-permute-start(f32[2,256,256]{2,1,0:T(8,128)S(1)} %select_add_fusion), channel_id=1, source_target_pairs={{0,1},{1,2},{2,3},{3,4},{4,5},{5,6},{6,7},{8,9},{9,10},{10,11},{11... | collective-permute-start | bytes 1572872 | tf_op jit(solution)/shard_map/ppermute | solution.py:430
  139.7 20.3 %collective-permute-start.26 = (f32[1024,256]{1,0:T(8,128)S(1)}, f32[1024,256]{1,0:T(8,128)}, u32[]{:S(2)}, u32[]{:S(2)}) collective-permute-start(f32[1024,256]{1,0:T(8,128)S(1)} %bitcast.71), channel_id=1, source_target_pairs={{0,8},{8,0},{1,9},{9,1},{2,10},{10,2},{3,11},{11,3},{4,12},{12,4},... | collective-permute-start | bytes 3145736 | tf_op jit(solution)/shard_map/ppermute | solution.py:549
  (10 other events, 65.7 us)

commit v10 on v9

--- a/solution.py
+++ b/solution.py
@@ -239,9 +239,12 @@
     return [(jnp.zeros((CH, H), F32), jnp.zeros((CH, H), F32))] * 4
 
 
-def first_kernel(place, mine, other, probes, table, q1, obj, op, mid, out):
+def first_kernel(place, mine, other, source, table, q1, obj, op, mid, out, probes, arrived):
     modes = probes.shape[0]
+    copy = pltpu.make_async_copy(source, probes, arrived)
+    copy.start()
     obj[0], obj[1] = window_of(place, mine, other)
+    copy.wait()
     for m in range(modes):
         for k in range(CHUNKS):
             row = k * CH
@@ -354,14 +357,22 @@
 
 def first(place, mine, other, probes, table):
     modes = probes.shape[0]
-    return call(
+    spec = pl.BlockSpec(memory_space=pltpu.VMEM)
+    scratch = [operand(modes)] + products_scratch(modes) + [(probes.shape, F32)]
+    return pl.pallas_call(
         first_kernel,
-        (place, mine, other, probes, table),
-        [(probes.shape, F32), ((2, N, N), F32)],
-        [operand(modes)] + products_scratch(modes),
-        3 << 30,
-        14,
-    )
+        in_specs=[pl.BlockSpec(memory_space=pltpu.SMEM), spec, spec]
+        + [pl.BlockSpec(memory_space=pl.ANY), spec],
+        out_specs=[spec, spec],
+        out_shape=[
+            jax.ShapeDtypeStruct(probes.shape, F32),
+            jax.ShapeDtypeStruct((2, N, N), F32),
+        ],
+        scratch_shapes=[pltpu.VMEM(shape, dtype) for shape, dtype in scratch]
+        + [pltpu.SemaphoreType.DMA],
+        compiler_params=pltpu.CompilerParams(vmem_limit_bytes=18 << 20),
+        cost_estimate=pl.CostEstimate(flops=3 << 30, bytes_accessed=4 << 20, transcendentals=0),
+    )(place, mine, other, probes, table)
 
 
 def second(place, mine, other, q1, amplitude, table, phases, probes, first_obj):

time: 164 us -> 164 us (level)
    pallas_call x0 -> x1, Pallas kernels: none -> 4.34 us  [first(): pl.pallas_call(first_kernel, in_specs=[pl.BlockSpec(memory_space=pltpu.SM...]
    pallas_call x2 -> x1, Pallas kernels: 14 us -> 10.4 us  [call(): pl.pallas_call(kernel, in_specs=[pl.BlockSpec(memory_space=pltpu.SMEM)] +...]
where the time goes in v10:
time: 164 us
  starting transfers between devices  73.2 us (45%)
  waiting for transfers between devices  48.4 us (30%)
  Pallas kernels  21.9 us (13%)
  other arithmetic  9.01 us (5%)
  between operations  6.31 us (4%)
  local copies, waits for them, and re-layouts  4.85 us (3%)
    ppermute x3, waiting for transfers between devices, shifted(): lax.ppermute(value, axes, [(source, source + steps) for source in range(f...  17.6 us
    ppermute x1, starting transfers between devices, per_device(): opposite = lax.ppermute(total, 'core', swap)  17.6 us
    ppermute x5, starting transfers between devices, moved(): return lax.ppermute(value, POS + TILE, pairs)  16.7 us
    ppermute x3, starting transfers between devices, shifted(): lax.ppermute(value, axes, [(source, source + steps) for source in range(f...  14.5 us
    ppermute x12, starting transfers between devices, ring(): lax.ppermute(value, axis, [(i, (i + step) % count) for i in range(count)])  13.3 us
    ppermute x4, waiting for transfers between devices, exchange(): return lax.ppermute(value, axes, [(i, i ^ bits) for i in range(count)])  12 us
    ppermute x12, waiting for transfers between devices, ring(): lax.ppermute(value, axis, [(i, (i + step) % count) for i in range(count)])  11.4 us
    pallas_call x1, Pallas kernels, call(): pl.pallas_call(kernel, in_specs=[pl.BlockSpec(memory_space=pltpu.SMEM)] +...  10.4 us
  transfers between devices with their start and end apart: 27, of which 15 were waited for; matrix products, arithmetic and copies ran while one was open for 4% of the time, Pallas kernels for 7%

profile of v10, /device:TPU:141, one launch (start us, length us, event | category | flops | bytes accessed | tf_op | source)
XLA Modules:
  0.0 163.7 jit_solution(6198238018132198895)
XLA Ops:
  3.3 2.6 %collective-permute-start.1 = (f32[2,2,256,256]{3,2,1,0:T(8,128)}, f32[2,2,256,256]{3,2,1,0:T(8,128)}, u32[]{:S(2)}, u32[]{:S(2)}) collective-permute-start(f32[2,2,256,256]{3,2,1,0:T(8,128)} %param.6), channel_id=1, source_target_pairs={{1,0},{2,1},{3,2},{4,3},{5,4},{6,5},{7,6},{9,8},{10,9},{11,10},{12... | collective-permute-start | bytes 3145736 | tf_op jit(solution)/shard_map/ppermute | solution.py:441
  6.0 7.2 %shard_map.77 = (f32[8,256,256]{2,1,0:T(8,128)}, bf16[5,2,256,256]{3,2,1,0:T(8,128)(2,1)}, f32[2,256,256]{2,1,0:T(8,128)}) custom-call(s32[1]{0:T(128)} %bitcast.8.core, f32[8,256,256]{2,1,0:T(8,128)} %bitcast.73, bf16[5,2,256,256]{3,2,1,0:T(8,128)(2,1)} %constant.82.clone.table, f32[2,256,256]{2,1,0:T(8,128)} %constant.83.clone.phases), custom_call_target="tpu_custom_call" | custom-call | tf_op jit(solution)/shard_map/pallas_call | solution.py:406
  17.1 9.8 %collective-permute-done.1 = f32[2,2,256,256]{3,2,1,0:T(8,128)} collective-permute-done((f32[2,2,256,256]{3,2,1,0:T(8,128)}, f32[2,2,256,256]{3,2,1,0:T(8,128)}, u32[]{:S(2)}, u32[]{:S(2)}) %collective-permute-start.1) | collective-permute-done | bytes 1048608 | tf_op jit(solution)/shard_map/ppermute | solution.py:441
  26.9 2.8 %bitcast_select_fusion = (f32[2,256,256]{2,1,0:T(8,128)}, f32[2,256,256]{2,1,0:T(8,128)}, f32[2,256,256]{2,1,0:T(8,128)S(1)}, f32[2,256,256]{2,1,0:T(8,128)S(1)}) fusion(f32[2,2,256,256]{3,2,1,0:T(8,128)} %param.6, f32[2,2,256,256]{3,2,1,0:T(8,128)} %collective-permute-done.1, pred[256]{0:T(512)(128)(4,1)S(1)} %get-tuple-element.62, ...), kind=kLoop, calls=%fused_computation.2 | loop fusion | flops 524288 | bytes 4194816 | tf_op jit(solution)/shard_map/jit(_where)/select_n | solution.py:529
  29.7 6.1 %collective-permute-start.3 = (f32[2,256,256]{2,1,0:T(8,128)}, f32[2,256,256]{2,1,0:T(8,128)}, u32[]{:S(2)}, u32[]{:S(2)}) collective-permute-start(f32[2,256,256]{2,1,0:T(8,128)} %get-tuple-element.42), channel_id=1, source_target_pairs={{1,9},{3,11},{5,13},{7,15},{8,0},{9,17},{10,2},{11,19},{12,4},{13,... | collective-permute-start | bytes 1572872 | tf_op jit(solution)/shard_map/ppermute | solution.py:512
  35.8 3.5 %collective-permute-start.2 = (f32[2,256,256]{2,1,0:T(8,128)}, f32[2,256,256]{2,1,0:T(8,128)S(1)}, u32[]{:S(2)}, u32[]{:S(2)}) collective-permute-start(f32[2,256,256]{2,1,0:T(8,128)} %get-tuple-element.43), channel_id=1, source_target_pairs={{1,9},{3,11},{5,13},{7,15},{8,0},{9,17},{10,2},{11,19},{12,4},{13,... | collective-permute-start | bytes 1572872 | tf_op jit(solution)/shard_map/ppermute | solution.py:512
  44.5 4.3 %shard_map.78 = (f32[4,2,256,256]{3,2,1,0:T(8,128)S(1)}, f32[2,256,256]{2,1,0:T(8,128)S(1)}) custom-call(s32[4]{0:T(128)S(1)} %pad_add_fusion.place, f32[2,256,256]{2,1,0:T(8,128)S(1)} %get-tuple-element.47.mine, f32[2,256,256]{2,1,0:T(8,128)} %collective-permute-done.3.other, f32[4,2,256,256]{3,2,1,0:T(8,128)S(1)} %bitcast.66, ...), custom_call_target="tpu_custom_call" | custom-call | flops 3221225472 | bytes 4194304 | tf_op jit(solution)/shard_map/pallas_call | solution.py:362
  48.9 10.4 %shard_map.79 = (f32[2,256,256]{2,1,0:T(8,128)S(1)}, f32[2,256,256]{2,1,0:T(8,128)S(1)}, f32[2,2,256,256]{3,2,1,0:T(8,128)}, f32[2,2,256,256]{3,2,1,0:T(8,128)S(1)}) custom-call(s32[4]{0:T(128)S(1)} %pad_add_fusion.place, f32[2,256,256]{2,1,0:T(8,128)S(1)} %get-tuple-element.46.mine, f32[2,256,256]{2,1,0:T(8,128)S(1)} %collective-permute-done.2.other, ...), custom_call_target="tpu_custom_call" | custom-call | flops 9663676416 | bytes 4194304 | tf_op jit(solution)/shard_map/pallas_call | solution.py:339
  60.8 2.5 %collective-permute-start.5 = (f32[2,256,256]{2,1,0:T(8,128)S(1)}, f32[2,256,256]{2,1,0:T(8,128)S(1)}, u32[]{:S(2)}, u32[]{:S(2)}) collective-permute-start(f32[2,256,256]{2,1,0:T(8,128)S(1)} %get-tuple-element.30), channel_id=1, source_target_pairs={{0,8},{1,249},{2,10},{3,251},{4,12},{5,253},{6,14},{7,255},{8,16},... | collective-permute-start | bytes 1572872 | tf_op jit(solution)/shard_map/ppermute | solution.py:512
  67.8 2.6 %collective-permute-start.9 = (f32[256,256]{1,0:T(8,128)S(1)}, f32[256,256]{1,0:T(8,128)S(1)}, u32[]{:S(2)}, u32[]{:S(2)}) collective-permute-start(f32[256,256]{1,0:T(8,128)S(1)} %get-tuple-element.50), channel_id=1, source_target_pairs={{0,128},{64,192},{128,0},{192,64},{1,129},{65,193},{129,1},{193,65... | collective-permute-start | bytes 786440 | tf_op jit(solution)/shard_map/ppermute | solution.py:450
  70.7 10.0 %collective-permute-start.13 = (f32[2,256,256]{2,1,0:T(8,128)S(1)}, f32[2,256,256]{2,1,0:T(8,128)}, u32[]{:S(2)}, u32[]{:S(2)}) collective-permute-start(f32[2,256,256]{2,1,0:T(8,128)S(1)} %select_add_fusion.1), channel_id=1, source_target_pairs={{0,1},{1,2},{2,3},{3,4},{4,5},{5,6},{6,7},{8,9},{9,10},{10,11},{11... | collective-permute-start | bytes 1572872 | tf_op jit(solution)/shard_map/ppermute | solution.py:441
  80.7 4.0 %collective-permute-start.7 = (f32[2,256,256]{2,1,0:T(8,128)S(1)}, f32[2,256,256]{2,1,0:T(8,128)S(1)}, u32[]{:S(2)}, u32[]{:S(2)}) collective-permute-start(f32[2,256,256]{2,1,0:T(8,128)S(1)} %get-tuple-element.34), channel_id=1, source_target_pairs={{0,8},{1,249},{2,10},{3,251},{4,12},{5,253},{6,14},{7,255},{8,16},... | collective-permute-start | bytes 1572872 | tf_op jit(solution)/shard_map/ppermute | solution.py:512
  85.1 3.4 %collective-permute-done.11 = f32[64,256]{1,0:T(8,128)S(1)} collective-permute-done((f32[64,256]{1,0:T(8,128)S(1)}, f32[64,256]{1,0:T(8,128)S(1)}, u32[]{:S(2)}, u32[]{:S(2)}) %collective-permute-start.11) | collective-permute-done | bytes 65568 | tf_op jit(solution)/shard_map/ppermute | solution.py:450
  88.8 3.5 %collective-permute-done.13 = f32[2,256,256]{2,1,0:T(8,128)} collective-permute-done((f32[2,256,256]{2,1,0:T(8,128)S(1)}, f32[2,256,256]{2,1,0:T(8,128)}, u32[]{:S(2)}, u32[]{:S(2)}) %collective-permute-start.13) | collective-permute-done | bytes 524320 | tf_op jit(solution)/shard_map/ppermute | solution.py:441
  92.9 5.1 %collective-permute-done.7 = f32[2,256,256]{2,1,0:T(8,128)S(1)} collective-permute-done((f32[2,256,256]{2,1,0:T(8,128)S(1)}, f32[2,256,256]{2,1,0:T(8,128)S(1)}, u32[]{:S(2)}, u32[]{:S(2)}) %collective-permute-start.7) | collective-permute-done | bytes 524320 | tf_op jit(solution)/shard_map/ppermute | solution.py:512
  99.8 6.1 %collective-permute-start.16 = (f32[64,256]{1,0:T(8,128)S(1)}, f32[64,256]{1,0:T(8,128)S(1)}, u32[]{:S(2)}, u32[]{:S(2)}) collective-permute-start(f32[64,256]{1,0:T(8,128)S(1)} %bitcast_add_fusion), channel_id=1, source_target_pairs={{0,16},{1,17},{16,0},{17,1},{32,48},{33,49},{48,32},{49,33},{2,18}... | collective-permute-start | bytes 196616 | tf_op jit(solution)/shard_map/ppermute | solution.py:495
  105.9 2.3 %collective-permute-done.16 = f32[64,256]{1,0:T(8,128)S(1)} collective-permute-done((f32[64,256]{1,0:T(8,128)S(1)}, f32[64,256]{1,0:T(8,128)S(1)}, u32[]{:S(2)}, u32[]{:S(2)}) %collective-permute-start.16) | collective-permute-done | bytes 65568 | tf_op jit(solution)/shard_map/ppermute | solution.py:495
  108.2 2.6 %collective-permute-done.17 = f32[64,256]{1,0:T(8,128)S(1)} collective-permute-done((f32[64,256]{1,0:T(8,128)S(1)}, f32[64,256]{1,0:T(8,128)S(1)}, u32[]{:S(2)}, u32[]{:S(2)}) %collective-permute-start.17) | collective-permute-done | bytes 65568 | tf_op jit(solution)/shard_map/ppermute | solution.py:495
  110.9 7.0 %collective-permute-done.18 = f32[64,256]{1,0:T(8,128)S(1)} collective-permute-done((f32[64,256]{1,0:T(8,128)S(1)}, f32[64,256]{1,0:T(8,128)S(1)}, u32[]{:S(2)}, u32[]{:S(2)}) %collective-permute-start.18) | collective-permute-done | bytes 65568 | tf_op jit(solution)/shard_map/ppermute | solution.py:495
  118.1 4.5 %collective-permute-start.20 = (f32[64,256]{1,0:T(8,128)S(1)}, f32[64,256]{1,0:T(8,128)S(1)}, u32[]{:S(2)}, u32[]{:S(2)}) collective-permute-start(f32[64,256]{1,0:T(8,128)S(1)} %get-tuple-element.41), channel_id=1, source_target_pairs={{0,4},{2,6},{4,0},{6,2},{1,5},{3,7},{5,1},{7,3},{8,12},{10,14},{12... | collective-permute-start | bytes 196616 | tf_op jit(solution)/shard_map/ppermute | solution.py:450
  131.1 2.7 %collective-permute-done.23 = f32[256,256]{1,0:T(8,128)S(1)} collective-permute-done((f32[256,256]{1,0:T(8,128)S(1)}, f32[256,256]{1,0:T(8,128)S(1)}, u32[]{:S(2)}, u32[]{:S(2)}) %collective-permute-start.23) | collective-permute-done | bytes 262176 | tf_op jit(solution)/shard_map/ppermute | solution.py:450
  133.8 2.1 %collective-permute-done.25 = f32[256,256]{1,0:T(8,128)S(1)} collective-permute-done((f32[256,256]{1,0:T(8,128)S(1)}, f32[256,256]{1,0:T(8,128)S(1)}, u32[]{:S(2)}, u32[]{:S(2)}) %collective-permute-start.25) | collective-permute-done | bytes 262176 | tf_op jit(solution)/shard_map/ppermute | solution.py:450
  135.9 4.3 %collective-permute-done.22 = f32[2,256,256]{2,1,0:T(8,128)} collective-permute-done((f32[2,256,256]{2,1,0:T(8,128)S(1)}, f32[2,256,256]{2,1,0:T(8,128)}, u32[]{:S(2)}, u32[]{:S(2)}) %collective-permute-start.22) | collective-permute-done | bytes 524320 | tf_op jit(solution)/shard_map/ppermute | solution.py:441
  140.2 17.6 %collective-permute-start.26 = (f32[1024,256]{1,0:T(8,128)S(1)}, f32[1024,256]{1,0:T(8,128)}, u32[]{:S(2)}, u32[]{:S(2)}) collective-permute-start(f32[1024,256]{1,0:T(8,128)S(1)} %bitcast.71), channel_id=1, source_target_pairs={{0,8},{8,0},{1,9},{9,1},{2,10},{10,2},{3,11},{11,3},{4,12},{12,4},... | collective-permute-start | bytes 3145736 | tf_op jit(solution)/shard_map/ppermute | solution.py:560
  (82 shorter events, 30.5 us)
Async XLA Ops:
  3.3 23.6 %collective-permute-start.1 = (f32[2,2,256,256]{3,2,1,0:T(8,128)}, f32[2,2,256,256]{3,2,1,0:T(8,128)}, u32[]{:S(2)}, u32[]{:S(2)}) collective-permute-start(f32[2,2,256,256]{3,2,1,0:T(8,128)} %param.6), channel_id=1, source_target_pairs={{1,0},{2,1},{3,2},{4,3},{5,4},{6,5},{7,6},{9,8},{10,9},{11,10},{12... | collective-permute-start | bytes 3145736 | tf_op jit(solution)/shard_map/ppermute | solution.py:441
  29.7 13.2 %collective-permute-start.3 = (f32[2,256,256]{2,1,0:T(8,128)}, f32[2,256,256]{2,1,0:T(8,128)}, u32[]{:S(2)}, u32[]{:S(2)}) collective-permute-start(f32[2,256,256]{2,1,0:T(8,128)} %get-tuple-element.42), channel_id=1, source_target_pairs={{1,9},{3,11},{5,13},{7,15},{8,0},{9,17},{10,2},{11,19},{12,4},{13,... | collective-permute-start | bytes 1572872 | tf_op jit(solution)/shard_map/ppermute | solution.py:512
  35.8 13.0 %collective-permute-start.2 = (f32[2,256,256]{2,1,0:T(8,128)}, f32[2,256,256]{2,1,0:T(8,128)S(1)}, u32[]{:S(2)}, u32[]{:S(2)}) collective-permute-start(f32[2,256,256]{2,1,0:T(8,128)} %get-tuple-element.43), channel_id=1, source_target_pairs={{1,9},{3,11},{5,13},{7,15},{8,0},{9,17},{10,2},{11,19},{12,4},{13,... | collective-permute-start | bytes 1572872 | tf_op jit(solution)/shard_map/ppermute | solution.py:512
  40.8 8.1 %collective-permute-start.4 = (f32[1,256,256]{2,1,0:T(8,128)S(1)}, f32[1,256,256]{2,1,0:T(8,128)S(1)}, u32[]{:S(2)}, u32[]{:S(2)}) collective-permute-start(f32[1,256,256]{2,1,0:T(8,128)S(1)} %copy-done.6), channel_id=1, source_target_pairs={{0,0},{1,9},{2,2},{3,11},{4,4},{5,13},{6,6},{7,15},{8,8},{9,17},{1... | collective-permute-start | bytes 786440 | tf_op jit(solution)/shard_map/ppermute | solution.py:512
  59.3 5.4 %collective-permute-start.6 = (f32[2,2,256,256]{3,2,1,0:T(8,128)}, f32[2,2,256,256]{3,2,1,0:T(8,128)}, u32[]{:S(2)}, u32[]{:S(2)}) collective-permute-start(f32[2,2,256,256]{3,2,1,0:T(8,128)} %get-tuple-element.32), channel_id=1, source_target_pairs={{0,8},{8,0},{1,9},{9,1},{2,10},{10,2},{3,11},{11,3},{4,12},{12,4},... | collective-permute-start | bytes 3145736 | tf_op jit(solution)/shard_map/ppermute | solution.py:547
  60.8 9.7 %collective-permute-start.5 = (f32[2,256,256]{2,1,0:T(8,128)S(1)}, f32[2,256,256]{2,1,0:T(8,128)S(1)}, u32[]{:S(2)}, u32[]{:S(2)}) collective-permute-start(f32[2,256,256]{2,1,0:T(8,128)S(1)} %get-tuple-element.30), channel_id=1, source_target_pairs={{0,8},{1,249},{2,10},{3,251},{4,12},{5,253},{6,14},{7,255},{8,16},... | collective-permute-start | bytes 1572872 | tf_op jit(solution)/shard_map/ppermute | solution.py:512
  66.1 18.5 %collective-permute-start.10 = (f32[256,256]{1,0:T(8,128)S(1)}, f32[256,256]{1,0:T(8,128)S(1)}, u32[]{:S(2)}, u32[]{:S(2)}) collective-permute-start(f32[256,256]{1,0:T(8,128)S(1)} %get-tuple-element.49), channel_id=1, source_target_pairs={{0,192},{64,0},{128,64},{192,128},{1,193},{65,1},{129,65},{193,129... | collective-permute-start | bytes 786440 | tf_op jit(solution)/shard_map/ppermute | solution.py:450
  66.6 18.1 %collective-permute-start.8 = (f32[256,256]{1,0:T(8,128)S(1)}, f32[256,256]{1,0:T(8,128)S(1)}, u32[]{:S(2)}, u32[]{:S(2)}) collective-permute-start(f32[256,256]{1,0:T(8,128)S(1)} %get-tuple-element.51), channel_id=1, source_target_pairs={{0,64},{64,128},{128,192},{192,0},{1,65},{65,129},{129,193},{193,1... | collective-permute-start | bytes 786440 | tf_op jit(solution)/shard_map/ppermute | solution.py:450
  67.8 16.8 %collective-permute-start.9 = (f32[256,256]{1,0:T(8,128)S(1)}, f32[256,256]{1,0:T(8,128)S(1)}, u32[]{:S(2)}, u32[]{:S(2)}) collective-permute-start(f32[256,256]{1,0:T(8,128)S(1)} %get-tuple-element.50), channel_id=1, source_target_pairs={{0,128},{64,192},{128,0},{192,64},{1,129},{65,193},{129,1},{193,65... | collective-permute-start | bytes 786440 | tf_op jit(solution)/shard_map/ppermute | solution.py:450
  70.7 21.7 %collective-permute-start.13 = (f32[2,256,256]{2,1,0:T(8,128)S(1)}, f32[2,256,256]{2,1,0:T(8,128)}, u32[]{:S(2)}, u32[]{:S(2)}) collective-permute-start(f32[2,256,256]{2,1,0:T(8,128)S(1)} %select_add_fusion.1), channel_id=1, source_target_pairs={{0,1},{1,2},{2,3},{3,4},{4,5},{5,6},{6,7},{8,9},{9,10},{10,11},{11... | collective-permute-start | bytes 1572872 | tf_op jit(solution)/shard_map/ppermute | solution.py:441
  80.7 17.3 %collective-permute-start.7 = (f32[2,256,256]{2,1,0:T(8,128)S(1)}, f32[2,256,256]{2,1,0:T(8,128)S(1)}, u32[]{:S(2)}, u32[]{:S(2)}) collective-permute-start(f32[2,256,256]{2,1,0:T(8,128)S(1)} %get-tuple-element.34), channel_id=1, source_target_pairs={{0,8},{1,249},{2,10},{3,251},{4,12},{5,253},{6,14},{7,255},{8,16},... | collective-permute-start | bytes 1572872 | tf_op jit(solution)/shard_map/ppermute | solution.py:512
  88.5 4.1 %collective-permute-start.12 = (f32[64,256]{1,0:T(8,128)S(1)}, f32[64,256]{1,0:T(8,128)S(1)}, u32[]{:S(2)}, u32[]{:S(2)}) collective-permute-start(f32[64,256]{1,0:T(8,128)S(1)} %bitcast_add_fusion.1), channel_id=1, source_target_pairs={{0,6},{2,0},{4,2},{6,4},{1,7},{3,1},{5,3},{7,5},{8,14},{10,8},{12,... | collective-permute-start | bytes 196616 | tf_op jit(solution)/shard_map/ppermute | solution.py:450
  92.6 5.6 %collective-permute-start.14 = (f32[64,256]{1,0:T(8,128)S(1)}, f32[64,256]{1,0:T(8,128)S(1)}, u32[]{:S(2)}, u32[]{:S(2)}) collective-permute-start(f32[64,256]{1,0:T(8,128)S(1)} %add.152), channel_id=1, source_target_pairs={{0,6},{2,0},{4,2},{6,4},{1,7},{3,1},{5,3},{7,5},{8,14},{10,8},{12,... | collective-permute-start | bytes 196616 | tf_op jit(solution)/shard_map/ppermute | solution.py:450
  98.2 7.6 %collective-permute-start.15 = (f32[64,256]{1,0:T(8,128)S(1)}, f32[64,256]{1,0:T(8,128)S(1)}, u32[]{:S(2)}, u32[]{:S(2)}) collective-permute-start(f32[64,256]{1,0:T(8,128)S(1)} %bitcast_add_fusion), channel_id=1, source_target_pairs={{0,1},{1,0},{16,17},{17,16},{32,33},{33,32},{48,49},{49,48},{2,3},... | collective-permute-start | bytes 196616 | tf_op jit(solution)/shard_map/ppermute | solution.py:495
  99.8 8.4 %collective-permute-start.16 = (f32[64,256]{1,0:T(8,128)S(1)}, f32[64,256]{1,0:T(8,128)S(1)}, u32[]{:S(2)}, u32[]{:S(2)}) collective-permute-start(f32[64,256]{1,0:T(8,128)S(1)} %bitcast_add_fusion), channel_id=1, source_target_pairs={{0,16},{1,17},{16,0},{17,1},{32,48},{33,49},{48,32},{49,33},{2,18}... | collective-permute-start | bytes 196616 | tf_op jit(solution)/shard_map/ppermute | solution.py:495
  105.9 4.9 %collective-permute-start.17 = (f32[64,256]{1,0:T(8,128)S(1)}, f32[64,256]{1,0:T(8,128)S(1)}, u32[]{:S(2)}, u32[]{:S(2)}) collective-permute-start(f32[64,256]{1,0:T(8,128)S(1)} %bitcast_add_fusion), channel_id=1, source_target_pairs={{0,17},{1,16},{16,1},{17,0},{32,49},{33,48},{48,33},{49,32},{2,19}... | collective-permute-start | bytes 196616 | tf_op jit(solution)/shard_map/ppermute | solution.py:495
  110.8 7.1 %collective-permute-start.18 = (f32[64,256]{1,0:T(8,128)S(1)}, f32[64,256]{1,0:T(8,128)S(1)}, u32[]{:S(2)}, u32[]{:S(2)}) collective-permute-start(f32[64,256]{1,0:T(8,128)S(1)} %add_add_fusion.1), channel_id=1, source_target_pairs={{0,32},{1,33},{16,48},{17,49},{32,0},{33,1},{48,16},{49,17},{2,34}... | collective-permute-start | bytes 196616 | tf_op jit(solution)/shard_map/ppermute | solution.py:495
  118.0 4.6 %collective-permute-start.19 = (f32[64,256]{1,0:T(8,128)S(1)}, f32[64,256]{1,0:T(8,128)S(1)}, u32[]{:S(2)}, u32[]{:S(2)}) collective-permute-start(f32[64,256]{1,0:T(8,128)S(1)} %get-tuple-element.41), channel_id=1, source_target_pairs={{0,6},{2,0},{4,2},{6,4},{1,7},{3,1},{5,3},{7,5},{8,14},{10,8},{12,... | collective-permute-start | bytes 196616 | tf_op jit(solution)/shard_map/ppermute | solution.py:450
  118.1 6.4 %collective-permute-start.20 = (f32[64,256]{1,0:T(8,128)S(1)}, f32[64,256]{1,0:T(8,128)S(1)}, u32[]{:S(2)}, u32[]{:S(2)}) collective-permute-start(f32[64,256]{1,0:T(8,128)S(1)} %get-tuple-element.41), channel_id=1, source_target_pairs={{0,4},{2,6},{4,0},{6,2},{1,5},{3,7},{5,1},{7,3},{8,12},{10,14},{12... | collective-permute-start | bytes 196616 | tf_op jit(solution)/shard_map/ppermute | solution.py:450
  125.7 8.1 %collective-permute-start.23 = (f32[256,256]{1,0:T(8,128)S(1)}, f32[256,256]{1,0:T(8,128)S(1)}, u32[]{:S(2)}, u32[]{:S(2)}) collective-permute-start(f32[256,256]{1,0:T(8,128)S(1)} %bitcast.77), channel_id=1, source_target_pairs={{0,192},{64,0},{128,64},{192,128},{1,193},{65,1},{129,65},{193,129... | collective-permute-start | bytes 786440 | tf_op jit(solution)/shard_map/ppermute | solution.py:450
  125.7 8.0 %collective-permute-start.24 = (f32[256,256]{1,0:T(8,128)S(1)}, f32[256,256]{1,0:T(8,128)S(1)}, u32[]{:S(2)}, u32[]{:S(2)}) collective-permute-start(f32[256,256]{1,0:T(8,128)S(1)} %bitcast.78), channel_id=1, source_target_pairs={{0,128},{64,192},{128,0},{192,64},{1,129},{65,193},{129,1},{193,65... | collective-permute-start | bytes 786440 | tf_op jit(solution)/shard_map/ppermute | solution.py:450
  127.1 8.8 %collective-permute-start.25 = (f32[256,256]{1,0:T(8,128)S(1)}, f32[256,256]{1,0:T(8,128)S(1)}, u32[]{:S(2)}, u32[]{:S(2)}) collective-permute-start(f32[256,256]{1,0:T(8,128)S(1)} %bitcast.79), channel_id=1, source_target_pairs={{0,64},{64,128},{128,192},{192,0},{1,65},{65,129},{129,193},{193,1... | collective-permute-start | bytes 786440 | tf_op jit(solution)/shard_map/ppermute | solution.py:450
  129.2 11.0 %collective-permute-start.22 = (f32[2,256,256]{2,1,0:T(8,128)S(1)}, f32[2,256,256]{2,1,0:T(8,128)}, u32[]{:S(2)}, u32[]{:S(2)}) collective-permute-start(f32[2,256,256]{2,1,0:T(8,128)S(1)} %select_add_fusion), channel_id=1, source_target_pairs={{0,1},{1,2},{2,3},{3,4},{4,5},{5,6},{6,7},{8,9},{9,10},{10,11},{11... | collective-permute-start | bytes 1572872 | tf_op jit(solution)/shard_map/ppermute | solution.py:441
  140.2 20.3 %collective-permute-start.26 = (f32[1024,256]{1,0:T(8,128)S(1)}, f32[1024,256]{1,0:T(8,128)}, u32[]{:S(2)}, u32[]{:S(2)}) collective-permute-start(f32[1024,256]{1,0:T(8,128)S(1)} %bitcast.71), channel_id=1, source_target_pairs={{0,8},{8,0},{1,9},{9,1},{2,10},{10,2},{3,11},{11,3},{4,12},{12,4},... | collective-permute-start | bytes 3145736 | tf_op jit(solution)/shard_map/ppermute | solution.py:560
  (10 other events, 66.6 us)
